TPU v7x, 1024 devices: a whole 4x8x16 slice. The times are simulated.
1024 devices in a mesh: replica: 64 (over y, z_lo, core), tensor: 16 (over x, z_hi).
Axes of the slice: x: 4, y: 8, z: 16 (z_hi: 4, z_lo: 4; z = z_hi * 4 + z_lo), core: 2. Of those that a mesh axis runs over, the one named last changes fastest.
Arguments:
- attention_heads_output: bfloat16 [16384, 8192], P('replica', 'tensor'), may hold values from -6 to 6
- output_projection_weight: bfloat16 [8192, 8192], P('tensor'), may hold values from -0.0625 to 0.0625
- adapter_down_factors: bfloat16 [512, 64, 8192], P(None, 'replica', 'tensor'), may hold values from -0.0625 to 0.0625
- adapter_up_factors: bfloat16 [512, 64, 8192], P(None, 'replica', 'tensor'), may hold values from -0.75 to 0.75
- group_working_adapters: int32 [64, 8], replicated, may hold values from 0 to 511, as said below
- adapter_store_row: int32 [512], replicated, may hold values from 0 to 511, each once
- request_working_slot: int32 [16384], P('replica'), may hold values from 0 to 7
Outputs:
- projected: bfloat16 [16384, 8192], P('replica', 'tensor')
Inputs may be any that keep to these rules, and one draw needn't show every extreme that they name: `group_working_adapters`: the 8 ids of one group are distinct. `adapter_store_row`: each adapter has its own row.
All inputs are finite; a program needn't handle non-finite values.
Results may differ from a plain program's by a relative error of at most 0.0028.
Values may be sent and summed in bfloat16 or wider, within the bound.
No kernel may reach another device: no remote copies, remote signals or barrier semaphores. Data moves between devices by JAX's collectives and lax.ppermute only.
A program may use at most 64 MiB of HBM per device.

v0:
```python
import jax
import jax.numpy as jnp
from jax import lax
from jax.sharding import PartitionSpec as P

ADAPTER_RANK = 64
WORKING_SLOTS = 8


ADAPTER_SCALE = 0.5


def body(
    attention_heads_output,
    output_projection_weight,
    adapter_down_factors,
    adapter_up_factors,
    group_working_adapters,
    adapter_store_row,
    request_working_slot,
):
    groups = lax.axis_size("replica")
    row_count, features = attention_heads_output.shape
    local_rank_count = adapter_down_factors.shape[1]
    needed_store_rows = jnp.take(adapter_store_row, group_working_adapters.reshape(-1), axis=0)
    outgoing_down_factors = jnp.take(adapter_down_factors, needed_store_rows, axis=0)
    outgoing_up_factors = jnp.take(adapter_up_factors, needed_store_rows, axis=0)
    outgoing = jnp.stack([outgoing_down_factors, outgoing_up_factors], axis=1).reshape(
        groups, WORKING_SLOTS, 2, local_rank_count * features
    )
    fetched = lax.all_to_all(outgoing, "replica", split_axis=0, concat_axis=0, tiled=True)
    fetched = fetched.reshape(groups, WORKING_SLOTS, 2, local_rank_count, features).transpose(
        2, 1, 0, 3, 4
    )
    fetched = fetched.reshape(2, WORKING_SLOTS * ADAPTER_RANK, features)
    down_factor_rows = fetched[0]
    up_factor_rows = fetched[1]
    selector = (
        request_working_slot[:, None] == jnp.arange(WORKING_SLOTS, dtype=jnp.int32)[None, :]
    ).astype(jnp.float32)
    all_ranks = lax.dot_general(
        attention_heads_output,
        down_factor_rows,
        (((1,), (1,)), ((), ())),
        preferred_element_type=jnp.float32,
    )
    rank_local = jnp.sum(
        all_ranks.reshape(row_count, WORKING_SLOTS, ADAPTER_RANK) * selector[:, :, None], axis=1
    )
    base_local = jnp.dot(
        attention_heads_output, output_projection_weight, preferred_element_type=jnp.float32
    )
    base_projection_sum = lax.psum_scatter(base_local, "tensor", scatter_dimension=1, tiled=True)
    rank_total = lax.psum(rank_local, "tensor")
    rounded = rank_total.astype(jnp.bfloat16)
    expanded = (rounded[:, None, :] * selector[:, :, None].astype(jnp.bfloat16)).reshape(
        row_count, WORKING_SLOTS * ADAPTER_RANK
    )
    adapter_contribution = jnp.dot(expanded, up_factor_rows, preferred_element_type=jnp.float32)
    return (base_projection_sum + ADAPTER_SCALE * adapter_contribution).astype(jnp.bfloat16)


def solution(mesh):
    in_specs = (
        P("replica", "tensor"),
        P("tensor", None),
        P(None, "replica", "tensor"),
        P(None, "replica", "tensor"),
        P(),
        P(),
        P("replica"),
    )
    out_specs = P("replica", "tensor")
    return jax.shard_map(body, mesh=mesh, in_specs=in_specs, out_specs=out_specs, check_vma=False)
```

profile of v0, /device:TPU:16, one launch (start us, length us, event | category | flops | bytes accessed | tf_op | source)
XLA Modules:
  0.0 296.7 jit_solution(15343737748224110530)
XLA Ops:
  6.5 0.0 copy-start
  6.5 0.0 reduce-scatter.2.cloned.1.call-start
  6.5 9.1 %fusion.7 = f32[256,8192]{1,0:T(8,128)} fusion(bf16[256,512]{1,0:T(8,128)(2,1)} %param.9, bf16[512,8192]{1,0:T(8,128)(2,1)} %param.10), kind=kOutput, calls=%fused_computation.24 | convolution fusion | flops 2147483648 | bytes 17039360 | tf_op jit(solution)/shard_map/dot_general | solution.py:50
  15.6 0.0 copy-start.4
  15.6 0.0 copy-start.1
  15.7 0.0 copy-start.2
  15.7 0.0 reduce-scatter.2.cloned.1.call-update
  15.7 0.7 copy-done.4
  16.3 0.1 copy.13
  16.4 0.1 reshape.141
  16.5 0.1 reshape.140
  16.6 0.0 copy-done.1
  16.6 3.5 %gather_fusion = s32[512]{0:T(512)S(1)} fusion(s32[512]{0:T(512)S(1)} %copy-done.1, s32[1024]{0:T(1024)S(1)} %pad_clamp_fusion.1), kind=kCustom, calls=%fused_computation.2 | custom fusion | bytes 6144 | tf_op jit(solution)/shard_map/jit(_take)/gather | solution.py:25
  20.1 0.0 copy-start.5
  20.2 0.0 copy-done
  20.2 2.0 gather_fusion.1
  22.2 0.0 copy-start.3
  22.2 0.0 copy-done.2
  22.2 2.0 gather_fusion.2
  24.2 0.2 fusion.3
  24.3 1.1 pad_maximum_fusion
  25.5 17.2 %all-to-all-start = ((bf16[64,8,2,512]{3,1,2,0:T(8,128)(2,1)}), bf16[64,8,2,512]{3,1,2,0:T(8,128)(2,1)S(1)}, u32[]{:S(2)}, u32[]{:S(2)}) async-start(bf16[64,8,2,512]{3,1,2,0:T(8,128)(2,1)} %pad_maximum_fusion), calls=%async_computation.1 | async-start | bytes 2097152 | tf_op jit(solution)/shard_map/all_to_all | solution.py:31
  42.7 0.0 copy-done.5
  42.7 119.4 %all-to-all-done = bf16[64,8,2,512]{3,1,2,0:T(8,128)(2,1)S(1)} async-done(((bf16[64,8,2,512]{3,1,2,0:T(8,128)(2,1)}), bf16[64,8,2,512]{3,1,2,0:T(8,128)(2,1)S(1)}, u32[]{:S(2)}, u32[]{:S(2)}) %all-to-all-start) | async-done | bytes 1048608 | tf_op jit(solution)/shard_map/all_to_all | solution.py:31
  162.1 0.6 copy.19
  162.7 0.1 fusion.6
  162.8 0.0 copy-done.3
  162.8 0.3 fusion.8
  163.1 124.6 %psum.7 = bf16[256,64]{0,1:T(8,128)(2,1)S(1)} all-reduce(f32[256,64]{0,1:T(8,128)S(1)} %multiply_reduce_fusion), channel_id=1, replica_groups=mesh['replica'=64,'tensor'=16] {'tensor'}, use_global_device_ids=true, to_apply=%region_2.4 | all-reduce | flops 16384 | bytes 98304 | tf_op jit(solution)/shard_map/psum | solution.py:54
  287.8 0.0 reduce-scatter.2.cloned.1.call-done
  287.8 2.1 fusion.1
  (7 shorter events, 0.1 us)
Async XLA Ops:
  6.5 13.6 %copy-start = (bf16[512,1,512]{2,0,1:T(8,128)(2,1)S(1)}, bf16[512,1,512]{2,0,1:T(8,128)(2,1)}, u32[]{:S(2)}) copy-start(bf16[512,1,512]{2,0,1:T(8,128)(2,1)} %param.11) | copy-start | bytes 1572868
  6.5 281.3 %reduce-scatter.2.cloned.1.call-start = ((), (), s32[]{:S(2)}) async-start(), calls=%async_computation.2 | async-start | bytes 8912896 | tf_op jit(solution)/shard_map/reduce_scatter | solution.py:53
  15.6 0.7 copy-start.4
  15.6 1.0 copy-start.1
  15.7 6.5 %copy-start.2 = (bf16[512,1,512]{2,0,1:T(8,128)(2,1)S(1)}, bf16[512,1,512]{2,0,1:T(8,128)(2,1)}, u32[]{:S(2)}) copy-start(bf16[512,1,512]{2,0,1:T(8,128)(2,1)} %param.12) | copy-start | bytes 1572868
  20.1 22.5 %copy-start.5 = (s32[256]{0:T(256)S(1)}, s32[256]{0:T(256)}, u32[]{:S(2)}) copy-start(s32[256]{0:T(256)} %param.15) | copy-start | bytes 3076
  22.2 140.6 %copy-start.3 = (bf16[256,512]{1,0:T(8,128)(2,1)S(1)}, bf16[256,512]{1,0:T(8,128)(2,1)}, u32[]{:S(2)}) copy-start(bf16[256,512]{1,0:T(8,128)(2,1)} %param.9) | copy-start | bytes 786436
  25.5 136.6 %all-to-all-start = ((bf16[64,8,2,512]{3,1,2,0:T(8,128)(2,1)}), bf16[64,8,2,512]{3,1,2,0:T(8,128)(2,1)S(1)}, u32[]{:S(2)}, u32[]{:S(2)}) async-start(bf16[64,8,2,512]{3,1,2,0:T(8,128)(2,1)} %pad_maximum_fusion), calls=%async_computation.1 | async-start | bytes 2097152 | tf_op jit(solution)/shard_map/all_to_all | solution.py:31
Sparse Core Ops, SparseCore 0:
  15.8 261.4 reduce-scatter.1
where the time goes:
time: 297 us
  blocking collectives  125 us (42%)
  waiting for transfers between devices  119 us (40%)
  starting transfers between devices  17.2 us (6%)
  between operations  13.6 us (5%)
  matrix products  11.5 us (4%)
  local copies, waits for them, and re-layouts  9.05 us (3%)
    psum x1, blocking collectives, body(): rank_total = lax.psum(rank_local, 'tensor')  125 us
    all_to_all x1, waiting for transfers between devices, body(): lax.all_to_all(outgoing, 'replica', split_axis=0, concat_axis=0, tiled=True)  119 us
    all_to_all x1, starting transfers between devices, body(): lax.all_to_all(outgoing, 'replica', split_axis=0, concat_axis=0, tiled=True)  17.2 us
    dot_general x1, matrix products, body(): jnp.dot(attention_heads_output, output_projection_weight, preferred_eleme...  9.11 us
  transfers between devices with their start and end apart: 2, of which 1 were waited for; matrix products, arithmetic and copies ran while one was open for 3% of the time, Pallas kernels for 0%

commit v1 on v0

v1 whole, which is shorter than its diff:
```python
import jax
import jax.numpy as jnp
from jax import lax
from jax.sharding import Mesh, PartitionSpec as P

ADAPTER_RANK = 64
WORKING_SLOTS = 8
ADAPTER_SCALE = 0.5
CHUNKS = ((2,), (1, 3), (0,))

f32 = jnp.float32
bf16 = jnp.bfloat16

REPLICA = ("y", "zl", "c")
TENSOR = ("x", "zh")


def fetch_adapters(down_store, up_store, working_adapters, store_row):
    groups = working_adapters.shape[0]
    adapters, _, features = down_store.shape
    ids = working_adapters.reshape(-1)
    is_adapter = ids[:, None] == lax.broadcasted_iota(jnp.int32, (ids.shape[0], adapters), 1)
    rows = jnp.sum(jnp.where(is_adapter, store_row[None, :], 0), axis=1)
    pick = (rows[:, None] == lax.broadcasted_iota(jnp.int32, (ids.shape[0], adapters), 1)).astype(bf16)
    down = jnp.dot(pick, down_store[:, 0, :], preferred_element_type=f32).astype(bf16)
    up = jnp.dot(pick, up_store[:, 0, :], preferred_element_type=f32).astype(bf16)
    outgoing = jnp.concatenate(
        [down.reshape(groups, WORKING_SLOTS, features), up.reshape(groups, WORKING_SLOTS, features)], axis=1
    )
    fetched = lax.all_to_all(outgoing, REPLICA, split_axis=0, concat_axis=0, tiled=True)
    fetched = fetched.transpose(1, 0, 2)
    down = fetched[:WORKING_SLOTS].reshape(WORKING_SLOTS * ADAPTER_RANK, features)
    up = fetched[WORKING_SLOTS:].reshape(WORKING_SLOTS * ADAPTER_RANK, features)
    return down, up


def sum_over_tensor(part):
    shape = part.shape
    pieces = part.reshape(16, -1, 128)
    pieces = lax.all_to_all(pieces, TENSOR, split_axis=0, concat_axis=0, tiled=True)
    own = jnp.sum(pieces, axis=0).astype(bf16)
    spread = jnp.broadcast_to(own[None], (16,) + own.shape)
    spread = lax.all_to_all(spread, TENSOR, split_axis=0, concat_axis=0, tiled=True)
    return spread.reshape(shape)


def shifted(value, axis, by):
    size = lax.axis_size(axis)
    return lax.ppermute(value, axis, [(i, (i + by) % size) for i in range(size)])


def body(x_block, weight, down_store, up_store, working_adapters, store_row, slot):
    rows, features = x_block.shape
    xs, zs = lax.axis_size("x"), lax.axis_size("zh")
    core, x_at, z_at = lax.axis_index("c"), lax.axis_index("x"), lax.axis_index("zh")
    half = features // 2

    swapped = jnp.concatenate([x_block[:, half:], x_block[:, :half]], axis=1)
    ordered = jnp.where(core == 0, x_block, swapped)
    blocks = [shifted(ordered, "x", by) for by in range(1, xs)]
    lhs_mine = jnp.concatenate([block[:, :half] for block in blocks], axis=1)
    lhs_other = jnp.concatenate([block[:, half:] for block in blocks], axis=1)

    down, up = fetch_adapters(down_store, up_store, working_adapters, store_row)
    selector = slot[:, None] == jnp.arange(WORKING_SLOTS, dtype=jnp.int32)[None, :]
    all_ranks = lax.dot_general(x_block, down, (((1,), (1,)), ((), ())), preferred_element_type=f32)
    rank_local = jnp.sum(
        all_ranks.reshape(rows, WORKING_SLOTS, ADAPTER_RANK) * selector.astype(f32)[:, :, None], axis=1
    )
    rounded = sum_over_tensor(rank_local)
    expanded = (rounded[:, None, :] * selector.astype(bf16)[:, :, None]).reshape(rows, WORKING_SLOTS * ADAPTER_RANK)

    def columns(x_by, z_by):
        return (lax.rem(x_at + x_by, xs) * zs + lax.rem(z_at + z_by, zs)) * features

    def weight_of(z_bys, x_by):
        return jnp.concatenate(
            [lax.dynamic_slice(weight, (core * half, columns(x_by, z_by)), (half, features)) for z_by in z_bys], axis=1
        )

    total = None
    for z_bys in CHUNKS:
        mine = jnp.concatenate([shifted(weight_of(z_bys, by), "x", by) for by in range(1, xs)], axis=0)
        other = shifted(mine, "c", 1)
        partial = jnp.dot(lhs_mine, mine, preferred_element_type=f32) + jnp.dot(
            lhs_other, other, preferred_element_type=f32
        )
        for k, z_by in enumerate(z_bys):
            own = lax.dynamic_slice(weight, (0, columns(0, z_by)), (features, features))
            part = partial[:, k * features:(k + 1) * features] + jnp.dot(x_block, own, preferred_element_type=f32)
            if z_by:
                part = shifted(part.astype(bf16), "zh", z_by).astype(f32)
            total = part if total is None else total + part
    term = jnp.dot(expanded, up, preferred_element_type=f32)
    return (total + ADAPTER_SCALE * term).astype(bf16)


def solution(mesh):
    fine = Mesh(mesh.devices.reshape(8, 4, 2, 4, 4), ("y", "zl", "c", "x", "zh"))
    in_specs = (
        P(REPLICA, TENSOR),
        P(TENSOR, None),
        P(None, REPLICA, TENSOR),
        P(None, REPLICA, TENSOR),
        P(),
        P(),
        P(REPLICA),
    )
    return jax.shard_map(body, mesh=fine, in_specs=in_specs, out_specs=P(REPLICA, TENSOR), check_vma=False)
```

time: 297 us -> 192 us (0.65)
  the two profiles are of different devices: /device:TPU:16 before, /device:TPU:56 now
where the time goes in v1:
time: 192 us; the launch traced here: 191 us
  starting transfers between devices  130 us (68%)
  waiting for transfers between devices  25 us (13%)
  matrix products  15.9 us (8%)
  local copies, waits for them, and re-layouts  14.5 us (8%)
  other arithmetic  4.81 us (3%)
    ppermute x18, starting transfers between devices, shifted(): lax.ppermute(value, axis, [(i, (i + by) % size) for i in range(size)])  82.7 us
    all_to_all x1, starting transfers between devices, sum_over_tensor(): lax.all_to_all(spread, TENSOR, split_axis=0, concat_axis=0, tiled=True)  29.1 us
    all_to_all x1, starting transfers between devices, fetch_adapters(): lax.all_to_all(outgoing, REPLICA, split_axis=0, concat_axis=0, tiled=True)  13.4 us
    all_to_all x1, waiting for transfers between devices, sum_over_tensor(): lax.all_to_all(spread, TENSOR, split_axis=0, concat_axis=0, tiled=True)  13.2 us
    unnamed x41, local copies, waits for them, and re-layouts  7.6 us
    dot_general x4, matrix products, body(): jnp.dot(x_block, own, preferred_element_type=f32)  6.79 us
    all_to_all x1, waiting for transfers between devices, sum_over_tensor(): lax.all_to_all(pieces, TENSOR, split_axis=0, concat_axis=0, tiled=True)  5.93 us
    ppermute x18, waiting for transfers between devices, shifted(): lax.ppermute(value, axis, [(i, (i + by) % size) for i in range(size)])  5.92 us
  transfers between devices with their start and end apart: 21, of which 4 were waited for; matrix products, arithmetic and copies ran while one was open for 15% of the time, Pallas kernels for 0%

profile of v1, /device:TPU:56, one launch (start us, length us, event | category | flops | bytes accessed | tf_op | source)
XLA Modules:
  0.0 190.8 jit_solution(8604136736605662281)
XLA Ops:
  0.0 3.1 %fusion.33 = (bf16[256,512]{1,0:T(8,128)(2,1)}, bf16[256,512]{1,0:T(8,128)(2,1)}, bf16[256,512]{1,0:T(8,128)(2,1)}, bf16[256,512]{1,0:T(8,128)(2,1)S(1)}, bf16[2...) fusion(bf16[512,8192]{1,0:T(8,128)(2,1)} %param.8, ...), kind=kLoop, calls=%fused_computation.64 | loop fusion | bytes 6291508 | tf_op jit(solution)/shard_map/dynamic_slice | solution.py:78
  3.1 3.5 %collective-permute-start.3 = (bf16[256,512]{1,0:T(8,128)(2,1)}, bf16[256,512]{1,0:T(8,128)(2,1)}, u32[]{:S(2)}, u32[]{:S(2)}) collective-permute-start(bf16[256,512]{1,0:T(8,128)(2,1)} %get-tuple-element.16), channel_id=1, source_target_pairs={{0,4},{4,8},{8,12},{12,0},{1,5},{5,9},{9,13},{13,1},{2,6},{6,10},{... | collective-permute-start | bytes 786440 | tf_op jit(solution)/shard_map/ppermute | solution.py:49
  6.7 4.6 %collective-permute-start.4 = (bf16[256,512]{1,0:T(8,128)(2,1)}, bf16[256,512]{1,0:T(8,128)(2,1)}, u32[]{:S(2)}, u32[]{:S(2)}) collective-permute-start(bf16[256,512]{1,0:T(8,128)(2,1)} %get-tuple-element.15), channel_id=1, source_target_pairs={{0,8},{4,12},{8,0},{12,4},{1,9},{5,13},{9,1},{13,5},{2,10},{6,14},... | collective-permute-start | bytes 786440 | tf_op jit(solution)/shard_map/ppermute | solution.py:49
  11.3 0.9 pad_maximum_fusion.1
  12.2 2.0 %collective-permute-start.8 = (bf16[256,1024]{1,0:T(8,128)(2,1)}, bf16[256,1024]{1,0:T(8,128)(2,1)}, u32[]{:S(2)}, u32[]{:S(2)}) collective-permute-start(bf16[256,1024]{1,0:T(8,128)(2,1)} %pad_maximum_fusion.1), channel_id=1, source_target_pairs={{0,4},{4,8},{8,12},{12,0},{1,5},{5,9},{9,13},{13,1},{2,6},{6,10},{... | collective-permute-start | bytes 1572872 | tf_op jit(solution)/shard_map/ppermute | solution.py:49
  14.2 0.9 pad_maximum_fusion.2
  15.1 4.8 %collective-permute-start.9 = (bf16[256,1024]{1,0:T(8,128)(2,1)}, bf16[256,1024]{1,0:T(8,128)(2,1)}, u32[]{:S(2)}, u32[]{:S(2)}) collective-permute-start(bf16[256,1024]{1,0:T(8,128)(2,1)} %pad_maximum_fusion.2), channel_id=1, source_target_pairs={{0,8},{4,12},{8,0},{12,4},{1,9},{5,13},{9,1},{13,5},{2,10},{6,14},... | collective-permute-start | bytes 1572872 | tf_op jit(solution)/shard_map/ppermute | solution.py:49
  19.9 3.1 %collective-permute-start.14 = (bf16[256,512]{1,0:T(8,128)(2,1)}, bf16[256,512]{1,0:T(8,128)(2,1)}, u32[]{:S(2)}, u32[]{:S(2)}) collective-permute-start(bf16[256,512]{1,0:T(8,128)(2,1)} %get-tuple-element.7), channel_id=1, source_target_pairs={{0,4},{4,8},{8,12},{12,0},{1,5},{5,9},{9,13},{13,1},{2,6},{6,10},{... | collective-permute-start | bytes 786440 | tf_op jit(solution)/shard_map/ppermute | solution.py:49
  23.0 0.1 copy.34
  23.1 0.1 eq.42
  23.2 0.2 select_reduce_fusion
  23.4 0.5 fusion.2
  23.9 0.5 fusion.3
  24.4 1.1 pad_maximum_fusion
  25.5 13.4 %all-to-all-start = ((bf16[64,16,512]{2,1,0:T(8,128)(2,1)}), bf16[64,16,512]{2,1,0:T(8,128)(2,1)S(1)}, u32[]{:S(2)}, u32[]{:S(2)}) async-start(bf16[64,16,512]{2,1,0:T(8,128)(2,1)} %pad_maximum_fusion), calls=%async_computation | async-start | bytes 2097152 | tf_op jit(solution)/shard_map/all_to_all | solution.py:30
  39.0 0.0 copy-start.15
  39.0 0.8 maximum_select_fusion
  39.8 1.3 convolution_bitcast_fusion.3
  41.1 1.3 convolution_bitcast_fusion
  42.5 0.9 pad_maximum_fusion.3
  43.4 5.1 %collective-permute-start.10 = (bf16[256,1024]{1,0:T(8,128)(2,1)}, bf16[256,1024]{1,0:T(8,128)(2,1)S(1)}, u32[]{:S(2)}, u32[]{:S(2)}) collective-permute-start(bf16[256,1024]{1,0:T(8,128)(2,1)} %pad_maximum_fusion.3), channel_id=1, source_target_pairs={{0,12},{4,0},{8,4},{12,8},{1,13},{5,1},{9,5},{13,9},{2,14},{6,2},{... | collective-permute-start | bytes 1572872 | tf_op jit(solution)/shard_map/ppermute | solution.py:49
  48.5 1.0 constant_dynamic-update-slice_fusion.2
  49.5 0.0 copy-start.12
  49.5 2.1 %collective-permute-start = (bf16[256,512]{1,0:T(8,128)(2,1)}, bf16[256,512]{1,0:T(8,128)(2,1)S(1)}, u32[]{:S(2)}, u32[]{:S(2)}) collective-permute-start(bf16[256,512]{1,0:T(8,128)(2,1)} %maximum_select_fusion), channel_id=1, source_target_pairs={{0,4},{4,8},{8,12},{12,0},{1,5},{5,9},{9,13},{13,1},{2,6},{6,10},{... | collective-permute-start | bytes 786440 | tf_op jit(solution)/shard_map/ppermute | solution.py:49
  51.6 1.7 constant_dynamic-update-slice_fusion.8
  53.3 4.2 %collective-permute-start.1 = (bf16[256,512]{1,0:T(8,128)(2,1)}, bf16[256,512]{1,0:T(8,128)(2,1)S(1)}, u32[]{:S(2)}, u32[]{:S(2)}) collective-permute-start(bf16[256,512]{1,0:T(8,128)(2,1)} %maximum_select_fusion), channel_id=1, source_target_pairs={{0,8},{4,12},{8,0},{12,4},{1,9},{5,13},{9,1},{13,5},{2,10},{6,14},... | collective-permute-start | bytes 786440 | tf_op jit(solution)/shard_map/ppermute | solution.py:49
  57.5 1.0 constant_dynamic-update-slice_fusion.1
  58.4 3.9 %collective-permute-start.5 = (bf16[256,512]{1,0:T(8,128)(2,1)}, bf16[256,512]{1,0:T(8,128)(2,1)S(1)}, u32[]{:S(2)}, u32[]{:S(2)}) collective-permute-start(bf16[256,512]{1,0:T(8,128)(2,1)} %get-tuple-element.14), channel_id=1, source_target_pairs={{0,12},{4,0},{8,4},{12,8},{1,13},{5,1},{9,5},{13,9},{2,14},{6,2},{... | collective-permute-start | bytes 786440 | tf_op jit(solution)/shard_map/ppermute | solution.py:49
  62.4 1.1 constant_dynamic-update-slice_fusion.5
  63.5 3.9 %collective-permute-start.15 = (bf16[256,512]{1,0:T(8,128)(2,1)}, bf16[256,512]{1,0:T(8,128)(2,1)S(1)}, u32[]{:S(2)}, u32[]{:S(2)}) collective-permute-start(bf16[256,512]{1,0:T(8,128)(2,1)} %get-tuple-element.6), channel_id=1, source_target_pairs={{0,8},{4,12},{8,0},{12,4},{1,9},{5,13},{9,1},{13,5},{2,10},{6,14},... | collective-permute-start | bytes 786440 | tf_op jit(solution)/shard_map/ppermute | solution.py:49
  67.4 1.1 constant_dynamic-update-slice_fusion.4
  68.5 3.4 %collective-permute-start.16 = (bf16[256,512]{1,0:T(8,128)(2,1)S(1)}, bf16[256,512]{1,0:T(8,128)(2,1)S(1)}, u32[]{:S(2)}, u32[]{:S(2)}) collective-permute-start(bf16[256,512]{1,0:T(8,128)(2,1)S(1)} %copy-done.12), channel_id=1, source_target_pairs={{0,12},{4,0},{8,4},{12,8},{1,13},{5,1},{9,5},{13,9},{2,14},{6,2},{... | collective-permute-start | bytes 786440 | tf_op jit(solution)/shard_map/ppermute | solution.py:49
  71.9 5.6 %collective-permute-done.5 = bf16[256,512]{1,0:T(8,128)(2,1)S(1)} collective-permute-done((bf16[256,512]{1,0:T(8,128)(2,1)}, bf16[256,512]{1,0:T(8,128)(2,1)S(1)}, u32[]{:S(2)}, u32[]{:S(2)}) %collective-permute-start.5) | collective-permute-done | bytes 262176 | tf_op jit(solution)/shard_map/ppermute | solution.py:49
  77.5 1.9 %collective-permute-start.11 = (bf16[768,1024]{1,0:T(8,128)(2,1)S(1)}, bf16[768,1024]{1,0:T(8,128)(2,1)S(1)}, u32[]{:S(2)}, u32[]{:S(2)}) collective-permute-start(bf16[768,1024]{1,0:T(8,128)(2,1)S(1)} %constant_dynamic-update-slice_fusion.3), channel_id=1, source_target_pairs={{0,16},{16,0},{1,17},{17,1},{2,18},{18,2},{3,19},{19,3},{4,20},{20... | collective-permute-start | bytes 4718600 | tf_op jit(solution)/shard_map/ppermute | solution.py:49
  79.5 5.6 %collective-permute-start.2 = (bf16[256,512]{1,0:T(8,128)(2,1)S(1)}, bf16[256,512]{1,0:T(8,128)(2,1)S(1)}, u32[]{:S(2)}, u32[]{:S(2)}) collective-permute-start(bf16[256,512]{1,0:T(8,128)(2,1)S(1)} %copy-done.11), channel_id=1, source_target_pairs={{0,12},{4,0},{8,4},{12,8},{1,13},{5,1},{9,5},{13,9},{2,14},{6,2},{... | collective-permute-start | bytes 786440 | tf_op jit(solution)/shard_map/ppermute | solution.py:49
  85.1 0.7 constant_dynamic-update-slice_fusion.7
  85.8 2.1 %collective-permute-start.6 = (bf16[768,512]{1,0:T(8,128)(2,1)S(1)}, bf16[768,512]{1,0:T(8,128)(2,1)S(1)}, u32[]{:S(2)}, u32[]{:S(2)}) collective-permute-start(bf16[768,512]{1,0:T(8,128)(2,1)S(1)} %constant_dynamic-update-slice_fusion), channel_id=1, source_target_pairs={{0,16},{16,0},{1,17},{17,1},{2,18},{18,2},{3,19},{19,3},{4,20},{20... | collective-permute-start | bytes 2359304 | tf_op jit(solution)/shard_map/ppermute | solution.py:49
  87.9 0.7 constant_dynamic-update-slice_fusion.6
  88.7 2.2 %collective-permute-start.17 = (bf16[768,512]{1,0:T(8,128)(2,1)}, bf16[768,512]{1,0:T(8,128)(2,1)}, u32[]{:S(2)}, u32[]{:S(2)}) collective-permute-start(bf16[768,512]{1,0:T(8,128)(2,1)} %constant_dynamic-update-slice_fusion.6), channel_id=1, source_target_pairs={{0,16},{16,0},{1,17},{17,1},{2,18},{18,2},{3,19},{19,3},{4,20},{20... | collective-permute-start | bytes 2359304 | tf_op jit(solution)/shard_map/ppermute | solution.py:49
  91.0 0.3 collective-permute-done.2
  91.4 0.4 fusion.32
  91.7 1.1 fusion.5
  92.8 16.2 %collective-permute-start.7 = (bf16[256,512]{1,0:T(8,128)(2,1)}, bf16[256,512]{1,0:T(8,128)(2,1)}, u32[]{:S(2)}, u32[]{:S(2)}) collective-permute-start(bf16[256,512]{1,0:T(8,128)(2,1)} %fusion.5), channel_id=1, source_target_pairs={{0,2},{1,3},{2,0},{3,1},{4,6},{5,7},{6,4},{7,5},{8,10},{9,11},{10,... | collective-permute-start | bytes 786440 | tf_op jit(solution)/shard_map/ppermute | solution.py:49
  109.0 0.6 fusion.31
  109.6 0.6 convolution_add_fusion
  110.2 2.1 %fusion.8 = bf16[256,512]{1,0:T(8,128)(2,1)} fusion(f32[256,1024]{1,0:T(8,128)S(1)} %convolution_add_fusion, bf16[256,512]{1,0:T(8,128)(2,1)S(1)} %copy-done.1, bf16[512,8192]{1,0:T(8,128)(2,1)} %param.8, s32[]{:T(128)S(6)} %select_n.87), kind=kOutput, calls=%fused_computation.25 | convolution fusion | flops 134479872 | bytes 1572868 | tf_op jit(solution)/shard_map/dot_general | solution.py:90
  112.3 6.1 %collective-permute-start.12 = (bf16[256,512]{1,0:T(8,128)(2,1)}, bf16[256,512]{1,0:T(8,128)(2,1)}, u32[]{:S(2)}, u32[]{:S(2)}) collective-permute-start(bf16[256,512]{1,0:T(8,128)(2,1)} %fusion.8), channel_id=1, source_target_pairs={{0,1},{1,2},{2,3},{3,0},{4,5},{5,6},{6,7},{7,4},{8,9},{9,10},{10,1... | collective-permute-start | bytes 786440 | tf_op jit(solution)/shard_map/ppermute | solution.py:49
  118.4 0.6 copy.43
  119.0 1.0 copy-done.2
  120.0 0.3 fusion.38
  120.4 0.1 copy.36
  120.5 0.7 reshape.68
  121.2 4.6 %all-to-all-start.1 = ((f32[16,8,128]{2,1,0:T(8,128)}), f32[16,8,128]{2,1,0:T(8,128)S(1)}, u32[]{:S(2)}, u32[]{:S(2)}) async-start(f32[16,8,128]{2,1,0:T(8,128)} %reshape.68), calls=%async_computation.1 | async-start | bytes 131072 | tf_op jit(solution)/shard_map/all_to_all | solution.py:40
  125.8 2.1 %fusion.7 = bf16[256,512]{1,0:T(8,128)(2,1)} fusion(f32[256,1024]{1,0:T(8,128)S(1)} %convolution_add_fusion, bf16[256,512]{1,0:T(8,128)(2,1)S(1)} %copy-done.1, bf16[512,8192]{1,0:T(8,128)(2,1)} %param.8, s32[]{:T(128)S(6)} %select_n.88), kind=kOutput, calls=%fused_computation.23 | convolution fusion | flops 134479872 | bytes 1572868 | tf_op jit(solution)/shard_map/dot_general | solution.py:90
  127.9 7.9 %collective-permute-start.13 = (bf16[256,512]{1,0:T(8,128)(2,1)}, bf16[256,512]{1,0:T(8,128)(2,1)}, u32[]{:S(2)}, u32[]{:S(2)}) collective-permute-start(bf16[256,512]{1,0:T(8,128)(2,1)} %fusion.7), channel_id=1, source_target_pairs={{0,3},{1,0},{2,1},{3,2},{4,7},{5,4},{6,5},{7,6},{8,11},{9,8},{10,9... | collective-permute-start | bytes 786440 | tf_op jit(solution)/shard_map/ppermute | solution.py:49
  135.7 5.9 %all-to-all-done.1 = f32[16,8,128]{2,1,0:T(8,128)S(1)} async-done(((f32[16,8,128]{2,1,0:T(8,128)}), f32[16,8,128]{2,1,0:T(8,128)S(1)}, u32[]{:S(2)}, u32[]{:S(2)}) %all-to-all-start.1) | async-done | bytes 65568 | tf_op jit(solution)/shard_map/all_to_all | solution.py:40
  141.7 0.6 broadcast_in_dim.16
  142.3 29.1 %all-to-all-start.2 = ((bf16[16,8,128]{2,1,0:T(8,128)(2,1)}), bf16[16,8,128]{2,1,0:T(8,128)(2,1)S(1)}, u32[]{:S(2)}, u32[]{:S(2)}) async-start(bf16[16,8,128]{2,1,0:T(8,128)(2,1)} %broadcast_in_dim.16), calls=%async_computation.2 | async-start | bytes 65536 | tf_op jit(solution)/shard_map/all_to_all | solution.py:43
  171.5 1.7 fusion.30
  173.2 13.2 %all-to-all-done.2 = bf16[16,8,128]{2,1,0:T(8,128)(2,1)S(1)} async-done(((bf16[16,8,128]{2,1,0:T(8,128)(2,1)}), bf16[16,8,128]{2,1,0:T(8,128)(2,1)S(1)}, u32[]{:S(2)}, u32[]{:S(2)}) %all-to-all-start.2) | async-done | bytes 32800 | tf_op jit(solution)/shard_map/all_to_all | solution.py:43
  186.4 0.1 mul.138
  186.5 0.7 copy.37
  187.2 1.1 fusion.4
  188.3 2.5 %add_convert_fusion = bf16[256,512]{1,0:T(8,128)(2,1)} fusion(f32[256,512]{1,0:T(8,128)S(1)} %fusion.4, bf16[256,512]{1,0:T(8,128)(2,1)} %collective-permute-done.13, bf16[256,512]{1,0:T(8,128)(2,1)} %collective-permute-done.12, bf16[256,512]{1,0:T(8,128)(2,1)} %collective-permute-done.7, f32[256,512]{1,0:T(8,128)S(1)} %convolution_bitcast_fusion, ...), kind=kOutput, calls=%fused_computation.31 | convolution fusion | flops 203816960 | bytes 3801088 | tf_op jit(solution)/shard_map/dot_general | solution.py:85
  (58 shorter events, 0.3 us)
Async XLA Ops:
  0.0 23.4 %copy-start = (bf16[512,1,512]{2,0,1:T(8,128)(2,1)S(1)}, bf16[512,1,512]{2,0,1:T(8,128)(2,1)}, u32[]{:S(2)}) copy-start(bf16[512,1,512]{2,0,1:T(8,128)(2,1)} %param.9) | copy-start | bytes 1572868
  3.1 19.9 %copy-start.13 = (s32[64,8]{0,1:T(8,128)S(1)}, s32[64,8]{0,1:T(8,128)}, u32[]{:S(2)}) copy-start(s32[64,8]{0,1:T(8,128)} %param.11) | copy-start | bytes 6148
  3.1 20.1 %copy-start.14 = (s32[512]{0:T(512)S(1)}, s32[512]{0:T(512)}, u32[]{:S(2)}) copy-start(s32[512]{0:T(512)} %param.12) | copy-start | bytes 6148
  3.1 40.3 %collective-permute-start.3 = (bf16[256,512]{1,0:T(8,128)(2,1)}, bf16[256,512]{1,0:T(8,128)(2,1)}, u32[]{:S(2)}, u32[]{:S(2)}) collective-permute-start(bf16[256,512]{1,0:T(8,128)(2,1)} %get-tuple-element.16), channel_id=1, source_target_pairs={{0,4},{4,8},{8,12},{12,0},{1,5},{5,9},{9,13},{13,1},{2,6},{6,10},{... | collective-permute-start | bytes 786440 | tf_op jit(solution)/shard_map/ppermute | solution.py:49
  6.7 46.6 %collective-permute-start.4 = (bf16[256,512]{1,0:T(8,128)(2,1)}, bf16[256,512]{1,0:T(8,128)(2,1)}, u32[]{:S(2)}, u32[]{:S(2)}) collective-permute-start(bf16[256,512]{1,0:T(8,128)(2,1)} %get-tuple-element.15), channel_id=1, source_target_pairs={{0,8},{4,12},{8,0},{12,4},{1,9},{5,13},{9,1},{13,5},{2,10},{6,14},... | collective-permute-start | bytes 786440 | tf_op jit(solution)/shard_map/ppermute | solution.py:49
  12.2 11.8 %copy-start.16 = (bf16[512,1,512]{2,0,1:T(8,128)(2,1)S(1)}, bf16[512,1,512]{2,0,1:T(8,128)(2,1)}, u32[]{:S(2)}) copy-start(bf16[512,1,512]{2,0,1:T(8,128)(2,1)} %param.10) | copy-start | bytes 1572868
  12.2 46.3 %collective-permute-start.8 = (bf16[256,1024]{1,0:T(8,128)(2,1)}, bf16[256,1024]{1,0:T(8,128)(2,1)}, u32[]{:S(2)}, u32[]{:S(2)}) collective-permute-start(bf16[256,1024]{1,0:T(8,128)(2,1)} %pad_maximum_fusion.1), channel_id=1, source_target_pairs={{0,4},{4,8},{8,12},{12,0},{1,5},{5,9},{9,13},{13,1},{2,6},{6,10},{... | collective-permute-start | bytes 1572872 | tf_op jit(solution)/shard_map/ppermute | solution.py:49
  15.1 48.4 %collective-permute-start.9 = (bf16[256,1024]{1,0:T(8,128)(2,1)}, bf16[256,1024]{1,0:T(8,128)(2,1)}, u32[]{:S(2)}, u32[]{:S(2)}) collective-permute-start(bf16[256,1024]{1,0:T(8,128)(2,1)} %pad_maximum_fusion.2), channel_id=1, source_target_pairs={{0,8},{4,12},{8,0},{12,4},{1,9},{5,13},{9,1},{13,5},{2,10},{6,14},... | collective-permute-start | bytes 1572872 | tf_op jit(solution)/shard_map/ppermute | solution.py:49
  19.9 29.6 %collective-permute-start.14 = (bf16[256,512]{1,0:T(8,128)(2,1)}, bf16[256,512]{1,0:T(8,128)(2,1)}, u32[]{:S(2)}, u32[]{:S(2)}) collective-permute-start(bf16[256,512]{1,0:T(8,128)(2,1)} %get-tuple-element.7), channel_id=1, source_target_pairs={{0,4},{4,8},{8,12},{12,0},{1,5},{5,9},{9,13},{13,1},{2,6},{6,10},{... | collective-permute-start | bytes 786440 | tf_op jit(solution)/shard_map/ppermute | solution.py:49
  25.5 13.4 %copy-start.1 = (bf16[256,512]{1,0:T(8,128)(2,1)S(1)}, bf16[256,512]{1,0:T(8,128)(2,1)}, u32[]{:S(2)}) copy-start(bf16[256,512]{1,0:T(8,128)(2,1)} %param.7) | copy-start | bytes 786436
  25.5 92.8 %all-to-all-start = ((bf16[64,16,512]{2,1,0:T(8,128)(2,1)}), bf16[64,16,512]{2,1,0:T(8,128)(2,1)S(1)}, u32[]{:S(2)}, u32[]{:S(2)}) async-start(bf16[64,16,512]{2,1,0:T(8,128)(2,1)} %pad_maximum_fusion), calls=%async_computation | async-start | bytes 2097152 | tf_op jit(solution)/shard_map/all_to_all | solution.py:30
  39.0 3.5 %copy-start.15 = (s32[256]{0:T(256)S(1)}, s32[256]{0:T(256)}, u32[]{:S(2)}) copy-start(s32[256]{0:T(256)} %param.13) | copy-start | bytes 3076
  43.4 25.0 %collective-permute-start.10 = (bf16[256,1024]{1,0:T(8,128)(2,1)}, bf16[256,1024]{1,0:T(8,128)(2,1)S(1)}, u32[]{:S(2)}, u32[]{:S(2)}) collective-permute-start(bf16[256,1024]{1,0:T(8,128)(2,1)} %pad_maximum_fusion.3), channel_id=1, source_target_pairs={{0,12},{4,0},{8,4},{12,8},{1,13},{5,1},{9,5},{13,9},{2,14},{6,2},{... | collective-permute-start | bytes 1572872 | tf_op jit(solution)/shard_map/ppermute | solution.py:49
  49.5 19.0 %copy-start.12 = (bf16[256,512]{1,0:T(8,128)(2,1)S(1)}, bf16[256,512]{1,0:T(8,128)(2,1)}, u32[]{:S(2)}) copy-start(bf16[256,512]{1,0:T(8,128)(2,1)} %get-tuple-element.5) | copy-start | bytes 786436
  49.5 39.2 %collective-permute-start = (bf16[256,512]{1,0:T(8,128)(2,1)}, bf16[256,512]{1,0:T(8,128)(2,1)S(1)}, u32[]{:S(2)}, u32[]{:S(2)}) collective-permute-start(bf16[256,512]{1,0:T(8,128)(2,1)} %maximum_select_fusion), channel_id=1, source_target_pairs={{0,4},{4,8},{8,12},{12,0},{1,5},{5,9},{9,13},{13,1},{2,6},{6,10},{... | collective-permute-start | bytes 786440 | tf_op jit(solution)/shard_map/ppermute | solution.py:49
  53.3 37.7 %collective-permute-start.1 = (bf16[256,512]{1,0:T(8,128)(2,1)}, bf16[256,512]{1,0:T(8,128)(2,1)S(1)}, u32[]{:S(2)}, u32[]{:S(2)}) collective-permute-start(bf16[256,512]{1,0:T(8,128)(2,1)} %maximum_select_fusion), channel_id=1, source_target_pairs={{0,8},{4,12},{8,0},{12,4},{1,9},{5,13},{9,1},{13,5},{2,10},{6,14},... | collective-permute-start | bytes 786440 | tf_op jit(solution)/shard_map/ppermute | solution.py:49
  58.4 19.0 %collective-permute-start.5 = (bf16[256,512]{1,0:T(8,128)(2,1)}, bf16[256,512]{1,0:T(8,128)(2,1)S(1)}, u32[]{:S(2)}, u32[]{:S(2)}) collective-permute-start(bf16[256,512]{1,0:T(8,128)(2,1)} %get-tuple-element.14), channel_id=1, source_target_pairs={{0,12},{4,0},{8,4},{12,8},{1,13},{5,1},{9,5},{13,9},{2,14},{6,2},{... | collective-permute-start | bytes 786440 | tf_op jit(solution)/shard_map/ppermute | solution.py:49
  63.5 16.0 %copy-start.11 = (bf16[256,512]{1,0:T(8,128)(2,1)S(1)}, bf16[256,512]{1,0:T(8,128)(2,1)}, u32[]{:S(2)}) copy-start(bf16[256,512]{1,0:T(8,128)(2,1)} %maximum_select_fusion) | copy-start | bytes 786436
  63.5 16.0 %collective-permute-start.15 = (bf16[256,512]{1,0:T(8,128)(2,1)}, bf16[256,512]{1,0:T(8,128)(2,1)S(1)}, u32[]{:S(2)}, u32[]{:S(2)}) collective-permute-start(bf16[256,512]{1,0:T(8,128)(2,1)} %get-tuple-element.6), channel_id=1, source_target_pairs={{0,8},{4,12},{8,0},{12,4},{1,9},{5,13},{9,1},{13,5},{2,10},{6,14},... | collective-permute-start | bytes 786440 | tf_op jit(solution)/shard_map/ppermute | solution.py:49
  68.5 17.4 %collective-permute-start.16 = (bf16[256,512]{1,0:T(8,128)(2,1)S(1)}, bf16[256,512]{1,0:T(8,128)(2,1)S(1)}, u32[]{:S(2)}, u32[]{:S(2)}) collective-permute-start(bf16[256,512]{1,0:T(8,128)(2,1)S(1)} %copy-done.12), channel_id=1, source_target_pairs={{0,12},{4,0},{8,4},{12,8},{1,13},{5,1},{9,5},{13,9},{2,14},{6,2},{... | collective-permute-start | bytes 786440 | tf_op jit(solution)/shard_map/ppermute | solution.py:49
  77.5 31.5 %collective-permute-start.11 = (bf16[768,1024]{1,0:T(8,128)(2,1)S(1)}, bf16[768,1024]{1,0:T(8,128)(2,1)S(1)}, u32[]{:S(2)}, u32[]{:S(2)}) collective-permute-start(bf16[768,1024]{1,0:T(8,128)(2,1)S(1)} %constant_dynamic-update-slice_fusion.3), channel_id=1, source_target_pairs={{0,16},{16,0},{1,17},{17,1},{2,18},{18,2},{3,19},{19,3},{4,20},{20... | collective-permute-start | bytes 4718600 | tf_op jit(solution)/shard_map/ppermute | solution.py:49
  79.5 11.9 %collective-permute-start.2 = (bf16[256,512]{1,0:T(8,128)(2,1)S(1)}, bf16[256,512]{1,0:T(8,128)(2,1)S(1)}, u32[]{:S(2)}, u32[]{:S(2)}) collective-permute-start(bf16[256,512]{1,0:T(8,128)(2,1)S(1)} %copy-done.11), channel_id=1, source_target_pairs={{0,12},{4,0},{8,4},{12,8},{1,13},{5,1},{9,5},{13,9},{2,14},{6,2},{... | collective-permute-start | bytes 786440 | tf_op jit(solution)/shard_map/ppermute | solution.py:49
  85.8 5.5 %collective-permute-start.6 = (bf16[768,512]{1,0:T(8,128)(2,1)S(1)}, bf16[768,512]{1,0:T(8,128)(2,1)S(1)}, u32[]{:S(2)}, u32[]{:S(2)}) collective-permute-start(bf16[768,512]{1,0:T(8,128)(2,1)S(1)} %constant_dynamic-update-slice_fusion), channel_id=1, source_target_pairs={{0,16},{16,0},{1,17},{17,1},{2,18},{18,2},{3,19},{19,3},{4,20},{20... | collective-permute-start | bytes 2359304 | tf_op jit(solution)/shard_map/ppermute | solution.py:49
  88.7 82.8 %collective-permute-start.17 = (bf16[768,512]{1,0:T(8,128)(2,1)}, bf16[768,512]{1,0:T(8,128)(2,1)}, u32[]{:S(2)}, u32[]{:S(2)}) collective-permute-start(bf16[768,512]{1,0:T(8,128)(2,1)} %constant_dynamic-update-slice_fusion.6), channel_id=1, source_target_pairs={{0,16},{16,0},{1,17},{17,1},{2,18},{18,2},{3,19},{19,3},{4,20},{20... | collective-permute-start | bytes 2359304 | tf_op jit(solution)/shard_map/ppermute | solution.py:49
  90.9 19.3 %copy-start.8 = (bf16[256,256]{1,0:T(8,128)(2,1)}, bf16[256,256]{1,0:T(8,128)(2,1)S(1)}, u32[]{:S(2)}) copy-start(bf16[256,256]{1,0:T(8,128)(2,1)S(1)} %get-tuple-element.18) | copy-start | bytes 393220
  91.0 18.6 %copy-start.4 = (bf16[256,256]{1,0:T(8,128)(2,1)}, bf16[256,256]{1,0:T(8,128)(2,1)S(1)}, u32[]{:S(2)}) copy-start(bf16[256,256]{1,0:T(8,128)(2,1)S(1)} %get-tuple-element.19) | copy-start | bytes 393220
  91.0 19.2 %copy-start.9 = (bf16[256,256]{1,0:T(8,128)(2,1)}, bf16[256,256]{1,0:T(8,128)(2,1)S(1)}, u32[]{:S(2)}) copy-start(bf16[256,256]{1,0:T(8,128)(2,1)S(1)} %get-tuple-element.20) | copy-start | bytes 393220
  91.3 17.7 %copy-start.10 = (bf16[256,256]{1,0:T(8,128)(2,1)}, bf16[256,256]{1,0:T(8,128)(2,1)S(1)}, u32[]{:S(2)}) copy-start(bf16[256,256]{1,0:T(8,128)(2,1)S(1)} %get-tuple-element.22) | copy-start | bytes 393220
  91.3 18.3 %copy-start.6 = (bf16[256,256]{1,0:T(8,128)(2,1)}, bf16[256,256]{1,0:T(8,128)(2,1)S(1)}, u32[]{:S(2)}) copy-start(bf16[256,256]{1,0:T(8,128)(2,1)S(1)} %get-tuple-element.21) | copy-start | bytes 393220
  92.8 95.5 %collective-permute-start.7 = (bf16[256,512]{1,0:T(8,128)(2,1)}, bf16[256,512]{1,0:T(8,128)(2,1)}, u32[]{:S(2)}, u32[]{:S(2)}) collective-permute-start(bf16[256,512]{1,0:T(8,128)(2,1)} %fusion.5), channel_id=1, source_target_pairs={{0,2},{1,3},{2,0},{3,1},{4,6},{5,7},{6,4},{7,5},{8,10},{9,11},{10,... | collective-permute-start | bytes 786440 | tf_op jit(solution)/shard_map/ppermute | solution.py:49
  112.3 76.0 %collective-permute-start.12 = (bf16[256,512]{1,0:T(8,128)(2,1)}, bf16[256,512]{1,0:T(8,128)(2,1)}, u32[]{:S(2)}, u32[]{:S(2)}) collective-permute-start(bf16[256,512]{1,0:T(8,128)(2,1)} %fusion.8), channel_id=1, source_target_pairs={{0,1},{1,2},{2,3},{3,0},{4,5},{5,6},{6,7},{7,4},{8,9},{9,10},{10,1... | collective-permute-start | bytes 786440 | tf_op jit(solution)/shard_map/ppermute | solution.py:49
  119.0 1.0 copy-start.2
  121.2 20.5 %all-to-all-start.1 = ((f32[16,8,128]{2,1,0:T(8,128)}), f32[16,8,128]{2,1,0:T(8,128)S(1)}, u32[]{:S(2)}, u32[]{:S(2)}) async-start(f32[16,8,128]{2,1,0:T(8,128)} %reshape.68), calls=%async_computation.1 | async-start | bytes 131072 | tf_op jit(solution)/shard_map/all_to_all | solution.py:40
  127.9 59.3 %copy-start.3 = (bf16[64,16,512]{2,0,1:T(8,128)(2,1)S(1)}, bf16[64,16,512]{2,0,1:T(8,128)(2,1)}, u32[]{:S(2)}) copy-start(bf16[64,16,512]{2,0,1:T(8,128)(2,1)} %copy-done.2) | copy-start | bytes 3145732
  127.9 60.4 %collective-permute-start.13 = (bf16[256,512]{1,0:T(8,128)(2,1)}, bf16[256,512]{1,0:T(8,128)(2,1)}, u32[]{:S(2)}, u32[]{:S(2)}) collective-permute-start(bf16[256,512]{1,0:T(8,128)(2,1)} %fusion.7), channel_id=1, source_target_pairs={{0,3},{1,0},{2,1},{3,2},{4,7},{5,4},{6,5},{7,6},{8,11},{9,8},{10,9... | collective-permute-start | bytes 786440 | tf_op jit(solution)/shard_map/ppermute | solution.py:49
  142.3 44.0 %all-to-all-start.2 = ((bf16[16,8,128]{2,1,0:T(8,128)(2,1)}), bf16[16,8,128]{2,1,0:T(8,128)(2,1)S(1)}, u32[]{:S(2)}, u32[]{:S(2)}) async-start(bf16[16,8,128]{2,1,0:T(8,128)(2,1)} %broadcast_in_dim.16), calls=%async_computation.2 | async-start | bytes 65536 | tf_op jit(solution)/shard_map/all_to_all | solution.py:43
  171.4 16.9 %copy-start.5 = (bf16[256,256]{1,0:T(8,128)(2,1)S(1)}, bf16[256,256]{1,0:T(8,128)(2,1)}, u32[]{:S(2)}) copy-start(bf16[256,256]{1,0:T(8,128)(2,1)} %copy-done.4) | copy-start | bytes 393220
  171.4 16.9 %copy-start.7 = (bf16[256,256]{1,0:T(8,128)(2,1)S(1)}, bf16[256,256]{1,0:T(8,128)(2,1)}, u32[]{:S(2)}) copy-start(bf16[256,256]{1,0:T(8,128)(2,1)} %copy-done.6) | copy-start | bytes 393220

commit v2 on v1

v2 whole, which is shorter than its diff:
```python
import jax
import jax.numpy as jnp
from jax import lax
from jax.sharding import Mesh, PartitionSpec as P

ADAPTER_RANK = 64
WORKING_SLOTS = 8
ADAPTER_SCALE = 0.5

f32 = jnp.float32
bf16 = jnp.bfloat16

REPLICA = ("y", "zl", "c")
TENSOR = ("x", "zh")


def after(value, *earlier):
    return lax.optimization_barrier((value,) + earlier)[0]


def picking(working_adapters, store_row, adapters):
    ids = working_adapters.reshape(-1)
    places = lax.broadcasted_iota(jnp.int32, (ids.shape[0], adapters), 1)
    rows = jnp.sum(jnp.where(ids[:, None] == places, store_row[None, :], 0), axis=1)
    return (rows[:, None] == places).astype(bf16)


def fetch(pick, store):
    features = store.shape[2]
    out = jnp.dot(pick, store[:, 0, :], preferred_element_type=f32).astype(bf16)
    out = out.reshape(-1, WORKING_SLOTS, features)
    fetched = lax.all_to_all(out, REPLICA, split_axis=0, concat_axis=0, tiled=True)
    return fetched.transpose(1, 0, 2).reshape(WORKING_SLOTS * ADAPTER_RANK, features)


def sum_over_tensor(part):
    shape = part.shape
    pieces = part.reshape(16, -1, 128)
    pieces = lax.all_to_all(pieces, TENSOR, split_axis=0, concat_axis=0, tiled=True)
    own = jnp.sum(pieces, axis=0).astype(bf16)
    spread = jnp.broadcast_to(own[None], (16,) + own.shape)
    spread = lax.all_to_all(spread, TENSOR, split_axis=0, concat_axis=0, tiled=True)
    return spread.reshape(shape)


def shifted(value, axis, by):
    size = lax.axis_size(axis)
    return lax.ppermute(value, axis, [(i, (i + by) % size) for i in range(size)])


def body(x_block, weight, down_store, up_store, working_adapters, store_row, slot):
    rows, features = x_block.shape
    xs, zs = lax.axis_size("x"), lax.axis_size("zh")
    core, x_at, z_at = lax.axis_index("c"), lax.axis_index("x"), lax.axis_index("zh")
    half = features // 2

    def columns(x_by, z_by):
        return (lax.rem(x_at + x_by, xs) * zs + lax.rem(z_at + z_by, zs)) * features

    def weight_of(source, x_by, z_by, c_by=0):
        return lax.dynamic_slice(source, (lax.rem(core + c_by, 2) * half, columns(x_by, z_by)), (half, features))

    def product(mine, other, z_bys, w):
        partial = jnp.dot(lhs_mine, mine, preferred_element_type=f32) + jnp.dot(
            lhs_other, other, preferred_element_type=f32
        )
        parts = []
        for k, z_by in enumerate(z_bys):
            own = lax.dynamic_slice(w, (0, columns(0, z_by)), (features, features))
            own = jnp.dot(x_block, own, preferred_element_type=f32)
            parts.append(partial[:, k * features:(k + 1) * features] + own)
        return parts

    pick = picking(working_adapters, store_row, down_store.shape[0])
    down = fetch(pick, down_store)

    swapped = jnp.concatenate([x_block[:, half:], x_block[:, :half]], axis=1)
    ordered = jnp.where(core == 0, x_block, swapped)
    got = [shifted(jnp.concatenate([ordered, weight_of(weight, by, 2)], axis=0), "x", by) for by in range(1, xs)]
    selector = slot[:, None] == jnp.arange(WORKING_SLOTS, dtype=jnp.int32)[None, :]
    all_ranks = lax.dot_general(x_block, down, (((1,), (1,)), ((), ())), preferred_element_type=f32)
    rank_local = jnp.sum(
        all_ranks.reshape(rows, WORKING_SLOTS, ADAPTER_RANK) * selector.astype(f32)[:, :, None], axis=1
    )
    lhs_mine = jnp.concatenate([block[:rows, :half] for block in got], axis=1)
    lhs_other = jnp.concatenate([block[:rows, half:] for block in got], axis=1)
    far_mine = jnp.concatenate([block[rows:] for block in got], axis=0)
    (far,) = product(far_mine, shifted(far_mine, "c", 1), (2,), weight)
    far = far.astype(bf16)
    far_sum = shifted(far, "zh", 2)
    rounded = sum_over_tensor(rank_local)
    expanded = (rounded[:, None, :] * selector.astype(bf16)[:, :, None]).reshape(rows, WORKING_SLOTS * ADAPTER_RANK)
    near_weight = after(weight, far)
    near = [
        shifted(jnp.concatenate([weight_of(near_weight, by, 1), weight_of(near_weight, by, 3)], axis=1), "x", by)
        for by in range(1, xs)
    ]

    near_mine = after(jnp.concatenate(near, axis=0), far_sum, rounded)
    up_part, down_part = product(near_mine, shifted(near_mine, "c", 1), (1, 3), weight)
    up_part, down_part = up_part.astype(bf16), down_part.astype(bf16)
    up_sum = shifted(up_part, "zh", 1)
    down_sum = shifted(down_part, "zh", 3)
    own_weight = after(weight, up_part, down_part)
    home = [
        shifted(
            jnp.concatenate([weight_of(own_weight, by, 0), weight_of(own_weight, by, 0, 1)], axis=1), "x", by
        )
        for by in range(1, xs)
    ]

    up = fetch(after(pick, rounded), up_store)
    home = after(jnp.concatenate(home, axis=0), up_sum, down_sum)
    (total,) = product(home[:, :features], home[:, features:], (0,), weight)
    total = total + far_sum.astype(f32) + up_sum.astype(f32) + down_sum.astype(f32)
    term = jnp.dot(expanded, up, preferred_element_type=f32)
    return (total + ADAPTER_SCALE * term).astype(bf16)


def solution(mesh):
    fine = Mesh(mesh.devices.reshape(8, 4, 2, 4, 4), ("y", "zl", "c", "x", "zh"))
    in_specs = (
        P(REPLICA, TENSOR),
        P(TENSOR, None),
        P(None, REPLICA, TENSOR),
        P(None, REPLICA, TENSOR),
        P(),
        P(),
        P(REPLICA),
    )
    return jax.shard_map(body, mesh=fine, in_specs=in_specs, out_specs=P(REPLICA, TENSOR), check_vma=False)
```

time: 192 us -> 195 us (1.016)
  the two profiles are of different devices: /device:TPU:56 before, /device:TPU:201 now
where the time goes in v2:
time: 195 us; the launch traced here: 194 us
  starting transfers between devices  113 us (58%)
  waiting for transfers between devices  39.4 us (20%)
  matrix products  18.7 us (10%)
  local copies, waits for them, and re-layouts  15.5 us (8%)
  other arithmetic  6.61 us (3%)
    ppermute x14, starting transfers between devices, shifted(): lax.ppermute(value, axis, [(i, (i + by) % size) for i in range(size)])  60.2 us
    all_to_all x2, starting transfers between devices, fetch(): lax.all_to_all(out, REPLICA, split_axis=0, concat_axis=0, tiled=True)  30.8 us
    ppermute x14, waiting for transfers between devices, shifted(): lax.ppermute(value, axis, [(i, (i + by) % size) for i in range(size)])  23.2 us
    all_to_all x1, starting transfers between devices, sum_over_tensor(): lax.all_to_all(pieces, TENSOR, split_axis=0, concat_axis=0, tiled=True)  16.1 us
    all_to_all x1, waiting for transfers between devices, sum_over_tensor(): lax.all_to_all(spread, TENSOR, split_axis=0, concat_axis=0, tiled=True)  14.1 us
    dot_general x4, matrix products, product(): own = jnp.dot(x_block, own, preferred_element_type=f32)  7.6 us
    all_to_all x1, starting transfers between devices, sum_over_tensor(): lax.all_to_all(spread, TENSOR, split_axis=0, concat_axis=0, tiled=True)  5.85 us
    dot_general x3, matrix products, product(): jnp.dot(lhs_mine, mine, preferred_element_type=f32)  3.96 us
  transfers between devices with their start and end apart: 18, of which 6 were waited for; matrix products, arithmetic and copies ran while one was open for 18% of the time, Pallas kernels for 0%

profile of v2, /device:TPU:201, one launch (start us, length us, event | category | flops | bytes accessed | tf_op | source)
XLA Modules:
  0.0 193.9 jit_solution(7257393649567801319)
XLA Ops:
  0.0 1.0 fusion.47
  1.1 1.2 fusion.43
  2.3 0.1 pad_maximum_fusion.5
  2.5 3.3 %collective-permute-start = (bf16[512,512]{1,0:T(8,128)(2,1)S(1)}, bf16[512,512]{1,0:T(8,128)(2,1)}, u32[]{:S(2)}, u32[]{:S(2)}) collective-permute-start(bf16[512,512]{1,0:T(8,128)(2,1)S(1)} %get-tuple-element.36), channel_id=1, source_target_pairs={{0,4},{4,8},{8,12},{12,0},{1,5},{5,9},{9,13},{13,1},{2,6},{6,10},{... | collective-permute-start | bytes 1572872 | tf_op jit(solution)/shard_map/ppermute | solution.py:48
  5.7 4.4 %collective-permute-start.1 = (bf16[512,512]{1,0:T(8,128)(2,1)S(1)}, bf16[512,512]{1,0:T(8,128)(2,1)}, u32[]{:S(2)}, u32[]{:S(2)}) collective-permute-start(bf16[512,512]{1,0:T(8,128)(2,1)S(1)} %get-tuple-element.37), channel_id=1, source_target_pairs={{0,8},{4,12},{8,0},{12,4},{1,9},{5,13},{9,1},{13,5},{2,10},{6,14},... | collective-permute-start | bytes 1572872 | tf_op jit(solution)/shard_map/ppermute | solution.py:48
  10.1 3.1 %collective-permute-start.2 = (bf16[512,512]{1,0:T(8,128)(2,1)S(1)}, bf16[512,512]{1,0:T(8,128)(2,1)}, u32[]{:S(2)}, u32[]{:S(2)}) collective-permute-start(bf16[512,512]{1,0:T(8,128)(2,1)S(1)} %get-tuple-element.38), channel_id=1, source_target_pairs={{0,12},{4,0},{8,4},{12,8},{1,13},{5,1},{9,5},{13,9},{2,14},{6,2},{... | collective-permute-start | bytes 1572872 | tf_op jit(solution)/shard_map/ppermute | solution.py:48
  13.2 0.1 copy.31
  13.3 0.1 eq.42
  13.4 0.2 select_reduce_fusion
  13.6 1.3 fusion.3
  14.9 13.4 %all-to-all-start = ((bf16[64,8,512]{2,1,0:T(8,128)(2,1)}), bf16[64,8,512]{2,1,0:T(8,128)(2,1)S(1)}, u32[]{:S(2)}, u32[]{:S(2)}) async-start(bf16[64,8,512]{2,1,0:T(8,128)(2,1)} %fusion.3), calls=%async_computation | async-start | bytes 1048576 | tf_op jit(solution)/shard_map/all_to_all | solution.py:32
  28.3 2.2 %convolution_bitcast_fusion.3 = f32[256,512]{1,0:T(8,128)} fusion(bf16[256,512]{1,0:T(8,128)(2,1)S(1)} %copy-done.1, bf16[512,8192]{1,0:T(8,128)(2,1)} %param.8, s32[]{:T(128)S(6)} %select_n.88), kind=kOutput, calls=%fused_computation.14 | convolution fusion | flops 134217728 | bytes 1310724 | tf_op jit(solution)/shard_map/dot_general | solution.py:70
  30.5 1.0 slice.63
  31.5 1.0 slice.64
  32.4 1.0 slice.65
  33.5 3.4 %collective-permute-start.3 = (bf16[768,512]{1,0:T(8,128)(2,1)S(1)}, bf16[768,512]{1,0:T(8,128)(2,1)}, u32[]{:S(2)}, u32[]{:S(2)}) collective-permute-start(bf16[768,512]{1,0:T(8,128)(2,1)S(1)} %pad_maximum_fusion.2), channel_id=1, source_target_pairs={{0,16},{16,0},{1,17},{17,1},{2,18},{18,2},{3,19},{19,3},{4,20},{20... | collective-permute-start | bytes 2359304 | tf_op jit(solution)/shard_map/ppermute | solution.py:48
  36.9 1.0 fusion.44
  37.9 1.0 fusion.45
  39.0 1.0 fusion.46
  40.0 0.6 copy-done.4
  40.6 1.5 fusion.40
  42.1 1.1 fusion.10
  43.2 1.5 fusion.42
  44.7 4.0 %collective-permute-start.4 = (bf16[256,1024]{1,0:T(8,128)(2,1)S(1)}, bf16[256,1024]{1,0:T(8,128)(2,1)}, u32[]{:S(2)}, u32[]{:S(2)}) collective-permute-start(bf16[256,1024]{1,0:T(8,128)(2,1)S(1)} %pad_maximum_fusion.6), channel_id=1, source_target_pairs={{0,4},{4,8},{8,12},{12,0},{1,5},{5,9},{9,13},{13,1},{2,6},{6,10},{... | collective-permute-start | bytes 1572872 | tf_op jit(solution)/shard_map/ppermute | solution.py:48
  48.8 3.3 %collective-permute-start.5 = (bf16[256,1024]{1,0:T(8,128)(2,1)S(1)}, bf16[256,1024]{1,0:T(8,128)(2,1)}, u32[]{:S(2)}, u32[]{:S(2)}) collective-permute-start(bf16[256,1024]{1,0:T(8,128)(2,1)S(1)} %pad_maximum_fusion.7), channel_id=1, source_target_pairs={{0,8},{4,12},{8,0},{12,4},{1,9},{5,13},{9,1},{13,5},{2,10},{6,14},... | collective-permute-start | bytes 1572872 | tf_op jit(solution)/shard_map/ppermute | solution.py:48
  52.2 3.2 %collective-permute-start.6 = (bf16[256,1024]{1,0:T(8,128)(2,1)S(1)}, bf16[256,1024]{1,0:T(8,128)(2,1)}, u32[]{:S(2)}, u32[]{:S(2)}) collective-permute-start(bf16[256,1024]{1,0:T(8,128)(2,1)S(1)} %pad_maximum_fusion.8), channel_id=1, source_target_pairs={{0,12},{4,0},{8,4},{12,8},{1,13},{5,1},{9,5},{13,9},{2,14},{6,2},{... | collective-permute-start | bytes 1572872 | tf_op jit(solution)/shard_map/ppermute | solution.py:48
  55.4 0.2 copy.32
  55.6 0.3 fusion.48
  55.9 0.7 multiply_reduce_fusion
  56.6 0.9 copy.33
  57.5 0.7 reshape.70
  58.2 16.1 %all-to-all-start.1 = ((f32[16,8,128]{2,1,0:T(8,128)}), f32[16,8,128]{2,1,0:T(8,128)S(1)}, u32[]{:S(2)}, u32[]{:S(2)}) async-start(f32[16,8,128]{2,1,0:T(8,128)} %reshape.70), calls=%async_computation.1 | async-start | bytes 131072 | tf_op jit(solution)/shard_map/all_to_all | solution.py:39
  74.3 12.0 %collective-permute-start.7 = (bf16[256,512]{1,0:T(8,128)(2,1)}, bf16[256,512]{1,0:T(8,128)(2,1)}, u32[]{:S(2)}, u32[]{:S(2)}) collective-permute-start(bf16[256,512]{1,0:T(8,128)(2,1)} %fusion.10), channel_id=1, source_target_pairs={{0,2},{1,3},{2,0},{3,1},{4,6},{5,7},{6,4},{7,5},{8,10},{9,11},{10,... | collective-permute-start | bytes 786440 | tf_op jit(solution)/shard_map/ppermute | solution.py:48
  86.3 2.1 %all-to-all-done.1 = f32[16,8,128]{2,1,0:T(8,128)S(1)} async-done(((f32[16,8,128]{2,1,0:T(8,128)}), f32[16,8,128]{2,1,0:T(8,128)S(1)}, u32[]{:S(2)}, u32[]{:S(2)}) %all-to-all-start.1) | async-done | bytes 65568 | tf_op jit(solution)/shard_map/all_to_all | solution.py:39
  88.4 0.6 broadcast_in_dim.16
  89.0 5.9 %all-to-all-start.2 = ((bf16[16,8,128]{2,1,0:T(8,128)(2,1)}), bf16[16,8,128]{2,1,0:T(8,128)(2,1)}, u32[]{:S(2)}, u32[]{:S(2)}) async-start(bf16[16,8,128]{2,1,0:T(8,128)(2,1)} %broadcast_in_dim.16), calls=%async_computation.2 | async-start | bytes 65536 | tf_op jit(solution)/shard_map/all_to_all | solution.py:42
  94.9 1.5 pad_maximum_fusion
  96.5 14.1 %all-to-all-done.2 = bf16[16,8,128]{2,1,0:T(8,128)(2,1)} async-done(((bf16[16,8,128]{2,1,0:T(8,128)(2,1)}), bf16[16,8,128]{2,1,0:T(8,128)(2,1)}, u32[]{:S(2)}, u32[]{:S(2)}) %all-to-all-start.2) | async-done | bytes 32800 | tf_op jit(solution)/shard_map/all_to_all | solution.py:42
  110.5 1.5 reshape.71
  112.0 5.7 %collective-permute-start.8 = (bf16[768,1024]{1,0:T(8,128)(2,1)S(1)}, bf16[768,1024]{1,0:T(8,128)(2,1)}, u32[]{:S(2)}, u32[]{:S(2)}) collective-permute-start(bf16[768,1024]{1,0:T(8,128)(2,1)S(1)} %pad_maximum_fusion), channel_id=1, source_target_pairs={{0,16},{16,0},{1,17},{17,1},{2,18},{18,2},{3,19},{19,3},{4,20},{20... | collective-permute-start | bytes 4718600 | tf_op jit(solution)/shard_map/ppermute | solution.py:48
  117.7 0.2 fusion.11
  117.9 1.2 fusion.5
  119.1 17.4 %all-to-all-start.3 = ((bf16[64,8,512]{2,1,0:T(8,128)(2,1)}), bf16[64,8,512]{2,1,0:T(8,128)(2,1)S(1)}, u32[]{:S(2)}, u32[]{:S(2)}) async-start(bf16[64,8,512]{2,1,0:T(8,128)(2,1)} %fusion.5), calls=%async_computation.3 | async-start | bytes 1048576 | tf_op jit(solution)/shard_map/all_to_all | solution.py:32
  136.6 2.1 %fusion.39 = f32[256,1024]{1,0:T(8,128)S(1)} fusion(bf16[768,1024]{1,0:T(8,128)(2,1)} %collective-permute-done.8, bf16[256,256]{1,0:T(8,128)(2,1)} %copy-done.4, bf16[256,256]{1,0:T(8,128)(2,1)S(1)} %get-tuple-element.33, bf16[256,256]{1,0:T(8,128)(2,1)S(1)} %get-tuple-element.31), kind=kOutput, calls=%fused_computation.67 | convolution fusion | flops 403832832 | bytes 3014656 | tf_op jit(solution)/shard_map/dot_general | solution.py:64
  138.7 0.6 convolution_add_fusion
  139.3 2.1 %fusion.15 = bf16[256,512]{1,0:T(8,128)(2,1)} fusion(f32[256,1024]{1,0:T(8,128)S(1)} %convolution_add_fusion, bf16[256,512]{1,0:T(8,128)(2,1)S(1)} %copy-done.1, bf16[512,8192]{1,0:T(8,128)(2,1)} %param.8, s32[]{:T(128)S(6)} %select_n.97), kind=kOutput, calls=%fused_computation.35 | convolution fusion | flops 134479872 | bytes 1572868 | tf_op jit(solution)/shard_map/dot_general | solution.py:70
  141.3 2.1 %fusion.16 = bf16[256,512]{1,0:T(8,128)(2,1)} fusion(f32[256,1024]{1,0:T(8,128)S(1)} %convolution_add_fusion, bf16[256,512]{1,0:T(8,128)(2,1)S(1)} %copy-done.1, bf16[512,8192]{1,0:T(8,128)(2,1)} %param.8, s32[]{:T(128)S(6)} %select_n.96), kind=kOutput, calls=%fused_computation.37 | convolution fusion | flops 134479872 | bytes 1572868 | tf_op jit(solution)/shard_map/dot_general | solution.py:70
  143.4 1.5 fusion.41
  144.9 2.2 %collective-permute-start.9 = (bf16[256,1024]{1,0:T(8,128)(2,1)S(1)}, bf16[256,1024]{1,0:T(8,128)(2,1)}, u32[]{:S(2)}, u32[]{:S(2)}) collective-permute-start(bf16[256,1024]{1,0:T(8,128)(2,1)S(1)} %pad_maximum_fusion.9), channel_id=1, source_target_pairs={{0,4},{4,8},{8,12},{12,0},{1,5},{5,9},{9,13},{13,1},{2,6},{6,10},{... | collective-permute-start | bytes 1572872 | tf_op jit(solution)/shard_map/ppermute | solution.py:48
  147.2 3.6 %collective-permute-start.10 = (bf16[256,1024]{1,0:T(8,128)(2,1)S(1)}, bf16[256,1024]{1,0:T(8,128)(2,1)}, u32[]{:S(2)}, u32[]{:S(2)}) collective-permute-start(bf16[256,1024]{1,0:T(8,128)(2,1)S(1)} %pad_maximum_fusion.10), channel_id=1, source_target_pairs={{0,8},{4,12},{8,0},{12,4},{1,9},{5,13},{9,1},{13,5},{2,10},{6,14},... | collective-permute-start | bytes 1572872 | tf_op jit(solution)/shard_map/ppermute | solution.py:48
  150.9 0.9 pad_maximum_fusion.11
  151.7 2.9 %collective-permute-start.11 = (bf16[256,1024]{1,0:T(8,128)(2,1)}, bf16[256,1024]{1,0:T(8,128)(2,1)}, u32[]{:S(2)}, u32[]{:S(2)}) collective-permute-start(bf16[256,1024]{1,0:T(8,128)(2,1)} %pad_maximum_fusion.11), channel_id=1, source_target_pairs={{0,12},{4,0},{8,4},{12,8},{1,13},{5,1},{9,5},{13,9},{2,14},{6,2},{... | collective-permute-start | bytes 1572872 | tf_op jit(solution)/shard_map/ppermute | solution.py:48
  154.6 1.3 convolution_bitcast_fusion
  156.0 0.9 copy.37
  156.9 3.1 %collective-permute-start.13 = (bf16[256,512]{1,0:T(8,128)(2,1)}, bf16[256,512]{1,0:T(8,128)(2,1)}, u32[]{:S(2)}, u32[]{:S(2)}) collective-permute-start(bf16[256,512]{1,0:T(8,128)(2,1)} %fusion.15), channel_id=1, source_target_pairs={{0,3},{1,0},{2,1},{3,2},{4,7},{5,4},{6,5},{7,6},{8,11},{9,8},{10,9... | collective-permute-start | bytes 786440 | tf_op jit(solution)/shard_map/ppermute | solution.py:48
  160.0 6.1 %collective-permute-start.12 = (bf16[256,512]{1,0:T(8,128)(2,1)}, bf16[256,512]{1,0:T(8,128)(2,1)}, u32[]{:S(2)}, u32[]{:S(2)}) collective-permute-start(bf16[256,512]{1,0:T(8,128)(2,1)} %fusion.16), channel_id=1, source_target_pairs={{0,1},{1,2},{2,3},{3,0},{4,5},{5,6},{6,7},{7,4},{8,9},{9,10},{10,1... | collective-permute-start | bytes 786440 | tf_op jit(solution)/shard_map/ppermute | solution.py:48
  166.1 0.4 fusion.4
  166.5 5.4 %collective-permute-done.10 = bf16[256,1024]{1,0:T(8,128)(2,1)} collective-permute-done((bf16[256,1024]{1,0:T(8,128)(2,1)S(1)}, bf16[256,1024]{1,0:T(8,128)(2,1)}, u32[]{:S(2)}, u32[]{:S(2)}) %collective-permute-start.10) | collective-permute-done | bytes 524320 | tf_op jit(solution)/shard_map/ppermute | solution.py:48
  171.9 2.9 %collective-permute-done.11 = bf16[256,1024]{1,0:T(8,128)(2,1)} collective-permute-done((bf16[256,1024]{1,0:T(8,128)(2,1)}, bf16[256,1024]{1,0:T(8,128)(2,1)}, u32[]{:S(2)}, u32[]{:S(2)}) %collective-permute-start.11) | collective-permute-done | bytes 524320 | tf_op jit(solution)/shard_map/ppermute | solution.py:48
  174.8 1.5 pad_maximum_fusion.1
  176.3 7.9 %collective-permute-done.13 = bf16[256,512]{1,0:T(8,128)(2,1)} collective-permute-done((bf16[256,512]{1,0:T(8,128)(2,1)}, bf16[256,512]{1,0:T(8,128)(2,1)}, u32[]{:S(2)}, u32[]{:S(2)}) %collective-permute-start.13) | collective-permute-done | bytes 262176 | tf_op jit(solution)/shard_map/ppermute | solution.py:48
  184.2 7.0 %collective-permute-done.12 = bf16[256,512]{1,0:T(8,128)(2,1)} collective-permute-done((bf16[256,512]{1,0:T(8,128)(2,1)}, bf16[256,512]{1,0:T(8,128)(2,1)}, u32[]{:S(2)}, u32[]{:S(2)}) %collective-permute-start.12) | collective-permute-done | bytes 262176 | tf_op jit(solution)/shard_map/ppermute | solution.py:48
  191.2 0.4 fusion.12
  191.5 2.3 %fusion.9 = bf16[256,512]{1,0:T(8,128)(2,1)} fusion(f32[256,512]{1,0:T(8,128)S(1)} %fusion.4, f32[256,512]{1,0:T(8,128)S(1)} %convolution_bitcast_fusion, f32[256,512]{1,0:T(8,128)S(1)} %fusion.12, bf16[768,1024]{1,0:T(8,128)(2,1)S(1)} %pad_maximum_fusion.1, bf16[256,512]{1,0:T(8,128)(2,1)} %collective-permute-done.13, ...), kind=kOutput, calls=%fused_computation.21 | convolution fusion | flops 203816960 | bytes 3801088 | tf_op jit(solution)/shard_map/dot_general | solution.py:64
  (37 shorter events, 0.4 us)
Async XLA Ops:
  0.0 13.6 %copy-start = (bf16[512,1,512]{2,0,1:T(8,128)(2,1)S(1)}, bf16[512,1,512]{2,0,1:T(8,128)(2,1)}, u32[]{:S(2)}) copy-start(bf16[512,1,512]{2,0,1:T(8,128)(2,1)} %param.9) | copy-start | bytes 1572868
  2.3 10.9 %copy-start.6 = (s32[64,8]{0,1:T(8,128)S(1)}, s32[64,8]{0,1:T(8,128)}, u32[]{:S(2)}) copy-start(s32[64,8]{0,1:T(8,128)} %param.11) | copy-start | bytes 6148
  2.3 11.0 %copy-start.7 = (s32[512]{0:T(512)S(1)}, s32[512]{0:T(512)}, u32[]{:S(2)}) copy-start(s32[512]{0:T(512)} %param.12) | copy-start | bytes 6148
  2.4 25.9 %copy-start.1 = (bf16[256,512]{1,0:T(8,128)(2,1)S(1)}, bf16[256,512]{1,0:T(8,128)(2,1)}, u32[]{:S(2)}) copy-start(bf16[256,512]{1,0:T(8,128)(2,1)} %param.7) | copy-start | bytes 786436
  2.5 28.0 %collective-permute-start = (bf16[512,512]{1,0:T(8,128)(2,1)S(1)}, bf16[512,512]{1,0:T(8,128)(2,1)}, u32[]{:S(2)}, u32[]{:S(2)}) collective-permute-start(bf16[512,512]{1,0:T(8,128)(2,1)S(1)} %get-tuple-element.36), channel_id=1, source_target_pairs={{0,4},{4,8},{8,12},{12,0},{1,5},{5,9},{9,13},{13,1},{2,6},{6,10},{... | collective-permute-start | bytes 1572872 | tf_op jit(solution)/shard_map/ppermute | solution.py:48
  5.7 25.7 %collective-permute-start.1 = (bf16[512,512]{1,0:T(8,128)(2,1)S(1)}, bf16[512,512]{1,0:T(8,128)(2,1)}, u32[]{:S(2)}, u32[]{:S(2)}) collective-permute-start(bf16[512,512]{1,0:T(8,128)(2,1)S(1)} %get-tuple-element.37), channel_id=1, source_target_pairs={{0,8},{4,12},{8,0},{12,4},{1,9},{5,13},{9,1},{13,5},{2,10},{6,14},... | collective-permute-start | bytes 1572872 | tf_op jit(solution)/shard_map/ppermute | solution.py:48
  10.1 22.4 %collective-permute-start.2 = (bf16[512,512]{1,0:T(8,128)(2,1)S(1)}, bf16[512,512]{1,0:T(8,128)(2,1)}, u32[]{:S(2)}, u32[]{:S(2)}) collective-permute-start(bf16[512,512]{1,0:T(8,128)(2,1)S(1)} %get-tuple-element.38), channel_id=1, source_target_pairs={{0,12},{4,0},{8,4},{12,8},{1,13},{5,1},{9,5},{13,9},{2,14},{6,2},{... | collective-permute-start | bytes 1572872 | tf_op jit(solution)/shard_map/ppermute | solution.py:48
  14.9 40.5 %all-to-all-start = ((bf16[64,8,512]{2,1,0:T(8,128)(2,1)}), bf16[64,8,512]{2,1,0:T(8,128)(2,1)S(1)}, u32[]{:S(2)}, u32[]{:S(2)}) async-start(bf16[64,8,512]{2,1,0:T(8,128)(2,1)} %fusion.3), calls=%async_computation | async-start | bytes 1048576 | tf_op jit(solution)/shard_map/all_to_all | solution.py:32
  30.5 6.4 %copy-start.8 = (s32[256]{0:T(256)S(1)}, s32[256]{0:T(256)}, u32[]{:S(2)}) copy-start(s32[256]{0:T(256)} %param.13) | copy-start | bytes 3076
  33.5 6.5 %collective-permute-start.3 = (bf16[768,512]{1,0:T(8,128)(2,1)S(1)}, bf16[768,512]{1,0:T(8,128)(2,1)}, u32[]{:S(2)}, u32[]{:S(2)}) collective-permute-start(bf16[768,512]{1,0:T(8,128)(2,1)S(1)} %pad_maximum_fusion.2), channel_id=1, source_target_pairs={{0,16},{16,0},{1,17},{17,1},{2,18},{18,2},{3,19},{19,3},{4,20},{20... | collective-permute-start | bytes 2359304 | tf_op jit(solution)/shard_map/ppermute | solution.py:48
  37.9 4.2 %copy-start.3 = (f32[256,512]{1,0:T(8,128)S(1)}, f32[256,512]{1,0:T(8,128)}, u32[]{:S(2)}) copy-start(f32[256,512]{1,0:T(8,128)} %convolution_bitcast_fusion.3) | copy-start | bytes 1572868
  40.0 0.6 copy-start.4
  44.7 50.2 %collective-permute-start.4 = (bf16[256,1024]{1,0:T(8,128)(2,1)S(1)}, bf16[256,1024]{1,0:T(8,128)(2,1)}, u32[]{:S(2)}, u32[]{:S(2)}) collective-permute-start(bf16[256,1024]{1,0:T(8,128)(2,1)S(1)} %pad_maximum_fusion.6), channel_id=1, source_target_pairs={{0,4},{4,8},{8,12},{12,0},{1,5},{5,9},{9,13},{13,1},{2,6},{6,10},{... | collective-permute-start | bytes 1572872 | tf_op jit(solution)/shard_map/ppermute | solution.py:48
  48.8 46.1 %collective-permute-start.5 = (bf16[256,1024]{1,0:T(8,128)(2,1)S(1)}, bf16[256,1024]{1,0:T(8,128)(2,1)}, u32[]{:S(2)}, u32[]{:S(2)}) collective-permute-start(bf16[256,1024]{1,0:T(8,128)(2,1)S(1)} %pad_maximum_fusion.7), channel_id=1, source_target_pairs={{0,8},{4,12},{8,0},{12,4},{1,9},{5,13},{9,1},{13,5},{2,10},{6,14},... | collective-permute-start | bytes 1572872 | tf_op jit(solution)/shard_map/ppermute | solution.py:48
  52.2 42.7 %collective-permute-start.6 = (bf16[256,1024]{1,0:T(8,128)(2,1)S(1)}, bf16[256,1024]{1,0:T(8,128)(2,1)}, u32[]{:S(2)}, u32[]{:S(2)}) collective-permute-start(bf16[256,1024]{1,0:T(8,128)(2,1)S(1)} %pad_maximum_fusion.8), channel_id=1, source_target_pairs={{0,12},{4,0},{8,4},{12,8},{1,13},{5,1},{9,5},{13,9},{2,14},{6,2},{... | collective-permute-start | bytes 1572872 | tf_op jit(solution)/shard_map/ppermute | solution.py:48
  58.2 30.2 %all-to-all-start.1 = ((f32[16,8,128]{2,1,0:T(8,128)}), f32[16,8,128]{2,1,0:T(8,128)S(1)}, u32[]{:S(2)}, u32[]{:S(2)}) async-start(f32[16,8,128]{2,1,0:T(8,128)} %reshape.70), calls=%async_computation.1 | async-start | bytes 131072 | tf_op jit(solution)/shard_map/all_to_all | solution.py:39
  74.3 37.7 %collective-permute-start.7 = (bf16[256,512]{1,0:T(8,128)(2,1)}, bf16[256,512]{1,0:T(8,128)(2,1)}, u32[]{:S(2)}, u32[]{:S(2)}) collective-permute-start(bf16[256,512]{1,0:T(8,128)(2,1)} %fusion.10), channel_id=1, source_target_pairs={{0,2},{1,3},{2,0},{3,1},{4,6},{5,7},{6,4},{7,5},{8,10},{9,11},{10,... | collective-permute-start | bytes 786440 | tf_op jit(solution)/shard_map/ppermute | solution.py:48
  89.0 21.5 %all-to-all-start.2 = ((bf16[16,8,128]{2,1,0:T(8,128)(2,1)}), bf16[16,8,128]{2,1,0:T(8,128)(2,1)}, u32[]{:S(2)}, u32[]{:S(2)}) async-start(bf16[16,8,128]{2,1,0:T(8,128)(2,1)} %broadcast_in_dim.16), calls=%async_computation.2 | async-start | bytes 65536 | tf_op jit(solution)/shard_map/all_to_all | solution.py:42
  94.9 23.0 %copy-start.2 = (bf16[512,1,512]{2,0,1:T(8,128)(2,1)S(1)}, bf16[512,1,512]{2,0,1:T(8,128)(2,1)}, u32[]{:S(2)}) copy-start(bf16[512,1,512]{2,0,1:T(8,128)(2,1)} %param.10) | copy-start | bytes 1572868
  112.0 24.6 %collective-permute-start.8 = (bf16[768,1024]{1,0:T(8,128)(2,1)S(1)}, bf16[768,1024]{1,0:T(8,128)(2,1)}, u32[]{:S(2)}, u32[]{:S(2)}) collective-permute-start(bf16[768,1024]{1,0:T(8,128)(2,1)S(1)} %pad_maximum_fusion), channel_id=1, source_target_pairs={{0,16},{16,0},{1,17},{17,1},{2,18},{18,2},{3,19},{19,3},{4,20},{20... | collective-permute-start | bytes 4718600 | tf_op jit(solution)/shard_map/ppermute | solution.py:48
  119.1 47.0 %all-to-all-start.3 = ((bf16[64,8,512]{2,1,0:T(8,128)(2,1)}), bf16[64,8,512]{2,1,0:T(8,128)(2,1)S(1)}, u32[]{:S(2)}, u32[]{:S(2)}) async-start(bf16[64,8,512]{2,1,0:T(8,128)(2,1)} %fusion.5), calls=%async_computation.3 | async-start | bytes 1048576 | tf_op jit(solution)/shard_map/all_to_all | solution.py:32
  144.9 21.6 %collective-permute-start.9 = (bf16[256,1024]{1,0:T(8,128)(2,1)S(1)}, bf16[256,1024]{1,0:T(8,128)(2,1)}, u32[]{:S(2)}, u32[]{:S(2)}) collective-permute-start(bf16[256,1024]{1,0:T(8,128)(2,1)S(1)} %pad_maximum_fusion.9), channel_id=1, source_target_pairs={{0,4},{4,8},{8,12},{12,0},{1,5},{5,9},{9,13},{13,1},{2,6},{6,10},{... | collective-permute-start | bytes 1572872 | tf_op jit(solution)/shard_map/ppermute | solution.py:48
  147.2 24.7 %collective-permute-start.10 = (bf16[256,1024]{1,0:T(8,128)(2,1)S(1)}, bf16[256,1024]{1,0:T(8,128)(2,1)}, u32[]{:S(2)}, u32[]{:S(2)}) collective-permute-start(bf16[256,1024]{1,0:T(8,128)(2,1)S(1)} %pad_maximum_fusion.10), channel_id=1, source_target_pairs={{0,8},{4,12},{8,0},{12,4},{1,9},{5,13},{9,1},{13,5},{2,10},{6,14},... | collective-permute-start | bytes 1572872 | tf_op jit(solution)/shard_map/ppermute | solution.py:48
  151.7 23.1 %collective-permute-start.11 = (bf16[256,1024]{1,0:T(8,128)(2,1)}, bf16[256,1024]{1,0:T(8,128)(2,1)}, u32[]{:S(2)}, u32[]{:S(2)}) collective-permute-start(bf16[256,1024]{1,0:T(8,128)(2,1)} %pad_maximum_fusion.11), channel_id=1, source_target_pairs={{0,12},{4,0},{8,4},{12,8},{1,13},{5,1},{9,5},{13,9},{2,14},{6,2},{... | collective-permute-start | bytes 1572872 | tf_op jit(solution)/shard_map/ppermute | solution.py:48
  156.9 27.3 %collective-permute-start.13 = (bf16[256,512]{1,0:T(8,128)(2,1)}, bf16[256,512]{1,0:T(8,128)(2,1)}, u32[]{:S(2)}, u32[]{:S(2)}) collective-permute-start(bf16[256,512]{1,0:T(8,128)(2,1)} %fusion.15), channel_id=1, source_target_pairs={{0,3},{1,0},{2,1},{3,2},{4,7},{5,4},{6,5},{7,6},{8,11},{9,8},{10,9... | collective-permute-start | bytes 786440 | tf_op jit(solution)/shard_map/ppermute | solution.py:48
  160.0 31.2 %collective-permute-start.12 = (bf16[256,512]{1,0:T(8,128)(2,1)}, bf16[256,512]{1,0:T(8,128)(2,1)}, u32[]{:S(2)}, u32[]{:S(2)}) collective-permute-start(bf16[256,512]{1,0:T(8,128)(2,1)} %fusion.16), channel_id=1, source_target_pairs={{0,1},{1,2},{2,3},{3,0},{4,5},{5,6},{6,7},{7,4},{8,9},{9,10},{10,1... | collective-permute-start | bytes 786440 | tf_op jit(solution)/shard_map/ppermute | solution.py:48
  166.5 24.7 %copy-start.5 = (bf16[256,256]{1,0:T(8,128)(2,1)S(1)}, bf16[256,256]{1,0:T(8,128)(2,1)}, u32[]{:S(2)}) copy-start(bf16[256,256]{1,0:T(8,128)(2,1)} %copy-done.4) | copy-start | bytes 393220

commit v3 on v2

v3 whole, which is shorter than its diff:
```python
import jax
import jax.numpy as jnp
from jax import lax
from jax.sharding import Mesh, PartitionSpec as P

ADAPTER_RANK = 64
WORKING_SLOTS = 8
ADAPTER_SCALE = 0.5

f32 = jnp.float32
bf16 = jnp.bfloat16

REPLICA = ("y", "zl", "c")
TENSOR = ("x", "zh")


def after(value, *earlier):
    return lax.optimization_barrier((value,) + earlier)[0]


def following(value, earlier):
    first = earlier[0, 0]
    return jnp.where(first != first, jnp.nan, value).astype(value.dtype)


def picking(working_adapters, store_row, adapters):
    ids = working_adapters.reshape(-1)
    places = lax.broadcasted_iota(jnp.int32, (ids.shape[0], adapters), 1)
    rows = jnp.sum(jnp.where(ids[:, None] == places, store_row[None, :], 0), axis=1)
    return (rows[:, None] == places).astype(bf16)


def picked(pick, store):
    rows = jnp.dot(pick, store[:, 0, :], preferred_element_type=f32).astype(bf16)
    return rows.reshape(-1, WORKING_SLOTS, store.shape[2])


def sum_over(part, axis):
    size = lax.axis_size(axis)
    spread = jnp.broadcast_to(part[None], (size,) + part.shape)
    return jnp.sum(lax.all_to_all(spread, axis, split_axis=0, concat_axis=0, tiled=True), axis=0)


def shifted(value, axis, by):
    size = lax.axis_size(axis)
    return lax.ppermute(value, axis, [(i, (i + by) % size) for i in range(size)])


def body(x_block, weight, down_store, up_store, working_adapters, store_row, slot):
    rows, features = x_block.shape
    xs, zs = lax.axis_size("x"), lax.axis_size("zh")
    core, x_at, z_at = lax.axis_index("c"), lax.axis_index("x"), lax.axis_index("zh")
    half = features // 2

    def columns(x_by, z_by):
        return (lax.rem(x_at + x_by, xs) * zs + lax.rem(z_at + z_by, zs)) * features

    def weight_of(source, x_by, z_by):
        return lax.dynamic_slice(source, (core * half, columns(x_by, z_by)), (half, features))

    def product(mine, other, z_bys, w):
        partial = jnp.dot(lhs_mine, mine, preferred_element_type=f32) + jnp.dot(
            lhs_other, other, preferred_element_type=f32
        )
        parts = []
        for k, z_by in enumerate(z_bys):
            own = lax.dynamic_slice(w, (0, columns(0, z_by)), (features, features))
            own = jnp.dot(x_block, own, preferred_element_type=f32)
            parts.append(partial[:, k * features:(k + 1) * features] + own)
        return parts

    pick = picking(working_adapters, store_row, down_store.shape[0])
    outgoing = jnp.concatenate([picked(pick, down_store), picked(pick, up_store)], axis=1)
    fetched = lax.all_to_all(outgoing, REPLICA, split_axis=0, concat_axis=0, tiled=True).transpose(1, 0, 2)
    down = fetched[:WORKING_SLOTS].reshape(WORKING_SLOTS * ADAPTER_RANK, features)
    up = fetched[WORKING_SLOTS:].reshape(WORKING_SLOTS * ADAPTER_RANK, features)

    swapped = jnp.concatenate([x_block[:, half:], x_block[:, :half]], axis=1)
    ordered = after(jnp.where(core == 0, x_block, swapped), outgoing)
    got = [shifted(jnp.concatenate([ordered, weight_of(weight, by, 2)], axis=0), "x", by) for by in range(1, xs)]
    lhs_mine = jnp.concatenate([block[:rows, :half] for block in got], axis=1)
    lhs_other = jnp.concatenate([block[:rows, half:] for block in got], axis=1)
    far_mine = jnp.concatenate([block[rows:] for block in got], axis=0)
    (far,) = product(far_mine, shifted(far_mine, "c", 1), (2,), weight)
    far = far.astype(bf16)
    far_sum = shifted(far, "zh", 2)

    selector = slot[None, :] == jnp.arange(WORKING_SLOTS, dtype=jnp.int32)[:, None]
    all_ranks = lax.dot_general(down, x_block, (((1,), (1,)), ((), ())), preferred_element_type=f32)
    ranks = jnp.sum(all_ranks.reshape(WORKING_SLOTS, ADAPTER_RANK, rows) * selector.astype(f32)[:, None, :], axis=0)
    ranks = following(sum_over(ranks, "x"), far_sum)
    rounded = sum_over(ranks, "zh").astype(bf16)
    expanded = (rounded[None] * selector.astype(bf16)[:, None, :]).reshape(WORKING_SLOTS * ADAPTER_RANK, rows)

    near_weight = after(weight, far)
    near = [
        shifted(jnp.concatenate([weight_of(near_weight, by, z_by) for z_by in (1, 3, 0)], axis=1), "x", by)
        for by in range(1, xs)
    ]
    near_mine = following(after(jnp.concatenate(near, axis=0), far_sum), rounded)
    up_part, down_part, total = product(near_mine, shifted(near_mine, "c", 1), (1, 3, 0), weight)
    up_sum = shifted(up_part.astype(bf16), "zh", 1)
    down_sum = shifted(down_part.astype(bf16), "zh", 3)
    term = lax.dot_general(expanded, up, (((0,), (0,)), ((), ())), preferred_element_type=f32)
    total = total + far_sum.astype(f32) + ADAPTER_SCALE * term
    return (total + up_sum.astype(f32) + down_sum.astype(f32)).astype(bf16)


def solution(mesh):
    fine = Mesh(mesh.devices.reshape(8, 4, 2, 4, 4), ("y", "zl", "c", "x", "zh"))
    in_specs = (
        P(REPLICA, TENSOR),
        P(TENSOR, None),
        P(None, REPLICA, TENSOR),
        P(None, REPLICA, TENSOR),
        P(),
        P(),
        P(REPLICA),
    )
    return jax.shard_map(body, mesh=fine, in_specs=in_specs, out_specs=P(REPLICA, TENSOR), check_vma=False)
```

time: 195 us -> 210 us (1.077)
  the two profiles are of different devices: /device:TPU:201 before, /device:TPU:3 now
where the time goes in v3:
time: 210 us; the launch traced here: 209 us
  waiting for transfers between devices  81.4 us (39%)
  starting transfers between devices  79.7 us (38%)
  matrix products  19 us (9%)
  local copies, waits for them, and re-layouts  14.3 us (7%)
  other arithmetic  11.2 us (5%)
  between operations  3.17 us (2%)
    ppermute x11, starting transfers between devices, shifted(): lax.ppermute(value, axis, [(i, (i + by) % size) for i in range(size)])  55.6 us
    ppermute x11, waiting for transfers between devices, shifted(): lax.ppermute(value, axis, [(i, (i + by) % size) for i in range(size)])  47.9 us
    all_to_all x2, waiting for transfers between devices, sum_over(): lax.all_to_all(spread, axis, split_axis=0, concat_axis=0, tiled=True)  33.4 us
    all_to_all x1, starting transfers between devices, body(): lax.all_to_all(outgoing, REPLICA, split_axis=0, concat_axis=0, tiled=True)  13.8 us
    all_to_all x2, starting transfers between devices, sum_over(): lax.all_to_all(spread, axis, split_axis=0, concat_axis=0, tiled=True)  10.3 us
    dot_general x4, matrix products, product(): own = jnp.dot(x_block, own, preferred_element_type=f32)  8.3 us
  transfers between devices with their start and end apart: 14, of which 8 were waited for; matrix products, arithmetic and copies ran while one was open for 11% of the time, Pallas kernels for 0%

profile of v3, /device:TPU:3, one launch (start us, length us, event | category | flops | bytes accessed | tf_op | source)
XLA Modules:
  0.0 208.7 jit_solution(13122944865886585198)
XLA Ops:
  0.0 0.8 copy.27
  0.8 0.1 eq.42
  0.9 0.9 select_reduce_fusion
  1.9 0.5 fusion.2
  2.4 1.5 fusion.1
  3.9 0.0 copy-start.1
  3.9 1.1 pad_maximum_fusion.1
  5.0 13.8 %all-to-all-start = ((bf16[64,16,512]{2,1,0:T(8,128)(2,1)}), bf16[64,16,512]{2,1,0:T(8,128)(2,1)S(1)}, u32[]{:S(2)}, u32[]{:S(2)}) async-start(bf16[64,16,512]{2,1,0:T(8,128)(2,1)} %pad_maximum_fusion.1), calls=%async_computation | async-start | bytes 2097152 | tf_op jit(solution)/shard_map/all_to_all | solution.py:74
  18.9 0.1 maximum_select_fusion
  19.0 1.2 fusion.45
  20.1 1.2 pad_maximum_fusion.8
  21.4 3.1 %collective-permute-start = (bf16[512,512]{1,0:T(8,128)(2,1)}, bf16[512,512]{1,0:T(8,128)(2,1)S(1)}, u32[]{:S(2)}, u32[]{:S(2)}) collective-permute-start(bf16[512,512]{1,0:T(8,128)(2,1)} %get-tuple-element.29), channel_id=1, source_target_pairs={{0,4},{4,8},{8,12},{12,0},{1,5},{5,9},{9,13},{13,1},{2,6},{6,10},{... | collective-permute-start | bytes 1572872 | tf_op jit(solution)/shard_map/ppermute | solution.py:46
  24.5 6.4 %collective-permute-start.1 = (bf16[512,512]{1,0:T(8,128)(2,1)}, bf16[512,512]{1,0:T(8,128)(2,1)}, u32[]{:S(2)}, u32[]{:S(2)}) collective-permute-start(bf16[512,512]{1,0:T(8,128)(2,1)} %get-tuple-element.30), channel_id=1, source_target_pairs={{0,8},{4,12},{8,0},{12,4},{1,9},{5,13},{9,1},{13,5},{2,10},{6,14},... | collective-permute-start | bytes 1572872 | tf_op jit(solution)/shard_map/ppermute | solution.py:46
  30.9 1.9 collective-permute-start.2
  32.8 0.0 copy-start.15
  32.8 1.3 convolution_bitcast_fusion.3
  34.2 5.1 %collective-permute-done = bf16[512,512]{1,0:T(8,128)(2,1)S(1)} collective-permute-done((bf16[512,512]{1,0:T(8,128)(2,1)}, bf16[512,512]{1,0:T(8,128)(2,1)S(1)}, u32[]{:S(2)}, u32[]{:S(2)}) %collective-permute-start) | collective-permute-done | bytes 524320 | tf_op jit(solution)/shard_map/ppermute | solution.py:46
  39.3 0.8 copy-done.5
  40.0 2.6 %collective-permute-done.1 = bf16[512,512]{1,0:T(8,128)(2,1)} collective-permute-done((bf16[512,512]{1,0:T(8,128)(2,1)}, bf16[512,512]{1,0:T(8,128)(2,1)}, u32[]{:S(2)}, u32[]{:S(2)}) %collective-permute-start.1) | collective-permute-done | bytes 524320 | tf_op jit(solution)/shard_map/ppermute | solution.py:46
  42.7 1.0 slice.76
  43.6 11.2 %collective-permute-done.2 = bf16[512,512]{1,0:T(8,128)(2,1)} collective-permute-done((bf16[512,512]{1,0:T(8,128)(2,1)}, bf16[512,512]{1,0:T(8,128)(2,1)}, u32[]{:S(2)}, u32[]{:S(2)}) %collective-permute-start.2) | collective-permute-done | bytes 524320 | tf_op jit(solution)/shard_map/ppermute | solution.py:46
  54.8 1.0 slice.77
  55.8 0.9 pad_maximum_fusion.2
  56.7 2.4 %collective-permute-start.3 = (bf16[768,512]{1,0:T(8,128)(2,1)}, bf16[768,512]{1,0:T(8,128)(2,1)}, u32[]{:S(2)}, u32[]{:S(2)}) collective-permute-start(bf16[768,512]{1,0:T(8,128)(2,1)} %pad_maximum_fusion.2), channel_id=1, source_target_pairs={{0,16},{16,0},{1,17},{17,1},{2,18},{18,2},{3,19},{19,3},{4,20},{20... | collective-permute-start | bytes 2359304 | tf_op jit(solution)/shard_map/ppermute | solution.py:46
  59.2 1.0 fusion.46
  60.2 1.0 fusion.47
  61.2 1.1 fusion.48
  62.4 1.6 fusion.31
  64.0 1.1 fusion.4
  65.0 14.9 %collective-permute-start.4 = (bf16[256,512]{1,0:T(8,128)(2,1)}, bf16[256,512]{1,0:T(8,128)(2,1)}, u32[]{:S(2)}, u32[]{:S(2)}) collective-permute-start(bf16[256,512]{1,0:T(8,128)(2,1)} %fusion.4), channel_id=1, source_target_pairs={{0,2},{1,3},{2,0},{3,1},{4,6},{5,7},{6,4},{7,5},{8,10},{9,11},{10,... | collective-permute-start | bytes 786440 | tf_op jit(solution)/shard_map/ppermute | solution.py:46
  79.9 1.9 fusion.44
  81.8 0.9 pad_maximum_fusion.4
  82.7 2.7 %collective-permute-start.6 = (bf16[256,1536]{1,0:T(8,128)(2,1)}, bf16[256,1536]{1,0:T(8,128)(2,1)}, u32[]{:S(2)}, u32[]{:S(2)}) collective-permute-start(bf16[256,1536]{1,0:T(8,128)(2,1)} %pad_maximum_fusion.4), channel_id=1, source_target_pairs={{0,8},{4,12},{8,0},{12,4},{1,9},{5,13},{9,1},{13,5},{2,10},{6,14},... | collective-permute-start | bytes 2359304 | tf_op jit(solution)/shard_map/ppermute | solution.py:46
  85.4 0.9 pad_maximum_fusion.5
  86.4 3.2 %collective-permute-start.7 = (bf16[256,1536]{1,0:T(8,128)(2,1)}, bf16[256,1536]{1,0:T(8,128)(2,1)}, u32[]{:S(2)}, u32[]{:S(2)}) collective-permute-start(bf16[256,1536]{1,0:T(8,128)(2,1)} %pad_maximum_fusion.5), channel_id=1, source_target_pairs={{0,12},{4,0},{8,4},{12,8},{1,13},{5,1},{9,5},{13,9},{2,14},{6,2},{... | collective-permute-start | bytes 2359304 | tf_op jit(solution)/shard_map/ppermute | solution.py:46
  89.6 0.0 all-to-all-done
  89.6 0.7 fusion.5
  90.3 0.7 broadcast_in_dim.42
  91.1 5.1 %all-to-all-start.1 = ((f32[4,64,256]{2,1,0:T(8,128)}), f32[4,64,256]{2,1,0:T(8,128)S(1)}, u32[]{:S(2)}, u32[]{:S(2)}) async-start(f32[4,64,256]{2,1,0:T(8,128)} %broadcast_in_dim.42), calls=%async_computation.1 | async-start | bytes 524288 | tf_op jit(solution)/shard_map/all_to_all | solution.py:41
  96.2 1.0 pad_maximum_fusion.3
  97.2 3.1 %collective-permute-start.5 = (bf16[256,1536]{1,0:T(8,128)(2,1)}, bf16[256,1536]{1,0:T(8,128)(2,1)}, u32[]{:S(2)}, u32[]{:S(2)}) collective-permute-start(bf16[256,1536]{1,0:T(8,128)(2,1)} %pad_maximum_fusion.3), channel_id=1, source_target_pairs={{0,4},{4,8},{8,12},{12,0},{1,5},{5,9},{9,13},{13,1},{2,6},{6,10},{... | collective-permute-start | bytes 2359304 | tf_op jit(solution)/shard_map/ppermute | solution.py:46
  100.2 0.0 collective-permute-done.4
  100.3 1.2 slice.81
  102.7 22.0 %all-to-all-done.1 = f32[4,64,256]{2,1,0:T(8,128)S(1)} async-done(((f32[4,64,256]{2,1,0:T(8,128)}), f32[4,64,256]{2,1,0:T(8,128)S(1)}, u32[]{:S(2)}, u32[]{:S(2)}) %all-to-all-start.1) | async-done | bytes 262176 | tf_op jit(solution)/shard_map/all_to_all | solution.py:41
  124.8 0.7 broadcast_in_dim.43
  125.5 5.2 %all-to-all-start.2 = ((f32[4,64,256]{2,1,0:T(8,128)}), f32[4,64,256]{2,1,0:T(8,128)S(1)}, u32[]{:S(2)}, u32[]{:S(2)}) async-start(f32[4,64,256]{2,1,0:T(8,128)} %broadcast_in_dim.43), calls=%async_computation.2 | async-start | bytes 524288 | tf_op jit(solution)/shard_map/all_to_all | solution.py:41
  130.7 1.8 pad_maximum_fusion
  132.5 11.5 %all-to-all-done.2 = f32[4,64,256]{2,1,0:T(8,128)S(1)} async-done(((f32[4,64,256]{2,1,0:T(8,128)}), f32[4,64,256]{2,1,0:T(8,128)S(1)}, u32[]{:S(2)}, u32[]{:S(2)}) %all-to-all-start.2) | async-done | bytes 262176 | tf_op jit(solution)/shard_map/all_to_all | solution.py:41
  143.9 0.6 reduce_sum.39
  144.5 1.2 slice.82
  147.0 1.6 broadcast_select_fusion
  148.6 8.8 %collective-permute-start.8 = (bf16[768,1536]{1,0:T(8,128)(2,1)}, bf16[768,1536]{1,0:T(8,128)(2,1)}, u32[]{:S(2)}, u32[]{:S(2)}) collective-permute-start(bf16[768,1536]{1,0:T(8,128)(2,1)} %broadcast_select_fusion), channel_id=1, source_target_pairs={{0,16},{16,0},{1,17},{17,1},{2,18},{18,2},{3,19},{19,3},{4,20},{20... | collective-permute-start | bytes 7077896 | tf_op jit(solution)/shard_map/ppermute | solution.py:46
  157.5 4.4 %collective-permute-done.8 = bf16[768,1536]{1,0:T(8,128)(2,1)} collective-permute-done((bf16[768,1536]{1,0:T(8,128)(2,1)}, bf16[768,1536]{1,0:T(8,128)(2,1)}, u32[]{:S(2)}, u32[]{:S(2)}) %collective-permute-start.8) | collective-permute-done | bytes 2359328 | tf_op jit(solution)/shard_map/ppermute | solution.py:46
  161.9 2.6 %fusion.30 = f32[256,1536]{1,0:T(8,128)S(1)} fusion(bf16[768,1536]{1,0:T(8,128)(2,1)} %collective-permute-done.8, bf16[256,256]{1,0:T(8,128)(2,1)} %copy-done.13, bf16[256,256]{1,0:T(8,128)(2,1)} %copy-done.12, bf16[256,256]{1,0:T(8,128)(2,1)S(1)} %copy-done.9), kind=kOutput, calls=%fused_computation.54 | convolution fusion | flops 605159424 | bytes 4325376 | tf_op jit(solution)/shard_map/dot_general | solution.py:62
  164.6 2.4 %convolution_add_fusion = f32[256,1536]{1,0:T(8,128)S(1)} fusion(f32[256,1536]{1,0:T(8,128)S(1)} %fusion.30, bf16[768,1536]{1,0:T(8,128)(2,1)} %broadcast_select_fusion, bf16[256,256]{1,0:T(8,128)(2,1)S(1)} %copy-done.11, bf16[256,256]{1,0:T(8,128)(2,1)S(1)} %copy-done.7, bf16[256,256]{1,0:T(8,128)(2,1)S(1)} %get-tuple-element.23), kind=kOutput, calls=%fused_computation | convolution fusion | flops 605552640 | bytes 5898240 | tf_op jit(solution)/shard_map/dot_general | solution.py:62
  167.0 2.5 %fusion.6 = bf16[256,512]{1,0:T(8,128)(2,1)} fusion(f32[256,1536]{1,0:T(8,128)S(1)} %convolution_add_fusion, bf16[256,512]{1,0:T(8,128)(2,1)S(1)} %copy-done.1, bf16[512,8192]{1,0:T(8,128)(2,1)} %param.8, s32[]{:T(128)S(6)} %select_n.117), kind=kOutput, calls=%fused_computation.31 | convolution fusion | flops 134479872 | bytes 1572868 | tf_op jit(solution)/shard_map/dot_general | solution.py:68
  169.6 2.1 fusion.7
  171.6 4.9 %collective-permute-start.9 = (bf16[256,512]{1,0:T(8,128)(2,1)}, bf16[256,512]{1,0:T(8,128)(2,1)S(1)}, u32[]{:S(2)}, u32[]{:S(2)}) collective-permute-start(bf16[256,512]{1,0:T(8,128)(2,1)} %fusion.7), channel_id=1, source_target_pairs={{0,1},{1,2},{2,3},{3,0},{4,5},{5,6},{6,7},{7,4},{8,9},{9,10},{10,1... | collective-permute-start | bytes 786440 | tf_op jit(solution)/shard_map/ppermute | solution.py:46
  176.6 4.2 %collective-permute-start.10 = (bf16[256,512]{1,0:T(8,128)(2,1)}, bf16[256,512]{1,0:T(8,128)(2,1)S(1)}, u32[]{:S(2)}, u32[]{:S(2)}) collective-permute-start(bf16[256,512]{1,0:T(8,128)(2,1)} %fusion.6), channel_id=1, source_target_pairs={{0,3},{1,0},{2,1},{3,2},{4,7},{5,4},{6,5},{7,6},{8,11},{9,8},{10,9... | collective-permute-start | bytes 786440 | tf_op jit(solution)/shard_map/ppermute | solution.py:46
  180.8 0.6 copy.39
  181.4 0.3 fusion.3
  181.8 10.6 %collective-permute-done.9 = bf16[256,512]{1,0:T(8,128)(2,1)S(1)} collective-permute-done((bf16[256,512]{1,0:T(8,128)(2,1)}, bf16[256,512]{1,0:T(8,128)(2,1)S(1)}, u32[]{:S(2)}, u32[]{:S(2)}) %collective-permute-start.9) | collective-permute-done | bytes 262176 | tf_op jit(solution)/shard_map/ppermute | solution.py:46
  192.4 14.0 %collective-permute-done.10 = bf16[256,512]{1,0:T(8,128)(2,1)S(1)} collective-permute-done((bf16[256,512]{1,0:T(8,128)(2,1)}, bf16[256,512]{1,0:T(8,128)(2,1)S(1)}, u32[]{:S(2)}, u32[]{:S(2)}) %collective-permute-start.10) | collective-permute-done | bytes 262176 | tf_op jit(solution)/shard_map/ppermute | solution.py:46
  206.4 2.4 %fusion.13 = bf16[256,512]{1,0:T(8,128)(2,1)} fusion(f32[256,512]{1,0:T(8,128)S(1)} %fusion.3, f32[256,1536]{1,0:T(8,128)} %copy-done.2, bf16[256,512]{1,0:T(8,128)(2,1)S(1)} %collective-permute-done.10, bf16[256,512]{1,0:T(8,128)(2,1)S(1)} %collective-permute-done.9, bf16[256,512]{1,0:T(8,128)(2,1)} %collective-permute-done.4, ...), kind=kOutput, calls=%fused_computation.40 | convolution fusion | flops 135397376 | bytes 2883588 | tf_op jit(solution)/shard_map/dot_general | solution.py:68
  (38 shorter events, 0.1 us)
Async XLA Ops:
  0.0 1.9 copy-start
  3.9 14.9 %copy-start.1 = (bf16[256,512]{1,0:T(8,128)(2,1)S(1)}, bf16[256,512]{1,0:T(8,128)(2,1)}, u32[]{:S(2)}) copy-start(bf16[256,512]{1,0:T(8,128)(2,1)} %param.7) | copy-start | bytes 786436
  5.0 84.6 %all-to-all-start = ((bf16[64,16,512]{2,1,0:T(8,128)(2,1)}), bf16[64,16,512]{2,1,0:T(8,128)(2,1)S(1)}, u32[]{:S(2)}, u32[]{:S(2)}) async-start(bf16[64,16,512]{2,1,0:T(8,128)(2,1)} %pad_maximum_fusion.1), calls=%async_computation | async-start | bytes 2097152 | tf_op jit(solution)/shard_map/all_to_all | solution.py:74
  21.4 17.9 %collective-permute-start = (bf16[512,512]{1,0:T(8,128)(2,1)}, bf16[512,512]{1,0:T(8,128)(2,1)S(1)}, u32[]{:S(2)}, u32[]{:S(2)}) collective-permute-start(bf16[512,512]{1,0:T(8,128)(2,1)} %get-tuple-element.29), channel_id=1, source_target_pairs={{0,4},{4,8},{8,12},{12,0},{1,5},{5,9},{9,13},{13,1},{2,6},{6,10},{... | collective-permute-start | bytes 1572872 | tf_op jit(solution)/shard_map/ppermute | solution.py:46
  24.5 18.2 %collective-permute-start.1 = (bf16[512,512]{1,0:T(8,128)(2,1)}, bf16[512,512]{1,0:T(8,128)(2,1)}, u32[]{:S(2)}, u32[]{:S(2)}) collective-permute-start(bf16[512,512]{1,0:T(8,128)(2,1)} %get-tuple-element.30), channel_id=1, source_target_pairs={{0,8},{4,12},{8,0},{12,4},{1,9},{5,13},{9,1},{13,5},{2,10},{6,14},... | collective-permute-start | bytes 1572872 | tf_op jit(solution)/shard_map/ppermute | solution.py:46
  30.9 23.9 %collective-permute-start.2 = (bf16[512,512]{1,0:T(8,128)(2,1)}, bf16[512,512]{1,0:T(8,128)(2,1)}, u32[]{:S(2)}, u32[]{:S(2)}) collective-permute-start(bf16[512,512]{1,0:T(8,128)(2,1)} %get-tuple-element.31), channel_id=1, source_target_pairs={{0,12},{4,0},{8,4},{12,8},{1,13},{5,1},{9,5},{13,9},{2,14},{6,2},{... | collective-permute-start | bytes 1572872 | tf_op jit(solution)/shard_map/ppermute | solution.py:46
  32.8 26.3 %copy-start.15 = (s32[256]{0:T(256)S(1)}, s32[256]{0:T(256)}, u32[]{:S(2)}) copy-start(s32[256]{0:T(256)} %param.13) | copy-start | bytes 3076
  39.2 0.8 copy-start.5
  56.7 5.7 %collective-permute-start.3 = (bf16[768,512]{1,0:T(8,128)(2,1)}, bf16[768,512]{1,0:T(8,128)(2,1)}, u32[]{:S(2)}, u32[]{:S(2)}) collective-permute-start(bf16[768,512]{1,0:T(8,128)(2,1)} %pad_maximum_fusion.2), channel_id=1, source_target_pairs={{0,16},{16,0},{1,17},{17,1},{2,18},{18,2},{3,19},{19,3},{4,20},{20... | collective-permute-start | bytes 2359304 | tf_op jit(solution)/shard_map/ppermute | solution.py:46
  60.2 4.8 %copy-start.8 = (bf16[256,256]{1,0:T(8,128)(2,1)}, bf16[256,256]{1,0:T(8,128)(2,1)S(1)}, u32[]{:S(2)}) copy-start(bf16[256,256]{1,0:T(8,128)(2,1)S(1)} %get-tuple-element.24) | copy-start | bytes 393220
  61.2 1.1 copy-start.12
  61.2 3.8 %copy-start.6 = (bf16[256,256]{1,0:T(8,128)(2,1)}, bf16[256,256]{1,0:T(8,128)(2,1)S(1)}, u32[]{:S(2)}) copy-start(bf16[256,256]{1,0:T(8,128)(2,1)S(1)} %get-tuple-element.25) | copy-start | bytes 393220
  62.3 1.6 copy-start.13
  62.3 2.7 %copy-start.10 = (bf16[256,256]{1,0:T(8,128)(2,1)}, bf16[256,256]{1,0:T(8,128)(2,1)S(1)}, u32[]{:S(2)}) copy-start(bf16[256,256]{1,0:T(8,128)(2,1)S(1)} %get-tuple-element.27) | copy-start | bytes 393220
  65.0 35.2 %collective-permute-start.4 = (bf16[256,512]{1,0:T(8,128)(2,1)}, bf16[256,512]{1,0:T(8,128)(2,1)}, u32[]{:S(2)}, u32[]{:S(2)}) collective-permute-start(bf16[256,512]{1,0:T(8,128)(2,1)} %fusion.4), channel_id=1, source_target_pairs={{0,2},{1,3},{2,0},{3,1},{4,6},{5,7},{6,4},{7,5},{8,10},{9,11},{10,... | collective-permute-start | bytes 786440 | tf_op jit(solution)/shard_map/ppermute | solution.py:46
  82.7 48.0 %collective-permute-start.6 = (bf16[256,1536]{1,0:T(8,128)(2,1)}, bf16[256,1536]{1,0:T(8,128)(2,1)}, u32[]{:S(2)}, u32[]{:S(2)}) collective-permute-start(bf16[256,1536]{1,0:T(8,128)(2,1)} %pad_maximum_fusion.4), channel_id=1, source_target_pairs={{0,8},{4,12},{8,0},{12,4},{1,9},{5,13},{9,1},{13,5},{2,10},{6,14},... | collective-permute-start | bytes 2359304 | tf_op jit(solution)/shard_map/ppermute | solution.py:46
  86.4 44.3 %collective-permute-start.7 = (bf16[256,1536]{1,0:T(8,128)(2,1)}, bf16[256,1536]{1,0:T(8,128)(2,1)}, u32[]{:S(2)}, u32[]{:S(2)}) collective-permute-start(bf16[256,1536]{1,0:T(8,128)(2,1)} %pad_maximum_fusion.5), channel_id=1, source_target_pairs={{0,12},{4,0},{8,4},{12,8},{1,13},{5,1},{9,5},{13,9},{2,14},{6,2},{... | collective-permute-start | bytes 2359304 | tf_op jit(solution)/shard_map/ppermute | solution.py:46
  89.6 35.1 %copy-start.3 = (bf16[64,16,512]{2,1,0:T(8,128)(2,1)}, bf16[64,16,512]{2,1,0:T(8,128)(2,1)S(1)}, u32[]{:S(2)}) copy-start(bf16[64,16,512]{2,1,0:T(8,128)(2,1)S(1)} %all-to-all-done) | copy-start | bytes 3145732
  91.1 33.6 %all-to-all-start.1 = ((f32[4,64,256]{2,1,0:T(8,128)}), f32[4,64,256]{2,1,0:T(8,128)S(1)}, u32[]{:S(2)}, u32[]{:S(2)}) async-start(f32[4,64,256]{2,1,0:T(8,128)} %broadcast_in_dim.42), calls=%async_computation.1 | async-start | bytes 524288 | tf_op jit(solution)/shard_map/all_to_all | solution.py:41
  97.2 33.5 %collective-permute-start.5 = (bf16[256,1536]{1,0:T(8,128)(2,1)}, bf16[256,1536]{1,0:T(8,128)(2,1)}, u32[]{:S(2)}, u32[]{:S(2)}) collective-permute-start(bf16[256,1536]{1,0:T(8,128)(2,1)} %pad_maximum_fusion.3), channel_id=1, source_target_pairs={{0,4},{4,8},{8,12},{12,0},{1,5},{5,9},{9,13},{13,1},{2,6},{6,10},{... | collective-permute-start | bytes 2359304 | tf_op jit(solution)/shard_map/ppermute | solution.py:46
  125.5 18.4 %all-to-all-start.2 = ((f32[4,64,256]{2,1,0:T(8,128)}), f32[4,64,256]{2,1,0:T(8,128)S(1)}, u32[]{:S(2)}, u32[]{:S(2)}) async-start(f32[4,64,256]{2,1,0:T(8,128)} %broadcast_in_dim.43), calls=%async_computation.2 | async-start | bytes 524288 | tf_op jit(solution)/shard_map/all_to_all | solution.py:41
  147.0 14.9 %copy-start.9 = (bf16[256,256]{1,0:T(8,128)(2,1)S(1)}, bf16[256,256]{1,0:T(8,128)(2,1)}, u32[]{:S(2)}) copy-start(bf16[256,256]{1,0:T(8,128)(2,1)} %copy-done.8) | copy-start | bytes 393220
  148.6 13.3 %collective-permute-start.8 = (bf16[768,1536]{1,0:T(8,128)(2,1)}, bf16[768,1536]{1,0:T(8,128)(2,1)}, u32[]{:S(2)}, u32[]{:S(2)}) collective-permute-start(bf16[768,1536]{1,0:T(8,128)(2,1)} %broadcast_select_fusion), channel_id=1, source_target_pairs={{0,16},{16,0},{1,17},{17,1},{2,18},{18,2},{3,19},{19,3},{4,20},{20... | collective-permute-start | bytes 7077896 | tf_op jit(solution)/shard_map/ppermute | solution.py:46
  157.5 7.1 %copy-start.7 = (bf16[256,256]{1,0:T(8,128)(2,1)S(1)}, bf16[256,256]{1,0:T(8,128)(2,1)}, u32[]{:S(2)}) copy-start(bf16[256,256]{1,0:T(8,128)(2,1)} %copy-done.6) | copy-start | bytes 393220
  157.5 7.1 %copy-start.11 = (bf16[256,256]{1,0:T(8,128)(2,1)S(1)}, bf16[256,256]{1,0:T(8,128)(2,1)}, u32[]{:S(2)}) copy-start(bf16[256,256]{1,0:T(8,128)(2,1)} %copy-done.10) | copy-start | bytes 393220
  167.0 2.6 %copy-start.2 = (f32[256,1536]{1,0:T(8,128)}, f32[256,1536]{1,0:T(8,128)S(1)}, u32[]{:S(2)}) copy-start(f32[256,1536]{1,0:T(8,128)S(1)} %convolution_add_fusion) | copy-start | bytes 4718596
  167.0 13.8 %copy-start.4 = (bf16[64,16,512]{2,1,0:T(8,128)(2,1)S(1)}, bf16[64,16,512]{2,1,0:T(8,128)(2,1)}, u32[]{:S(2)}) copy-start(bf16[64,16,512]{2,1,0:T(8,128)(2,1)} %copy-done.3) | copy-start | bytes 3145732
  169.6 11.9 %copy-start.14 = (bf16[64,256]{1,0:T(8,128)(2,1)S(1)}, bf16[64,256]{1,0:T(8,128)(2,1)}, u32[]{:S(2)}) copy-start(bf16[64,256]{1,0:T(8,128)(2,1)} %reduce_sum.39) | copy-start | bytes 98308
  171.6 20.7 %collective-permute-start.9 = (bf16[256,512]{1,0:T(8,128)(2,1)}, bf16[256,512]{1,0:T(8,128)(2,1)S(1)}, u32[]{:S(2)}, u32[]{:S(2)}) collective-permute-start(bf16[256,512]{1,0:T(8,128)(2,1)} %fusion.7), channel_id=1, source_target_pairs={{0,1},{1,2},{2,3},{3,0},{4,5},{5,6},{6,7},{7,4},{8,9},{9,10},{10,1... | collective-permute-start | bytes 786440 | tf_op jit(solution)/shard_map/ppermute | solution.py:46
  176.6 29.8 %collective-permute-start.10 = (bf16[256,512]{1,0:T(8,128)(2,1)}, bf16[256,512]{1,0:T(8,128)(2,1)S(1)}, u32[]{:S(2)}, u32[]{:S(2)}) collective-permute-start(bf16[256,512]{1,0:T(8,128)(2,1)} %fusion.6), channel_id=1, source_target_pairs={{0,3},{1,0},{2,1},{3,2},{4,7},{5,4},{6,5},{7,6},{8,11},{9,8},{10,9... | collective-permute-start | bytes 786440 | tf_op jit(solution)/shard_map/ppermute | solution.py:46

commit v4 on v3

v4 whole, which is shorter than its diff:
```python
import jax
import jax.numpy as jnp
from jax import lax
from jax.sharding import Mesh, PartitionSpec as P

ADAPTER_RANK = 64
WORKING_SLOTS = 8
ADAPTER_SCALE = 0.5

f32 = jnp.float32
bf16 = jnp.bfloat16

REPLICA = ("y", "zl", "c")
TENSOR = ("x", "zh")


def after(value, *earlier):
    return lax.optimization_barrier((value,) + earlier)[0]


def following(value, earlier):
    first = earlier[0, 0]
    return jnp.where(first != first, jnp.nan, value).astype(value.dtype)


def picking(working_adapters, store_row, adapters):
    ids = working_adapters.reshape(-1)
    places = lax.broadcasted_iota(jnp.int32, (ids.shape[0], adapters), 1)
    rows = jnp.sum(jnp.where(ids[:, None] == places, store_row[None, :], 0), axis=1)
    return (rows[:, None] == places).astype(bf16)


def picked(pick, store):
    rows = jnp.dot(pick, store[:, 0, :], preferred_element_type=f32).astype(bf16)
    return rows.reshape(-1, WORKING_SLOTS, store.shape[2])


def sum_over(part, axis):
    size = lax.axis_size(axis)
    spread = jnp.broadcast_to(part[None], (size,) + part.shape)
    return jnp.sum(lax.all_to_all(spread, axis, split_axis=0, concat_axis=0, tiled=True), axis=0)


def shifted(value, axis, by):
    size = lax.axis_size(axis)
    return lax.ppermute(value, axis, [(i, (i + by) % size) for i in range(size)])


def body(x_block, weight, down_store, up_store, working_adapters, store_row, slot):
    rows, features = x_block.shape
    xs, zs = lax.axis_size("x"), lax.axis_size("zh")
    core, x_at, z_at = lax.axis_index("c"), lax.axis_index("x"), lax.axis_index("zh")
    half = features // 2

    pick = picking(working_adapters, store_row, down_store.shape[0])
    outgoing = jnp.concatenate([picked(pick, down_store), picked(pick, up_store)], axis=1)
    fetched = lax.all_to_all(outgoing, REPLICA, split_axis=0, concat_axis=0, tiled=True).transpose(1, 0, 2)
    down = fetched[:WORKING_SLOTS].reshape(WORKING_SLOTS * ADAPTER_RANK, features)
    up = fetched[WORKING_SLOTS:].reshape(WORKING_SLOTS * ADAPTER_RANK, features)

    def columns(x_by, z_by):
        return (lax.rem(x_at + x_by, xs) * zs + lax.rem(z_at + z_by, zs)) * features

    swapped = jnp.concatenate([x_block[:, half:], x_block[:, :half]], axis=1)
    ordered = jnp.where(core == 0, x_block, swapped)
    runs = [slice(k * (rows // zs), (k + 1) * (rows // zs)) for k in range(zs)]
    beside = after(jnp.concatenate([ordered[run] for run in runs], axis=1), outgoing)
    halves, blocks = [], []
    for by in range(1, xs):
        begin = lax.rem(x_at + by, xs) * zs * features
        part = lax.dynamic_slice(weight, (core * half, begin), (half, zs * features))
        part = shifted(jnp.concatenate([part, beside], axis=0), "x", by)
        halves.append(part[:half])
        blocks.append(jnp.concatenate([part[half:, k * features:(k + 1) * features] for k in range(zs)], axis=0))

    selector = slot[None, :] == jnp.arange(WORKING_SLOTS, dtype=jnp.int32)[:, None]
    all_ranks = lax.dot_general(down, x_block, (((1,), (1,)), ((), ())), preferred_element_type=f32)
    ranks = jnp.sum(all_ranks.reshape(WORKING_SLOTS, ADAPTER_RANK, rows) * selector.astype(f32)[:, None, :], axis=0)
    lhs_mine = jnp.concatenate([block[:, :half] for block in blocks], axis=1)
    lhs_other = jnp.concatenate([block[:, half:] for block in blocks], axis=1)
    ranks = sum_over(ranks, "x")
    high = ranks.astype(bf16)
    low = (ranks - high.astype(f32)).astype(bf16)
    both = jnp.concatenate([high, low], axis=1)

    mine = jnp.concatenate([following(halves[0], ranks)] + halves[1:], axis=0)
    other = shifted(mine, "c", 1)

    def at(part, z_by):
        return lax.dynamic_slice(part, (0, lax.rem(z_at + z_by, zs) * features), (part.shape[0], features))

    total = None
    for z_by in (2, 1, 3, 0):
        own = lax.dynamic_slice(weight, (0, columns(0, z_by)), (features, features))
        base = jnp.dot(x_block, own, preferred_element_type=f32)
        base = base + jnp.dot(lhs_mine, at(mine, z_by), preferred_element_type=f32)
        base = base + jnp.dot(lhs_other, at(other, z_by), preferred_element_type=f32)
        if z_by:
            block = shifted(jnp.concatenate([base.astype(bf16), both], axis=0), "zh", z_by).astype(f32)
            base = block[:rows]
            ranks = ranks + (block[rows:, :rows] + block[rows:, rows:])
        total = base if total is None else total + base
    rounded = ranks.astype(bf16)
    expanded = (rounded[None] * selector.astype(bf16)[:, None, :]).reshape(WORKING_SLOTS * ADAPTER_RANK, rows)
    term = lax.dot_general(expanded, up, (((0,), (0,)), ((), ())), preferred_element_type=f32)
    return (total + ADAPTER_SCALE * term).astype(bf16)


def solution(mesh):
    fine = Mesh(mesh.devices.reshape(8, 4, 2, 4, 4), ("y", "zl", "c", "x", "zh"))
    in_specs = (
        P(REPLICA, TENSOR),
        P(TENSOR, None),
        P(None, REPLICA, TENSOR),
        P(None, REPLICA, TENSOR),
        P(),
        P(),
        P(REPLICA),
    )
    return jax.shard_map(body, mesh=fine, in_specs=in_specs, out_specs=P(REPLICA, TENSOR), check_vma=False)
```

time: 210 us -> 194 us (0.924)
  the two profiles are of different devices: /device:TPU:3 before, /device:TPU:56 now
where the time goes in v4:
time: 194 us; the launch traced here: 191 us
  waiting for transfers between devices  94.4 us (49%)
  starting transfers between devices  53.1 us (27%)
  matrix products  21.2 us (11%)
  local copies, waits for them, and re-layouts  11.4 us (6%)
  other arithmetic  8.71 us (4%)
    ppermute x7, waiting for transfers between devices, shifted(): lax.ppermute(value, axis, [(i, (i + by) % size) for i in range(size)])  75.2 us
    ppermute x7, starting transfers between devices, shifted(): lax.ppermute(value, axis, [(i, (i + by) % size) for i in range(size)])  32.8 us
    all_to_all x1, starting transfers between devices, body(): lax.all_to_all(outgoing, REPLICA, split_axis=0, concat_axis=0, tiled=True)  16.9 us
    all_to_all x1, waiting for transfers between devices, body(): lax.all_to_all(outgoing, REPLICA, split_axis=0, concat_axis=0, tiled=True)  15.9 us
    dot_general x4, matrix products, body(): base = base + jnp.dot(lhs_mine, at(mine, z_by), preferred_element_type=f32)  6.04 us
    dot_general x4, matrix products, body(): jnp.dot(lhs_other, at(other, z_by), preferred_element_type=f32)  6 us
    dot_general x4, matrix products, body(): base = jnp.dot(x_block, own, preferred_element_type=f32)  5.36 us
  transfers between devices with their start and end apart: 9, of which 6 were waited for; matrix products, arithmetic and copies ran while one was open for 11% of the time, Pallas kernels for 0%

profile of v4, /device:TPU:56, one launch (start us, length us, event | category | flops | bytes accessed | tf_op | source)
XLA Modules:
  0.0 190.6 jit_solution(7636313341018679151)
XLA Ops:
  0.0 0.0 copy-start
  0.0 0.8 copy.18
  0.8 0.1 eq.42
  0.9 0.9 select_reduce_fusion
  1.9 0.0 copy-done
  1.9 0.5 fusion.4
  2.4 0.0 copy-start.1
  2.4 1.6 fusion.5
  3.9 1.1 pad_maximum_fusion.4
  5.1 16.9 %all-to-all-start = ((bf16[64,16,512]{2,1,0:T(8,128)(2,1)}), bf16[64,16,512]{2,1,0:T(8,128)(2,1)S(1)}, u32[]{:S(2)}, u32[]{:S(2)}) async-start(bf16[64,16,512]{2,1,0:T(8,128)(2,1)} %pad_maximum_fusion.4), calls=%async_computation | async-start | bytes 2097152 | tf_op jit(solution)/shard_map/all_to_all | solution.py:57
  22.0 0.0 copy-done.1
  22.0 0.1 maximum_select_fusion
  22.1 2.1 %fusion.64 = (bf16[256,2048]{1,0:T(8,128)(2,1)S(1)}, bf16[256,2048]{1,0:T(8,128)(2,1)S(1)}, bf16[256,2048]{1,0:T(8,128)(2,1)S(1)}) fusion(bf16[512,8192]{1,0:T(8,128)(2,1)} %param.8, s32[]{:T(128)S(6)} %select_n.63, s32[]{:T(128)S(6)} %select_n.64, s32[]{:T(128)S(6)} %select_n.69, s32[]{:T(128)S(6)} %select_n.68), kind=kLoop, calls=%fused_computation.97 | loop fusion | bytes 6291472 | tf_op jit(solution)/shard_map/dynamic_slice | solution.py:71
  24.2 0.0 copy-start.2
  24.3 2.0 %pad_maximum_fusion.3 = (bf16[320,2048]{1,0:T(8,128)(2,1)}, bf16[320,2048]{1,0:T(8,128)(2,1)S(1)}, bf16[320,2048]{1,0:T(8,128)(2,1)}) fusion(bf16[64,2048]{1,0:T(8,128)(2,1)S(1)} %pad_maximum_fusion.8, bf16[256,2048]{1,0:T(8,128)(2,1)S(1)} %get-tuple-element.9, bf16[256,2048]{1,0:T(8,128)(2,1)S(1)} %get-tuple-element.11, ...), kind=kLoop, calls=%fused_computation.3 | loop fusion | flops 6553600 | bytes 7340032 | tf_op jit(solution)/shard_map/concatenate | solution.py:72
  26.2 1.9 %collective-permute-start.1 = (bf16[320,2048]{1,0:T(8,128)(2,1)S(1)}, bf16[320,2048]{1,0:T(8,128)(2,1)}, u32[]{:S(2)}, u32[]{:S(2)}) collective-permute-start(bf16[320,2048]{1,0:T(8,128)(2,1)S(1)} %get-tuple-element.31), channel_id=1, source_target_pairs={{0,8},{4,12},{8,0},{12,4},{1,9},{5,13},{9,1},{13,5},{2,10},{6,14},... | collective-permute-start | bytes 3932168 | tf_op jit(solution)/shard_map/ppermute | solution.py:46
  28.2 2.3 %collective-permute-start.2 = (bf16[320,2048]{1,0:T(8,128)(2,1)}, bf16[320,2048]{1,0:T(8,128)(2,1)}, u32[]{:S(2)}, u32[]{:S(2)}) collective-permute-start(bf16[320,2048]{1,0:T(8,128)(2,1)} %get-tuple-element.32), channel_id=1, source_target_pairs={{0,12},{4,0},{8,4},{12,8},{1,13},{5,1},{9,5},{13,9},{2,14},{6,2},{... | collective-permute-start | bytes 3932168 | tf_op jit(solution)/shard_map/ppermute | solution.py:46
  30.5 3.5 %collective-permute-start = (bf16[320,2048]{1,0:T(8,128)(2,1)}, bf16[320,2048]{1,0:T(8,128)(2,1)}, u32[]{:S(2)}, u32[]{:S(2)}) collective-permute-start(bf16[320,2048]{1,0:T(8,128)(2,1)} %get-tuple-element.30), channel_id=1, source_target_pairs={{0,4},{4,8},{8,12},{12,0},{1,5},{5,9},{9,13},{13,1},{2,6},{6,10},{... | collective-permute-start | bytes 3932168 | tf_op jit(solution)/shard_map/ppermute | solution.py:46
  34.0 0.0 copy-done.2
  34.0 15.9 %all-to-all-done = bf16[64,16,512]{2,1,0:T(8,128)(2,1)S(1)} async-done(((bf16[64,16,512]{2,1,0:T(8,128)(2,1)}), bf16[64,16,512]{2,1,0:T(8,128)(2,1)S(1)}, u32[]{:S(2)}, u32[]{:S(2)}) %all-to-all-start) | async-done | bytes 1048608 | tf_op jit(solution)/shard_map/all_to_all | solution.py:57
  49.9 0.7 fusion.10
  50.7 0.7 broadcast_in_dim.20
  51.4 3.4 %all-to-all-start.1 = ((f32[4,64,256]{2,1,0:T(8,128)}), f32[4,64,256]{2,1,0:T(8,128)S(1)}, u32[]{:S(2)}, u32[]{:S(2)}) async-start(f32[4,64,256]{2,1,0:T(8,128)} %broadcast_in_dim.20), calls=%async_computation.1 | async-start | bytes 524288 | tf_op jit(solution)/shard_map/all_to_all | solution.py:41
  54.8 6.6 %collective-permute-done.1 = bf16[320,2048]{1,0:T(8,128)(2,1)} collective-permute-done((bf16[320,2048]{1,0:T(8,128)(2,1)S(1)}, bf16[320,2048]{1,0:T(8,128)(2,1)}, u32[]{:S(2)}, u32[]{:S(2)}) %collective-permute-start.1) | collective-permute-done | bytes 1310752 | tf_op jit(solution)/shard_map/ppermute | solution.py:46
  61.4 1.3 slice.177
  62.7 23.1 %collective-permute-done.2 = bf16[320,2048]{1,0:T(8,128)(2,1)} collective-permute-done((bf16[320,2048]{1,0:T(8,128)(2,1)}, bf16[320,2048]{1,0:T(8,128)(2,1)}, u32[]{:S(2)}, u32[]{:S(2)}) %collective-permute-start.2) | collective-permute-done | bytes 1310752 | tf_op jit(solution)/shard_map/ppermute | solution.py:46
  85.8 2.3 %slice.178 = bf16[256,2048]{1,0:T(8,128)(2,1)} slice(bf16[320,2048]{1,0:T(8,128)(2,1)} %collective-permute-done.2), slice={[0:256], [0:2048]} | slice | bytes 2097152 | tf_op jit(solution)/shard_map/slice | solution.py:73
  88.1 3.3 %all-to-all-done.1 = f32[4,64,256]{2,1,0:T(8,128)S(1)} async-done(((f32[4,64,256]{2,1,0:T(8,128)}), f32[4,64,256]{2,1,0:T(8,128)S(1)}, u32[]{:S(2)}, u32[]{:S(2)}) %all-to-all-start.1) | async-done | bytes 262176 | tf_op jit(solution)/shard_map/all_to_all | solution.py:41
  91.4 0.5 slice.175
  93.2 0.0 collective-permute-done
  93.2 1.3 slice_select_fusion
  94.6 2.9 %pad_maximum_fusion = bf16[768,2048]{1,0:T(8,128)(2,1)} fusion(bf16[256,2048]{1,0:T(8,128)(2,1)} %slice.178, bf16[256,2048]{1,0:T(8,128)(2,1)S(1)} %slice.177, bf16[256,2048]{1,0:T(8,128)(2,1)S(1)} %slice_select_fusion), kind=kLoop, calls=%fused_computation | loop fusion | flops 9437184 | bytes 6291456 | tf_op jit(solution)/shard_map/concatenate | solution.py:86
  97.4 1.9 %collective-permute-start.3 = (bf16[768,2048]{1,0:T(8,128)(2,1)}, bf16[768,2048]{1,0:T(8,128)(2,1)}, u32[]{:S(2)}, u32[]{:S(2)}) collective-permute-start(bf16[768,2048]{1,0:T(8,128)(2,1)} %pad_maximum_fusion), channel_id=1, source_target_pairs={{0,16},{16,0},{1,17},{17,1},{2,18},{18,2},{3,19},{19,3},{4,20},{20... | collective-permute-start | bytes 9437192 | tf_op jit(solution)/shard_map/ppermute | solution.py:46
  99.4 1.3 convolution_bitcast_fusion.1
  100.7 1.3 convolution_bitcast_fusion.2
  102.1 1.3 convolution_bitcast_fusion.3
  103.4 1.3 convolution_bitcast_fusion
  104.8 1.0 fusion.65
  105.8 1.0 fusion.66
  106.8 1.0 fusion.67
  107.8 0.6 copy.24
  108.4 0.0 collective-permute-done.3
  108.4 1.5 fusion.14
  110.0 1.5 fusion.7
  111.5 1.5 fusion.17
  113.0 1.5 fusion.8
  114.5 1.5 fusion.20
  116.0 1.5 fusion.9
  117.5 0.1 fusion.37
  117.6 13.4 %collective-permute-start.4 = (bf16[320,512]{1,0:T(8,128)(2,1)S(1)}, bf16[320,512]{1,0:T(8,128)(2,1)S(1)}, u32[]{:S(2)}, u32[]{:S(2)}) collective-permute-start(bf16[320,512]{1,0:T(8,128)(2,1)S(1)} %get-tuple-element.39), channel_id=1, source_target_pairs={{0,2},{1,3},{2,0},{3,1},{4,6},{5,7},{6,4},{7,5},{8,10},{9,11},{10,... | collective-permute-start | bytes 983048 | tf_op jit(solution)/shard_map/ppermute | solution.py:46
  131.0 6.1 %collective-permute-start.5 = (bf16[320,512]{1,0:T(8,128)(2,1)S(1)}, bf16[320,512]{1,0:T(8,128)(2,1)S(1)}, u32[]{:S(2)}, u32[]{:S(2)}) collective-permute-start(bf16[320,512]{1,0:T(8,128)(2,1)S(1)} %get-tuple-element.40), channel_id=1, source_target_pairs={{0,1},{1,2},{2,3},{3,0},{4,5},{5,6},{6,7},{7,4},{8,9},{9,10},{10,1... | collective-permute-start | bytes 983048 | tf_op jit(solution)/shard_map/ppermute | solution.py:46
  137.1 3.6 %collective-permute-start.6 = (bf16[320,512]{1,0:T(8,128)(2,1)S(1)}, bf16[320,512]{1,0:T(8,128)(2,1)S(1)}, u32[]{:S(2)}, u32[]{:S(2)}) collective-permute-start(bf16[320,512]{1,0:T(8,128)(2,1)S(1)} %get-tuple-element.41), channel_id=1, source_target_pairs={{0,3},{1,0},{2,1},{3,2},{4,7},{5,4},{6,5},{7,6},{8,11},{9,8},{10,9... | collective-permute-start | bytes 983048 | tf_op jit(solution)/shard_map/ppermute | solution.py:46
  140.8 1.5 fusion.11
  142.3 1.5 fusion.3
  143.8 0.0 collective-permute-done.4
  143.8 0.1 convert_element_type.63
  143.9 11.0 %collective-permute-done.5 = bf16[320,512]{1,0:T(8,128)(2,1)S(1)} collective-permute-done((bf16[320,512]{1,0:T(8,128)(2,1)S(1)}, bf16[320,512]{1,0:T(8,128)(2,1)S(1)}, u32[]{:S(2)}, u32[]{:S(2)}) %collective-permute-start.5) | collective-permute-done | bytes 327712 | tf_op jit(solution)/shard_map/ppermute | solution.py:46
  154.9 0.1 convert_element_type.65
  155.0 34.5 %collective-permute-done.6 = bf16[320,512]{1,0:T(8,128)(2,1)S(1)} collective-permute-done((bf16[320,512]{1,0:T(8,128)(2,1)S(1)}, bf16[320,512]{1,0:T(8,128)(2,1)S(1)}, u32[]{:S(2)}, u32[]{:S(2)}) %collective-permute-start.6) | collective-permute-done | bytes 327712 | tf_op jit(solution)/shard_map/ppermute | solution.py:46
  189.5 0.1 convert_element_type.67
  189.6 1.0 fusion.26
  (13 shorter events, 0.2 us)
Async XLA Ops:
  0.0 1.9 copy-start
  2.4 19.6 %copy-start.1 = (bf16[256,512]{1,0:T(8,128)(2,1)S(1)}, bf16[256,512]{1,0:T(8,128)(2,1)}, u32[]{:S(2)}) copy-start(bf16[256,512]{1,0:T(8,128)(2,1)} %param.7) | copy-start | bytes 786436
  5.1 44.9 %all-to-all-start = ((bf16[64,16,512]{2,1,0:T(8,128)(2,1)}), bf16[64,16,512]{2,1,0:T(8,128)(2,1)S(1)}, u32[]{:S(2)}, u32[]{:S(2)}) async-start(bf16[64,16,512]{2,1,0:T(8,128)(2,1)} %pad_maximum_fusion.4), calls=%async_computation | async-start | bytes 2097152 | tf_op jit(solution)/shard_map/all_to_all | solution.py:57
  24.2 9.8 %copy-start.2 = (s32[256]{0:T(256)S(1)}, s32[256]{0:T(256)}, u32[]{:S(2)}) copy-start(s32[256]{0:T(256)} %param.13) | copy-start | bytes 3076
  26.2 35.2 %collective-permute-start.1 = (bf16[320,2048]{1,0:T(8,128)(2,1)S(1)}, bf16[320,2048]{1,0:T(8,128)(2,1)}, u32[]{:S(2)}, u32[]{:S(2)}) collective-permute-start(bf16[320,2048]{1,0:T(8,128)(2,1)S(1)} %get-tuple-element.31), channel_id=1, source_target_pairs={{0,8},{4,12},{8,0},{12,4},{1,9},{5,13},{9,1},{13,5},{2,10},{6,14},... | collective-permute-start | bytes 3932168 | tf_op jit(solution)/shard_map/ppermute | solution.py:46
  28.2 57.7 %collective-permute-start.2 = (bf16[320,2048]{1,0:T(8,128)(2,1)}, bf16[320,2048]{1,0:T(8,128)(2,1)}, u32[]{:S(2)}, u32[]{:S(2)}) collective-permute-start(bf16[320,2048]{1,0:T(8,128)(2,1)} %get-tuple-element.32), channel_id=1, source_target_pairs={{0,12},{4,0},{8,4},{12,8},{1,13},{5,1},{9,5},{13,9},{2,14},{6,2},{... | collective-permute-start | bytes 3932168 | tf_op jit(solution)/shard_map/ppermute | solution.py:46
  30.5 62.8 %collective-permute-start = (bf16[320,2048]{1,0:T(8,128)(2,1)}, bf16[320,2048]{1,0:T(8,128)(2,1)}, u32[]{:S(2)}, u32[]{:S(2)}) collective-permute-start(bf16[320,2048]{1,0:T(8,128)(2,1)} %get-tuple-element.30), channel_id=1, source_target_pairs={{0,4},{4,8},{8,12},{12,0},{1,5},{5,9},{9,13},{13,1},{2,6},{6,10},{... | collective-permute-start | bytes 3932168 | tf_op jit(solution)/shard_map/ppermute | solution.py:46
  51.4 40.0 %all-to-all-start.1 = ((f32[4,64,256]{2,1,0:T(8,128)}), f32[4,64,256]{2,1,0:T(8,128)S(1)}, u32[]{:S(2)}, u32[]{:S(2)}) async-start(f32[4,64,256]{2,1,0:T(8,128)} %broadcast_in_dim.20), calls=%async_computation.1 | async-start | bytes 524288 | tf_op jit(solution)/shard_map/all_to_all | solution.py:41
  97.4 11.0 %collective-permute-start.3 = (bf16[768,2048]{1,0:T(8,128)(2,1)}, bf16[768,2048]{1,0:T(8,128)(2,1)}, u32[]{:S(2)}, u32[]{:S(2)}) collective-permute-start(bf16[768,2048]{1,0:T(8,128)(2,1)} %pad_maximum_fusion), channel_id=1, source_target_pairs={{0,16},{16,0},{1,17},{17,1},{2,18},{18,2},{3,19},{19,3},{4,20},{20... | collective-permute-start | bytes 9437192 | tf_op jit(solution)/shard_map/ppermute | solution.py:46
  117.6 26.2 %collective-permute-start.4 = (bf16[320,512]{1,0:T(8,128)(2,1)S(1)}, bf16[320,512]{1,0:T(8,128)(2,1)S(1)}, u32[]{:S(2)}, u32[]{:S(2)}) collective-permute-start(bf16[320,512]{1,0:T(8,128)(2,1)S(1)} %get-tuple-element.39), channel_id=1, source_target_pairs={{0,2},{1,3},{2,0},{3,1},{4,6},{5,7},{6,4},{7,5},{8,10},{9,11},{10,... | collective-permute-start | bytes 983048 | tf_op jit(solution)/shard_map/ppermute | solution.py:46
  131.0 23.9 %collective-permute-start.5 = (bf16[320,512]{1,0:T(8,128)(2,1)S(1)}, bf16[320,512]{1,0:T(8,128)(2,1)S(1)}, u32[]{:S(2)}, u32[]{:S(2)}) collective-permute-start(bf16[320,512]{1,0:T(8,128)(2,1)S(1)} %get-tuple-element.40), channel_id=1, source_target_pairs={{0,1},{1,2},{2,3},{3,0},{4,5},{5,6},{6,7},{7,4},{8,9},{9,10},{10,1... | collective-permute-start | bytes 983048 | tf_op jit(solution)/shard_map/ppermute | solution.py:46
  137.1 52.3 %collective-permute-start.6 = (bf16[320,512]{1,0:T(8,128)(2,1)S(1)}, bf16[320,512]{1,0:T(8,128)(2,1)S(1)}, u32[]{:S(2)}, u32[]{:S(2)}) collective-permute-start(bf16[320,512]{1,0:T(8,128)(2,1)S(1)} %get-tuple-element.41), channel_id=1, source_target_pairs={{0,3},{1,0},{2,1},{3,2},{4,7},{5,4},{6,5},{7,6},{8,11},{9,8},{10,9... | collective-permute-start | bytes 983048 | tf_op jit(solution)/shard_map/ppermute | solution.py:46

commit v5 on v4

--- a/solution.py
+++ b/solution.py
@@ -58,43 +58,50 @@
     down = fetched[:WORKING_SLOTS].reshape(WORKING_SLOTS * ADAPTER_RANK, features)
     up = fetched[WORKING_SLOTS:].reshape(WORKING_SLOTS * ADAPTER_RANK, features)
 
-    def columns(x_by, z_by):
-        return (lax.rem(x_at + x_by, xs) * zs + lax.rem(z_at + z_by, zs)) * features
-
     swapped = jnp.concatenate([x_block[:, half:], x_block[:, :half]], axis=1)
     ordered = jnp.where(core == 0, x_block, swapped)
     runs = [slice(k * (rows // zs), (k + 1) * (rows // zs)) for k in range(zs)]
-    beside = after(jnp.concatenate([ordered[run] for run in runs], axis=1), outgoing)
-    halves, blocks = [], []
+    beside = jnp.concatenate([ordered[run] for run in runs], axis=1)
+    parts = []
     for by in range(1, xs):
         begin = lax.rem(x_at + by, xs) * zs * features
         part = lax.dynamic_slice(weight, (core * half, begin), (half, zs * features))
-        part = shifted(jnp.concatenate([part, beside], axis=0), "x", by)
-        halves.append(part[:half])
-        blocks.append(jnp.concatenate([part[half:, k * features:(k + 1) * features] for k in range(zs)], axis=0))
+        parts.append(shifted(jnp.concatenate([part, beside], axis=0), "x", by))
+    ahead, across, behind = parts
+
+    def requests_of(part):
+        block = jnp.concatenate([part[half:, k * features:(k + 1) * features] for k in range(zs)], axis=0)
+        return block[:, :half], block[:, half:]
+
+    def product(part):
+        mine, other = requests_of(part)
+        far = shifted(part, "c", 1)
+        return jnp.dot(mine, part[:half], preferred_element_type=f32) + jnp.dot(
+            other, far[:half], preferred_element_type=f32
+        )
+
+    own = lax.dynamic_slice(weight, (0, x_at * zs * features), (features, zs * features))
+    near = jnp.dot(x_block, own, preferred_element_type=f32) + product(ahead) + product(behind)
 
     selector = slot[None, :] == jnp.arange(WORKING_SLOTS, dtype=jnp.int32)[:, None]
     all_ranks = lax.dot_general(down, x_block, (((1,), (1,)), ((), ())), preferred_element_type=f32)
     ranks = jnp.sum(all_ranks.reshape(WORKING_SLOTS, ADAPTER_RANK, rows) * selector.astype(f32)[:, None, :], axis=0)
-    lhs_mine = jnp.concatenate([block[:, :half] for block in blocks], axis=1)
-    lhs_other = jnp.concatenate([block[:, half:] for block in blocks], axis=1)
     ranks = sum_over(ranks, "x")
-    high = ranks.astype(bf16)
-    low = (ranks - high.astype(f32)).astype(bf16)
-    both = jnp.concatenate([high, low], axis=1)
+    high = lax.reduce_precision(ranks, 8, 7)
+    both = jnp.concatenate([high, ranks - high], axis=1).astype(bf16)
 
-    mine = jnp.concatenate([following(halves[0], ranks)] + halves[1:], axis=0)
-    other = shifted(mine, "c", 1)
+    across = following(following(across, near), ranks)
+    other_across = shifted(across, "c", 1)
+    lhs_mine, lhs_other = requests_of(across)
 
-    def at(part, z_by):
-        return lax.dynamic_slice(part, (0, lax.rem(z_at + z_by, zs) * features), (part.shape[0], features))
+    def at(part, z_by, count):
+        return lax.dynamic_slice(part, (0, lax.rem(z_at + z_by, zs) * features), (count, features))
 
     total = None
     for z_by in (2, 1, 3, 0):
-        own = lax.dynamic_slice(weight, (0, columns(0, z_by)), (features, features))
-        base = jnp.dot(x_block, own, preferred_element_type=f32)
-        base = base + jnp.dot(lhs_mine, at(mine, z_by), preferred_element_type=f32)
-        base = base + jnp.dot(lhs_other, at(other, z_by), preferred_element_type=f32)
+        base = at(near, z_by, rows)
+        base = base + jnp.dot(lhs_mine, at(across, z_by, half), preferred_element_type=f32)
+        base = base + jnp.dot(lhs_other, at(other_across, z_by, half), preferred_element_type=f32)
         if z_by:
             block = shifted(jnp.concatenate([base.astype(bf16), both], axis=0), "zh", z_by).astype(f32)
             base = block[:rows]

time: 194 us -> 211 us (1.088)
  other arithmetic: 8.71 us -> 17.9 us
  starting transfers between devices: 53.1 us -> 58.7 us
  waiting for transfers between devices: 94.4 us -> 97.2 us
  local copies, waits for them, and re-layouts: 11.4 us -> 8.68 us
    ppermute x7 -> x9, waiting for transfers between devices: 75.2 us -> 95 us  [shifted(): lax.ppermute(value, axis, [(i, (i + by) % size) for i in range(size)])]
    all_to_all x1, waiting for transfers between devices: 15.9 us -> 0.01 us  [body(): lax.all_to_all(outgoing, REPLICA, split_axis=0, concat_axis=0, tiled=True)]
    ppermute x7 -> x9, starting transfers between devices: 32.8 us -> 37.7 us  [shifted(): lax.ppermute(value, axis, [(i, (i + by) % size) for i in range(size)])]
    slice x9 -> x4, local copies, waits for them, and re-layouts: 6.58 us -> 1.96 us  [the longest x3 1.94 us: requests_of(): part[half:, k * features:(k + 1) * features]]
    dot_general x12 -> x13, matrix products: 17.4 us -> 20.7 us  [the longest x4 5.48 us: body(): jnp.dot(lhs_other, at(other_across, z_by, half), preferred_element_type=f32)]
    concatenate x6 -> x4, other arithmetic: 4.92 us -> 8.02 us  [the longest x1 7.96 us: body(): parts.append(shifted(jnp.concatenate([part, beside], axis=0), 'x', by))]
    convert_element_type x3, other arithmetic: 0.2 us -> 3.12 us  [body(): shifted(jnp.concatenate([base.astype(bf16), both], axis=0), 'zh', z_by)]
  transfers between devices with their start and end apart: 9 -> 11, of which waited for: 6 -> 5; matrix products, arithmetic and copies ran while one was open for 11% -> 17% of each run, Pallas kernels for 0% -> 0%
where the time goes in v5:
time: 211 us; the launch traced here: 208 us
  waiting for transfers between devices  97.2 us (46%)
  starting transfers between devices  58.7 us (28%)
  matrix products  22.7 us (11%)
  other arithmetic  17.9 us (8%)
  local copies, waits for them, and re-layouts  8.68 us (4%)
  between operations  3.15 us (1%)
    ppermute x9, waiting for transfers between devices, shifted(): lax.ppermute(value, axis, [(i, (i + by) % size) for i in range(size)])  95 us
    ppermute x9, starting transfers between devices, shifted(): lax.ppermute(value, axis, [(i, (i + by) % size) for i in range(size)])  37.7 us
    all_to_all x1, starting transfers between devices, body(): lax.all_to_all(outgoing, REPLICA, split_axis=0, concat_axis=0, tiled=True)  17 us
    concatenate x1, other arithmetic, body(): parts.append(shifted(jnp.concatenate([part, beside], axis=0), 'x', by))  7.96 us
    dot_general x4, matrix products, body(): jnp.dot(lhs_other, at(other_across, z_by, half), preferred_element_type=f32)  5.48 us
    dot_general x2, matrix products, product(): jnp.dot(other, far[:half], preferred_element_type=f32)  4.76 us
    dot_general x4, matrix products, body(): jnp.dot(lhs_mine, at(across, z_by, half), preferred_element_type=f32)  4.69 us
  transfers between devices with their start and end apart: 11, of which 5 were waited for; matrix products, arithmetic and copies ran while one was open for 17% of the time, Pallas kernels for 0%

profile of v5, /device:TPU:56, one launch (start us, length us, event | category | flops | bytes accessed | tf_op | source)
XLA Modules:
  0.0 208.4 jit_solution(6848524240420766714)
XLA Ops:
  0.0 0.0 copy-start
  0.0 0.9 copy.15
  0.9 0.1 eq.42
  1.0 0.9 select_reduce_fusion
  1.9 0.0 copy-done
  1.9 0.5 fusion.3
  2.4 0.0 copy-done.4
  2.4 0.5 fusion.4
  2.9 1.2 pad_maximum_fusion.4
  4.1 17.0 %all-to-all-start = ((bf16[64,16,512]{2,1,0:T(8,128)(2,1)}), bf16[64,16,512]{2,1,0:T(8,128)(2,1)S(1)}, u32[]{:S(2)}, u32[]{:S(2)}) async-start(bf16[64,16,512]{2,1,0:T(8,128)(2,1)} %pad_maximum_fusion.4), calls=%async_computation | async-start | bytes 2097152 | tf_op jit(solution)/shard_map/all_to_all | solution.py:57
  21.1 0.0 copy-done.2
  21.2 0.1 maximum_select_fusion
  21.3 2.1 %fusion.80 = (bf16[256,2048]{1,0:T(8,128)(2,1)S(1)}, bf16[256,2048]{1,0:T(8,128)(2,1)S(1)}, bf16[256,2048]{1,0:T(8,128)(2,1)S(1)}) fusion(bf16[512,8192]{1,0:T(8,128)(2,1)} %param.8, s32[]{:T(128)S(6)} %select_n.64, s32[]{:T(128)S(6)} %select_n.68, s32[]{:T(128)S(6)} %select_n.65, s32[]{:T(128)S(6)} %select_n.73), kind=kLoop, calls=%fused_computation.105 | loop fusion | bytes 6291472 | tf_op jit(solution)/shard_map/dynamic_slice | solution.py:68
  23.4 0.0 copy-start.3
  23.4 8.0 %pad_maximum_fusion.2 = (bf16[320,2048]{1,0:T(8,128)(2,1)}, bf16[320,2048]{1,0:T(8,128)(2,1)}, bf16[320,2048]{1,0:T(8,128)(2,1)}) fusion(bf16[256,2048]{1,0:T(8,128)(2,1)S(1)} %get-tuple-element.5, bf16[64,512]{1,0:T(8,128)(2,1)S(1)} %get-tuple-element.24, bf16[64,512]{1,0:T(8,128)(2,1)S(1)} %get-tuple-element.25, bf16[64,512]{1,0:T(8,128)(2,1)S(1)} %get-tuple-element.26, ...), kind=kLoop, calls=%fused_computation.8 | loop fusion | flops 10485760 | bytes 7340032 | tf_op jit(solution)/shard_map/concatenate | solution.py:69
  31.4 1.9 collective-permute-start
  33.3 5.1 %collective-permute-start.2 = (bf16[320,2048]{1,0:T(8,128)(2,1)}, bf16[320,2048]{1,0:T(8,128)(2,1)S(1)}, u32[]{:S(2)}, u32[]{:S(2)}) collective-permute-start(bf16[320,2048]{1,0:T(8,128)(2,1)} %get-tuple-element.20), channel_id=1, source_target_pairs={{0,12},{4,0},{8,4},{12,8},{1,13},{5,1},{9,5},{13,9},{2,14},{6,2},{... | collective-permute-start | bytes 3932168 | tf_op jit(solution)/shard_map/ppermute | solution.py:46
  38.4 1.9 collective-permute-start.4
  40.4 0.0 copy-done.3
  40.4 2.3 %convolution_bitcast_fusion = f32[256,2048]{1,0:T(8,128)S(1)} fusion(bf16[256,512]{1,0:T(8,128)(2,1)S(1)} %copy-done.2, bf16[512,8192]{1,0:T(8,128)(2,1)} %param.8, s32[]{:T(128)S(6)} %select_n.63), kind=kOutput, calls=%fused_computation | convolution fusion | flops 536870912 | bytes 4456452 | tf_op jit(solution)/shard_map/dot_general | solution.py:84
  42.7 51.0 %collective-permute-done = bf16[320,2048]{1,0:T(8,128)(2,1)} collective-permute-done((bf16[320,2048]{1,0:T(8,128)(2,1)}, bf16[320,2048]{1,0:T(8,128)(2,1)}, u32[]{:S(2)}, u32[]{:S(2)}) %collective-permute-start) | collective-permute-done | bytes 1310752 | tf_op jit(solution)/shard_map/ppermute | solution.py:46
  93.7 1.9 collective-permute-start.1
  95.6 0.0 collective-permute-done.2
  95.6 2.4 %collective-permute-start.3 = (bf16[320,2048]{1,0:T(8,128)(2,1)S(1)}, bf16[320,2048]{1,0:T(8,128)(2,1)}, u32[]{:S(2)}, u32[]{:S(2)}) collective-permute-start(bf16[320,2048]{1,0:T(8,128)(2,1)S(1)} %collective-permute-done.2), channel_id=1, source_target_pairs={{0,16},{16,0},{1,17},{17,1},{2,18},{18,2},{3,19},{19,3},{4,20},{20... | collective-permute-start | bytes 3932168 | tf_op jit(solution)/shard_map/ppermute | solution.py:46
  98.1 1.0 fusion.83
  99.1 1.8 fusion.8
  100.9 1.7 fusion.11
  102.5 0.0 collective-permute-done.1
  102.5 1.8 fusion.1
  104.3 0.0 all-to-all-done
  104.3 0.7 fusion.6
  105.1 0.7 broadcast_in_dim.32
  105.8 4.0 %all-to-all-start.1 = ((f32[4,64,256]{2,1,0:T(8,128)}), f32[4,64,256]{2,1,0:T(8,128)}, u32[]{:S(2)}, u32[]{:S(2)}) async-start(f32[4,64,256]{2,1,0:T(8,128)} %broadcast_in_dim.32), calls=%async_computation.1 | async-start | bytes 524288 | tf_op jit(solution)/shard_map/all_to_all | solution.py:41
  109.8 0.0 collective-permute-done.3
  109.9 3.0 %fusion = f32[256,2048]{1,0:T(8,128)S(1)} fusion(f32[256,2048]{1,0:T(8,128)} %fusion.1, f32[256,2048]{1,0:T(8,128)} %fusion.8, bf16[320,2048]{1,0:T(8,128)(2,1)} %collective-permute-done.3, bf16[256,512]{1,0:T(8,128)(2,1)S(1)} %pad_maximum_fusion.7), kind=kOutput, calls=%fused_computation.2 | convolution fusion | flops 269484032 | bytes 7471104 | tf_op jit(solution)/shard_map/dot_general | solution.py:79
  112.8 0.6 slice.185
  114.8 2.2 %all-to-all-done.1 = f32[4,64,256]{2,1,0:T(8,128)} async-done(((f32[4,64,256]{2,1,0:T(8,128)}), f32[4,64,256]{2,1,0:T(8,128)}, u32[]{:S(2)}, u32[]{:S(2)}) %all-to-all-start.1) | async-done | bytes 262176 | tf_op jit(solution)/shard_map/all_to_all | solution.py:41
  117.0 1.0 reduce_sum.29
  118.0 0.5 slice.184
  119.8 0.0 collective-permute-done.4
  119.8 2.6 %select_select_fusion = bf16[320,2048]{1,0:T(8,128)(2,1)} fusion(bf16[320,2048]{1,0:T(8,128)(2,1)} %collective-permute-done.4, pred[]{:T(512)} %bitcast.8, pred[]{:T(512)} %bitcast.7), kind=kLoop, calls=%fused_computation.10 | loop fusion | flops 1310720 | bytes 2621442 | tf_op jit(solution)/shard_map/jit(_where)/select_n | solution.py:23
  122.4 1.9 collective-permute-start.5
  124.3 1.0 fusion.81
  125.3 1.2 fusion.36
  126.5 1.2 fusion.42
  127.7 1.2 fusion.48
  128.9 0.0 collective-permute-done.5
  128.9 1.2 add_convert_fusion
  130.1 1.2 add_convert_fusion.1
  131.3 1.2 add_convert_fusion.2
  132.4 0.9 fusion.23
  133.4 12.7 %collective-permute-start.6 = (bf16[320,512]{1,0:T(8,128)(2,1)}, bf16[320,512]{1,0:T(8,128)(2,1)}, u32[]{:S(2)}, u32[]{:S(2)}) collective-permute-start(bf16[320,512]{1,0:T(8,128)(2,1)} %get-tuple-element.29), channel_id=1, source_target_pairs={{0,2},{1,3},{2,0},{3,1},{4,6},{5,7},{6,4},{7,5},{8,10},{9,11},{10,... | collective-permute-start | bytes 983048 | tf_op jit(solution)/shard_map/ppermute | solution.py:46
  146.1 6.1 %collective-permute-start.7 = (bf16[320,512]{1,0:T(8,128)(2,1)}, bf16[320,512]{1,0:T(8,128)(2,1)}, u32[]{:S(2)}, u32[]{:S(2)}) collective-permute-start(bf16[320,512]{1,0:T(8,128)(2,1)} %get-tuple-element.30), channel_id=1, source_target_pairs={{0,1},{1,2},{2,3},{3,0},{4,5},{5,6},{6,7},{7,4},{8,9},{9,10},{10,1... | collective-permute-start | bytes 983048 | tf_op jit(solution)/shard_map/ppermute | solution.py:46
  152.2 3.7 %collective-permute-start.8 = (bf16[320,512]{1,0:T(8,128)(2,1)S(1)}, bf16[320,512]{1,0:T(8,128)(2,1)}, u32[]{:S(2)}, u32[]{:S(2)}) collective-permute-start(bf16[320,512]{1,0:T(8,128)(2,1)S(1)} %get-tuple-element.31), channel_id=1, source_target_pairs={{0,3},{1,0},{2,1},{3,2},{4,7},{5,4},{6,5},{7,6},{8,11},{9,8},{10,9... | collective-permute-start | bytes 983048 | tf_op jit(solution)/shard_map/ppermute | solution.py:46
  155.9 1.8 copy.19
  157.7 1.2 fusion.30
  158.9 1.5 collective-permute-done.6
  160.4 1.0 convert_element_type.53
  161.5 8.8 %collective-permute-done.7 = bf16[320,512]{1,0:T(8,128)(2,1)} collective-permute-done((bf16[320,512]{1,0:T(8,128)(2,1)}, bf16[320,512]{1,0:T(8,128)(2,1)}, u32[]{:S(2)}, u32[]{:S(2)}) %collective-permute-start.7) | collective-permute-done | bytes 327712 | tf_op jit(solution)/shard_map/ppermute | solution.py:46
  170.2 1.0 convert_element_type.55
  171.3 33.7 %collective-permute-done.8 = bf16[320,512]{1,0:T(8,128)(2,1)} collective-permute-done((bf16[320,512]{1,0:T(8,128)(2,1)S(1)}, bf16[320,512]{1,0:T(8,128)(2,1)}, u32[]{:S(2)}, u32[]{:S(2)}) %collective-permute-start.8) | collective-permute-done | bytes 327712 | tf_op jit(solution)/shard_map/ppermute | solution.py:46
  205.0 1.0 convert_element_type.57
  206.1 0.3 fusion.5
  206.4 1.9 fusion.16
  (13 shorter events, 0.2 us)
Async XLA Ops:
  0.0 1.9 copy-start
  0.0 2.4 %copy-start.4 = (bf16[512,1,512]{2,0,1:T(8,128)(2,1)S(1)}, bf16[512,1,512]{2,0,1:T(8,128)(2,1)}, u32[]{:S(2)}) copy-start(bf16[512,1,512]{2,0,1:T(8,128)(2,1)} %param.10) | copy-start | bytes 1572868
  4.1 17.0 %copy-start.2 = (bf16[256,512]{1,0:T(8,128)(2,1)S(1)}, bf16[256,512]{1,0:T(8,128)(2,1)}, u32[]{:S(2)}) copy-start(bf16[256,512]{1,0:T(8,128)(2,1)} %param.7) | copy-start | bytes 786436
  4.1 100.2 %all-to-all-start = ((bf16[64,16,512]{2,1,0:T(8,128)(2,1)}), bf16[64,16,512]{2,1,0:T(8,128)(2,1)S(1)}, u32[]{:S(2)}, u32[]{:S(2)}) async-start(bf16[64,16,512]{2,1,0:T(8,128)(2,1)} %pad_maximum_fusion.4), calls=%async_computation | async-start | bytes 2097152 | tf_op jit(solution)/shard_map/all_to_all | solution.py:57
  23.4 17.0 %copy-start.3 = (s32[256]{0:T(256)S(1)}, s32[256]{0:T(256)}, u32[]{:S(2)}) copy-start(s32[256]{0:T(256)} %param.13) | copy-start | bytes 3076
  31.4 62.3 %collective-permute-start = (bf16[320,2048]{1,0:T(8,128)(2,1)}, bf16[320,2048]{1,0:T(8,128)(2,1)}, u32[]{:S(2)}, u32[]{:S(2)}) collective-permute-start(bf16[320,2048]{1,0:T(8,128)(2,1)} %get-tuple-element.22), channel_id=1, source_target_pairs={{0,4},{4,8},{8,12},{12,0},{1,5},{5,9},{9,13},{13,1},{2,6},{6,10},{... | collective-permute-start | bytes 3932168 | tf_op jit(solution)/shard_map/ppermute | solution.py:46
  33.3 62.3 %collective-permute-start.2 = (bf16[320,2048]{1,0:T(8,128)(2,1)}, bf16[320,2048]{1,0:T(8,128)(2,1)S(1)}, u32[]{:S(2)}, u32[]{:S(2)}) collective-permute-start(bf16[320,2048]{1,0:T(8,128)(2,1)} %get-tuple-element.20), channel_id=1, source_target_pairs={{0,12},{4,0},{8,4},{12,8},{1,13},{5,1},{9,5},{13,9},{2,14},{6,2},{... | collective-permute-start | bytes 3932168 | tf_op jit(solution)/shard_map/ppermute | solution.py:46
  38.4 81.4 %collective-permute-start.4 = (bf16[320,2048]{1,0:T(8,128)(2,1)}, bf16[320,2048]{1,0:T(8,128)(2,1)}, u32[]{:S(2)}, u32[]{:S(2)}) collective-permute-start(bf16[320,2048]{1,0:T(8,128)(2,1)} %get-tuple-element.21), channel_id=1, source_target_pairs={{0,8},{4,12},{8,0},{12,4},{1,9},{5,13},{9,1},{13,5},{2,10},{6,14},... | collective-permute-start | bytes 3932168 | tf_op jit(solution)/shard_map/ppermute | solution.py:46
  93.7 8.8 %collective-permute-start.1 = (bf16[320,2048]{1,0:T(8,128)(2,1)}, bf16[320,2048]{1,0:T(8,128)(2,1)S(1)}, u32[]{:S(2)}, u32[]{:S(2)}) collective-permute-start(bf16[320,2048]{1,0:T(8,128)(2,1)} %collective-permute-done), channel_id=1, source_target_pairs={{0,16},{16,0},{1,17},{17,1},{2,18},{18,2},{3,19},{19,3},{4,20},{20... | collective-permute-start | bytes 3932168 | tf_op jit(solution)/shard_map/ppermute | solution.py:46
  95.6 14.2 %collective-permute-start.3 = (bf16[320,2048]{1,0:T(8,128)(2,1)S(1)}, bf16[320,2048]{1,0:T(8,128)(2,1)}, u32[]{:S(2)}, u32[]{:S(2)}) collective-permute-start(bf16[320,2048]{1,0:T(8,128)(2,1)S(1)} %collective-permute-done.2), channel_id=1, source_target_pairs={{0,16},{16,0},{1,17},{17,1},{2,18},{18,2},{3,19},{19,3},{4,20},{20... | collective-permute-start | bytes 3932168 | tf_op jit(solution)/shard_map/ppermute | solution.py:46
  104.3 5.5 %copy-start.1 = (bf16[64,16,512]{2,1,0:T(8,128)(2,1)}, bf16[64,16,512]{2,1,0:T(8,128)(2,1)S(1)}, u32[]{:S(2)}) copy-start(bf16[64,16,512]{2,1,0:T(8,128)(2,1)S(1)} %all-to-all-done) | copy-start | bytes 3145732
  105.8 11.2 %all-to-all-start.1 = ((f32[4,64,256]{2,1,0:T(8,128)}), f32[4,64,256]{2,1,0:T(8,128)}, u32[]{:S(2)}, u32[]{:S(2)}) async-start(f32[4,64,256]{2,1,0:T(8,128)} %broadcast_in_dim.32), calls=%async_computation.1 | async-start | bytes 524288 | tf_op jit(solution)/shard_map/all_to_all | solution.py:41
  122.4 6.5 %collective-permute-start.5 = (bf16[320,2048]{1,0:T(8,128)(2,1)}, bf16[320,2048]{1,0:T(8,128)(2,1)}, u32[]{:S(2)}, u32[]{:S(2)}) collective-permute-start(bf16[320,2048]{1,0:T(8,128)(2,1)} %select_select_fusion), channel_id=1, source_target_pairs={{0,16},{16,0},{1,17},{17,1},{2,18},{18,2},{3,19},{19,3},{4,20},{20... | collective-permute-start | bytes 3932168 | tf_op jit(solution)/shard_map/ppermute | solution.py:46
  133.4 27.0 %collective-permute-start.6 = (bf16[320,512]{1,0:T(8,128)(2,1)}, bf16[320,512]{1,0:T(8,128)(2,1)}, u32[]{:S(2)}, u32[]{:S(2)}) collective-permute-start(bf16[320,512]{1,0:T(8,128)(2,1)} %get-tuple-element.29), channel_id=1, source_target_pairs={{0,2},{1,3},{2,0},{3,1},{4,6},{5,7},{6,4},{7,5},{8,10},{9,11},{10,... | collective-permute-start | bytes 983048 | tf_op jit(solution)/shard_map/ppermute | solution.py:46
  146.1 24.1 %collective-permute-start.7 = (bf16[320,512]{1,0:T(8,128)(2,1)}, bf16[320,512]{1,0:T(8,128)(2,1)}, u32[]{:S(2)}, u32[]{:S(2)}) collective-permute-start(bf16[320,512]{1,0:T(8,128)(2,1)} %get-tuple-element.30), channel_id=1, source_target_pairs={{0,1},{1,2},{2,3},{3,0},{4,5},{5,6},{6,7},{7,4},{8,9},{9,10},{10,1... | collective-permute-start | bytes 983048 | tf_op jit(solution)/shard_map/ppermute | solution.py:46
  152.2 52.8 %collective-permute-start.8 = (bf16[320,512]{1,0:T(8,128)(2,1)S(1)}, bf16[320,512]{1,0:T(8,128)(2,1)}, u32[]{:S(2)}, u32[]{:S(2)}) collective-permute-start(bf16[320,512]{1,0:T(8,128)(2,1)S(1)} %get-tuple-element.31), channel_id=1, source_target_pairs={{0,3},{1,0},{2,1},{3,2},{4,7},{5,4},{6,5},{7,6},{8,11},{9,8},{10,9... | collective-permute-start | bytes 983048 | tf_op jit(solution)/shard_map/ppermute | solution.py:46

commit v6 on v3

--- a/solution.py
+++ b/solution.py
@@ -81,29 +81,37 @@
     lhs_mine = jnp.concatenate([block[:rows, :half] for block in got], axis=1)
     lhs_other = jnp.concatenate([block[:rows, half:] for block in got], axis=1)
     far_mine = jnp.concatenate([block[rows:] for block in got], axis=0)
-    (far,) = product(far_mine, shifted(far_mine, "c", 1), (2,), weight)
-    far = far.astype(bf16)
-    far_sum = shifted(far, "zh", 2)
-
     selector = slot[None, :] == jnp.arange(WORKING_SLOTS, dtype=jnp.int32)[:, None]
     all_ranks = lax.dot_general(down, x_block, (((1,), (1,)), ((), ())), preferred_element_type=f32)
     ranks = jnp.sum(all_ranks.reshape(WORKING_SLOTS, ADAPTER_RANK, rows) * selector.astype(f32)[:, None, :], axis=0)
-    ranks = following(sum_over(ranks, "x"), far_sum)
-    rounded = sum_over(ranks, "zh").astype(bf16)
-    expanded = (rounded[None] * selector.astype(bf16)[:, None, :]).reshape(WORKING_SLOTS * ADAPTER_RANK, rows)
+    ranks = sum_over(ranks, "x")
+    high = lax.reduce_precision(ranks, 8, 7)
+    both = jnp.concatenate([high, ranks - high], axis=1).astype(bf16)
+
+    def with_ranks(base):
+        return jnp.concatenate([base.astype(bf16), both], axis=0)
+
+    (far,) = product(far_mine, shifted(far_mine, "c", 1), (2,), weight)
+    far = with_ranks(far)
+    far_sum = shifted(far, "zh", 2)
 
     near_weight = after(weight, far)
     near = [
         shifted(jnp.concatenate([weight_of(near_weight, by, z_by) for z_by in (1, 3, 0)], axis=1), "x", by)
         for by in range(1, xs)
     ]
-    near_mine = following(after(jnp.concatenate(near, axis=0), far_sum), rounded)
+    near_mine = following(jnp.concatenate(near, axis=0), far_sum)
     up_part, down_part, total = product(near_mine, shifted(near_mine, "c", 1), (1, 3, 0), weight)
-    up_sum = shifted(up_part.astype(bf16), "zh", 1)
-    down_sum = shifted(down_part.astype(bf16), "zh", 3)
+    up_sum = shifted(with_ranks(up_part), "zh", 1)
+    down_sum = shifted(with_ranks(down_part), "zh", 3)
+    for block in (far_sum, up_sum, down_sum):
+        block = block.astype(f32)
+        total = total + block[:rows]
+        ranks = ranks + (block[rows:, :rows] + block[rows:, rows:])
+    rounded = ranks.astype(bf16)
+    expanded = (rounded[None] * selector.astype(bf16)[:, None, :]).reshape(WORKING_SLOTS * ADAPTER_RANK, rows)
     term = lax.dot_general(expanded, up, (((0,), (0,)), ((), ())), preferred_element_type=f32)
-    total = total + far_sum.astype(f32) + ADAPTER_SCALE * term
-    return (total + up_sum.astype(f32) + down_sum.astype(f32)).astype(bf16)
+    return (total + ADAPTER_SCALE * term).astype(bf16)
 
 
 def solution(mesh):

time: 210 us -> 195 us (0.929)
  the two profiles are of different devices: /device:TPU:3 before, /device:TPU:56 now
where the time goes in v6:
time: 195 us; the launch traced here: 194 us
  waiting for transfers between devices  78.2 us (40%)
  starting transfers between devices  73.9 us (38%)
  matrix products  18.8 us (10%)
  local copies, waits for them, and re-layouts  12.4 us (6%)
  other arithmetic  8.13 us (4%)
  between operations  2.07 us (1%)
    ppermute x11, waiting for transfers between devices, shifted(): lax.ppermute(value, axis, [(i, (i + by) % size) for i in range(size)])  72.9 us
    ppermute x11, starting transfers between devices, shifted(): lax.ppermute(value, axis, [(i, (i + by) % size) for i in range(size)])  53.5 us
    all_to_all x1, starting transfers between devices, body(): lax.all_to_all(outgoing, REPLICA, split_axis=0, concat_axis=0, tiled=True)  17 us
    dot_general x4, matrix products, product(): own = jnp.dot(x_block, own, preferred_element_type=f32)  7.66 us
    all_to_all x1, waiting for transfers between devices, sum_over(): lax.all_to_all(spread, axis, split_axis=0, concat_axis=0, tiled=True)  5.29 us
    dot_general x2, matrix products, product(): jnp.dot(lhs_other, other, preferred_element_type=f32)  5.04 us
  transfers between devices with their start and end apart: 13, of which 9 were waited for; matrix products, arithmetic and copies ran while one was open for 9% of the time, Pallas kernels for 0%

profile of v6, /device:TPU:56, one launch (start us, length us, event | category | flops | bytes accessed | tf_op | source)
XLA Modules:
  0.0 193.5 jit_solution(11374549642835939817)
XLA Ops:
  0.0 0.8 copy.18
  0.8 0.1 eq.42
  0.9 0.9 select_reduce_fusion
  1.9 0.5 fusion.2
  2.4 1.5 fusion.1
  3.9 1.1 pad_maximum_fusion
  5.0 17.0 %all-to-all-start = ((bf16[64,16,512]{2,1,0:T(8,128)(2,1)}), bf16[64,16,512]{2,1,0:T(8,128)(2,1)S(1)}, u32[]{:S(2)}, u32[]{:S(2)}) async-start(bf16[64,16,512]{2,1,0:T(8,128)(2,1)} %pad_maximum_fusion), calls=%async_computation | async-start | bytes 2097152 | tf_op jit(solution)/shard_map/all_to_all | solution.py:74
  22.1 0.1 maximum_select_fusion.1
  22.2 1.2 fusion.50
  23.4 1.2 pad_maximum_fusion.7
  24.6 1.9 collective-permute-start.2
  26.5 1.9 collective-permute-start.1
  28.5 3.9 %collective-permute-start = (bf16[512,512]{1,0:T(8,128)(2,1)}, bf16[512,512]{1,0:T(8,128)(2,1)}, u32[]{:S(2)}, u32[]{:S(2)}) collective-permute-start(bf16[512,512]{1,0:T(8,128)(2,1)} %get-tuple-element.27), channel_id=1, source_target_pairs={{0,4},{4,8},{8,12},{12,0},{1,5},{5,9},{9,13},{13,1},{2,6},{6,10},{... | collective-permute-start | bytes 1572872 | tf_op jit(solution)/shard_map/ppermute | solution.py:46
  32.4 2.1 %convolution_bitcast_fusion.3 = f32[256,512]{1,0:T(8,128)} fusion(bf16[256,512]{1,0:T(8,128)(2,1)S(1)} %copy-done.1, bf16[512,8192]{1,0:T(8,128)(2,1)} %param.8, s32[]{:T(128)S(6)} %select_n.89), kind=kOutput, calls=%fused_computation.12 | convolution fusion | flops 134217728 | bytes 1310724 | tf_op jit(solution)/shard_map/dot_general | solution.py:68
  34.6 6.9 %collective-permute-done.2 = bf16[512,512]{1,0:T(8,128)(2,1)S(1)} collective-permute-done((bf16[512,512]{1,0:T(8,128)(2,1)}, bf16[512,512]{1,0:T(8,128)(2,1)S(1)}, u32[]{:S(2)}, u32[]{:S(2)}) %collective-permute-start.2) | collective-permute-done | bytes 524320 | tf_op jit(solution)/shard_map/ppermute | solution.py:46
  41.5 0.8 copy-done.5
  42.3 2.8 %collective-permute-done.1 = bf16[512,512]{1,0:T(8,128)(2,1)} collective-permute-done((bf16[512,512]{1,0:T(8,128)(2,1)}, bf16[512,512]{1,0:T(8,128)(2,1)}, u32[]{:S(2)}, u32[]{:S(2)}) %collective-permute-start.1) | collective-permute-done | bytes 524320 | tf_op jit(solution)/shard_map/ppermute | solution.py:46
  45.1 1.0 slice.108
  46.0 9.4 %collective-permute-done = bf16[512,512]{1,0:T(8,128)(2,1)} collective-permute-done((bf16[512,512]{1,0:T(8,128)(2,1)}, bf16[512,512]{1,0:T(8,128)(2,1)}, u32[]{:S(2)}, u32[]{:S(2)}) %collective-permute-start) | collective-permute-done | bytes 524320 | tf_op jit(solution)/shard_map/ppermute | solution.py:46
  55.5 1.0 slice.107
  56.4 0.9 pad_maximum_fusion.1
  57.4 1.9 collective-permute-start.3
  59.4 1.0 fusion.53
  60.4 1.0 fusion.52
  61.4 1.0 fusion.51
  62.5 2.4 %fusion.31 = f32[256,512]{1,0:T(8,128)} fusion(bf16[768,512]{1,0:T(8,128)(2,1)} %collective-permute-done.3, bf16[256,256]{1,0:T(8,128)(2,1)S(1)} %get-tuple-element.26, bf16[256,256]{1,0:T(8,128)(2,1)S(1)} %get-tuple-element.24, bf16[256,256]{1,0:T(8,128)(2,1)S(1)} %get-tuple-element.22), kind=kOutput, calls=%fused_computation.58 | convolution fusion | flops 202506240 | bytes 1703936 | tf_op jit(solution)/shard_map/dot_general | solution.py:62
  64.9 0.7 fusion.5
  65.7 0.7 broadcast_in_dim.20
  66.4 3.4 %all-to-all-start.1 = ((f32[4,64,256]{2,1,0:T(8,128)}), f32[4,64,256]{2,1,0:T(8,128)S(1)}, u32[]{:S(2)}, u32[]{:S(2)}) async-start(f32[4,64,256]{2,1,0:T(8,128)} %broadcast_in_dim.20), calls=%async_computation.1 | async-start | bytes 524288 | tf_op jit(solution)/shard_map/all_to_all | solution.py:41
  69.8 2.3 %fusion.4 = bf16[256,512]{1,0:T(8,128)(2,1)} fusion(f32[256,512]{1,0:T(8,128)} %convolution_bitcast_fusion.3, f32[256,512]{1,0:T(8,128)} %fusion.31, bf16[256,256]{1,0:T(8,128)(2,1)S(1)} %get-tuple-element.25, bf16[256,256]{1,0:T(8,128)(2,1)S(1)} %get-tuple-element.23, bf16[256,256]{1,0:T(8,128)(2,1)S(1)} %get-tuple-element.21, ...), kind=kOutput, calls=%fused_computation.15 | convolution fusion | flops 205258752 | bytes 2490368 | tf_op jit(solution)/shard_map/dot_general | solution.py:62
  72.1 5.3 %all-to-all-done.1 = f32[4,64,256]{2,1,0:T(8,128)S(1)} async-done(((f32[4,64,256]{2,1,0:T(8,128)}), f32[4,64,256]{2,1,0:T(8,128)S(1)}, u32[]{:S(2)}, u32[]{:S(2)}) %all-to-all-start.1) | async-done | bytes 262176 | tf_op jit(solution)/shard_map/all_to_all | solution.py:41
  77.4 0.0 copy-start.15
  77.4 0.6 copy-done.13
  78.0 0.0 copy-done.15
  78.0 1.0 fusion.27
  79.0 1.9 fusion.49
  80.9 0.1 pad_maximum_fusion.4
  81.0 3.1 %collective-permute-start.7 = (bf16[256,1536]{1,0:T(8,128)(2,1)S(1)}, bf16[256,1536]{1,0:T(8,128)(2,1)S(1)}, u32[]{:S(2)}, u32[]{:S(2)}) collective-permute-start(bf16[256,1536]{1,0:T(8,128)(2,1)S(1)} %pad_maximum_fusion.4), channel_id=1, source_target_pairs={{0,12},{4,0},{8,4},{12,8},{1,13},{5,1},{9,5},{13,9},{2,14},{6,2},{... | collective-permute-start | bytes 2359304 | tf_op jit(solution)/shard_map/ppermute | solution.py:46
  84.0 0.1 pad_maximum_fusion.3
  84.1 3.4 %collective-permute-start.6 = (bf16[256,1536]{1,0:T(8,128)(2,1)S(1)}, bf16[256,1536]{1,0:T(8,128)(2,1)S(1)}, u32[]{:S(2)}, u32[]{:S(2)}) collective-permute-start(bf16[256,1536]{1,0:T(8,128)(2,1)S(1)} %pad_maximum_fusion.3), channel_id=1, source_target_pairs={{0,8},{4,12},{8,0},{12,4},{1,9},{5,13},{9,1},{13,5},{2,10},{6,14},... | collective-permute-start | bytes 2359304 | tf_op jit(solution)/shard_map/ppermute | solution.py:46
  87.5 0.1 pad_maximum_fusion.2
  87.5 1.9 collective-permute-start.5
  89.5 15.4 %collective-permute-start.4 = (bf16[320,512]{1,0:T(8,128)(2,1)S(1)}, bf16[320,512]{1,0:T(8,128)(2,1)S(1)}, u32[]{:S(2)}, u32[]{:S(2)}) collective-permute-start(bf16[320,512]{1,0:T(8,128)(2,1)S(1)} %fusion.27), channel_id=1, source_target_pairs={{0,2},{1,3},{2,0},{3,1},{4,6},{5,7},{6,4},{7,5},{8,10},{9,11},{10,... | collective-permute-start | bytes 983048 | tf_op jit(solution)/shard_map/ppermute | solution.py:46
  104.8 7.3 %collective-permute-done.4 = bf16[320,512]{1,0:T(8,128)(2,1)S(1)} collective-permute-done((bf16[320,512]{1,0:T(8,128)(2,1)S(1)}, bf16[320,512]{1,0:T(8,128)(2,1)S(1)}, u32[]{:S(2)}, u32[]{:S(2)}) %collective-permute-start.4) | collective-permute-done | bytes 327712 | tf_op jit(solution)/shard_map/ppermute | solution.py:46
  112.2 0.6 slice.113
  114.2 9.0 %collective-permute-done.5 = bf16[256,1536]{1,0:T(8,128)(2,1)S(1)} collective-permute-done((bf16[256,1536]{1,0:T(8,128)(2,1)S(1)}, bf16[256,1536]{1,0:T(8,128)(2,1)S(1)}, u32[]{:S(2)}, u32[]{:S(2)}) %collective-permute-start.5) | collective-permute-done | bytes 786464 | tf_op jit(solution)/shard_map/ppermute | solution.py:46
  123.2 0.4 maximum_select_fusion
  123.6 1.9 collective-permute-start.8
  125.6 4.6 %collective-permute-done.8 = bf16[768,1536]{1,0:T(8,128)(2,1)} collective-permute-done((bf16[768,1536]{1,0:T(8,128)(2,1)S(1)}, bf16[768,1536]{1,0:T(8,128)(2,1)}, u32[]{:S(2)}, u32[]{:S(2)}) %collective-permute-start.8) | collective-permute-done | bytes 2359328 | tf_op jit(solution)/shard_map/ppermute | solution.py:46
  130.2 2.7 %fusion.30 = f32[256,1536]{1,0:T(8,128)S(1)} fusion(bf16[768,1536]{1,0:T(8,128)(2,1)} %collective-permute-done.8, bf16[256,256]{1,0:T(8,128)(2,1)} %copy-done.6, bf16[256,256]{1,0:T(8,128)(2,1)} %copy-done.9, bf16[256,256]{1,0:T(8,128)(2,1)} %copy-done.10), kind=kOutput, calls=%fused_computation.57 | convolution fusion | flops 605159424 | bytes 4325376 | tf_op jit(solution)/shard_map/dot_general | solution.py:62
  132.9 0.8 convolution_add_fusion
  133.7 0.0 copy-start.16
  133.7 1.8 fusion.10
  135.6 1.4 fusion.9
  137.1 16.2 %collective-permute-start.10 = (bf16[320,512]{1,0:T(8,128)(2,1)S(1)}, bf16[320,512]{1,0:T(8,128)(2,1)}, u32[]{:S(2)}, u32[]{:S(2)}) collective-permute-start(bf16[320,512]{1,0:T(8,128)(2,1)S(1)} %get-tuple-element.33), channel_id=1, source_target_pairs={{0,3},{1,0},{2,1},{3,2},{4,7},{5,4},{6,5},{7,6},{8,11},{9,8},{10,9... | collective-permute-start | bytes 983048 | tf_op jit(solution)/shard_map/ppermute | solution.py:46
  153.3 1.9 collective-permute-start.9
  155.3 0.6 copy.24
  155.9 0.1 convert_element_type.52
  156.0 25.7 %collective-permute-done.10 = bf16[320,512]{1,0:T(8,128)(2,1)} collective-permute-done((bf16[320,512]{1,0:T(8,128)(2,1)S(1)}, bf16[320,512]{1,0:T(8,128)(2,1)}, u32[]{:S(2)}, u32[]{:S(2)}) %collective-permute-start.10) | collective-permute-done | bytes 327712 | tf_op jit(solution)/shard_map/ppermute | solution.py:46
  181.7 1.0 convert_element_type.56
  182.7 7.1 %collective-permute-done.9 = bf16[320,512]{1,0:T(8,128)(2,1)} collective-permute-done((bf16[320,512]{1,0:T(8,128)(2,1)S(1)}, bf16[320,512]{1,0:T(8,128)(2,1)}, u32[]{:S(2)}, u32[]{:S(2)}) %collective-permute-start.9) | collective-permute-done | bytes 327712 | tf_op jit(solution)/shard_map/ppermute | solution.py:46
  189.8 1.0 convert_element_type.54
  190.9 0.3 fusion.3
  191.3 2.3 %fusion.8 = bf16[256,512]{1,0:T(8,128)(2,1)} fusion(f32[256,512]{1,0:T(8,128)S(1)} %fusion.3, f32[320,512]{1,0:T(8,128)S(1)} %convert_element_type.56, f32[320,512]{1,0:T(8,128)S(1)} %convert_element_type.54, f32[320,512]{1,0:T(8,128)S(1)} %convert_element_type.52, f32[256,1536]{1,0:T(8,128)} %copy-done.2, bf16[256,512]{1,0:T(8,128)(2,1)S(1)} %copy-done.1, ...), kind=kOutput, calls=%fused_computation.32 | convolution fusion | flops 135004160 | bytes 3670020 | tf_op jit(solution)/shard_map/dot_general | solution.py:68
  (42 shorter events, 0.2 us)
Async XLA Ops:
  0.0 1.9 copy-start
  5.0 17.1 %copy-start.1 = (bf16[256,512]{1,0:T(8,128)(2,1)S(1)}, bf16[256,512]{1,0:T(8,128)(2,1)}, u32[]{:S(2)}) copy-start(bf16[256,512]{1,0:T(8,128)(2,1)} %param.7) | copy-start | bytes 786436
  5.0 59.9 %all-to-all-start = ((bf16[64,16,512]{2,1,0:T(8,128)(2,1)}), bf16[64,16,512]{2,1,0:T(8,128)(2,1)S(1)}, u32[]{:S(2)}, u32[]{:S(2)}) async-start(bf16[64,16,512]{2,1,0:T(8,128)(2,1)} %pad_maximum_fusion), calls=%async_computation | async-start | bytes 2097152 | tf_op jit(solution)/shard_map/all_to_all | solution.py:74
  24.6 16.9 %collective-permute-start.2 = (bf16[512,512]{1,0:T(8,128)(2,1)}, bf16[512,512]{1,0:T(8,128)(2,1)S(1)}, u32[]{:S(2)}, u32[]{:S(2)}) collective-permute-start(bf16[512,512]{1,0:T(8,128)(2,1)} %get-tuple-element.29), channel_id=1, source_target_pairs={{0,12},{4,0},{8,4},{12,8},{1,13},{5,1},{9,5},{13,9},{2,14},{6,2},{... | collective-permute-start | bytes 1572872 | tf_op jit(solution)/shard_map/ppermute | solution.py:46
  26.5 18.5 %collective-permute-start.1 = (bf16[512,512]{1,0:T(8,128)(2,1)}, bf16[512,512]{1,0:T(8,128)(2,1)}, u32[]{:S(2)}, u32[]{:S(2)}) collective-permute-start(bf16[512,512]{1,0:T(8,128)(2,1)} %get-tuple-element.28), channel_id=1, source_target_pairs={{0,8},{4,12},{8,0},{12,4},{1,9},{5,13},{9,1},{13,5},{2,10},{6,14},... | collective-permute-start | bytes 1572872 | tf_op jit(solution)/shard_map/ppermute | solution.py:46
  28.5 27.0 %collective-permute-start = (bf16[512,512]{1,0:T(8,128)(2,1)}, bf16[512,512]{1,0:T(8,128)(2,1)}, u32[]{:S(2)}, u32[]{:S(2)}) collective-permute-start(bf16[512,512]{1,0:T(8,128)(2,1)} %get-tuple-element.27), channel_id=1, source_target_pairs={{0,4},{4,8},{8,12},{12,0},{1,5},{5,9},{9,13},{13,1},{2,6},{6,10},{... | collective-permute-start | bytes 1572872 | tf_op jit(solution)/shard_map/ppermute | solution.py:46
  34.6 24.8 %copy-start.17 = (s32[256]{0:T(256)S(1)}, s32[256]{0:T(256)}, u32[]{:S(2)}) copy-start(s32[256]{0:T(256)} %param.13) | copy-start | bytes 3076
  41.5 0.8 copy-start.5
  57.4 5.1 %collective-permute-start.3 = (bf16[768,512]{1,0:T(8,128)(2,1)}, bf16[768,512]{1,0:T(8,128)(2,1)}, u32[]{:S(2)}, u32[]{:S(2)}) collective-permute-start(bf16[768,512]{1,0:T(8,128)(2,1)} %pad_maximum_fusion.1), channel_id=1, source_target_pairs={{0,16},{16,0},{1,17},{17,1},{2,18},{18,2},{3,19},{19,3},{4,20},{20... | collective-permute-start | bytes 2359304 | tf_op jit(solution)/shard_map/ppermute | solution.py:46
  60.4 6.0 %copy-start.6 = (bf16[256,256]{1,0:T(8,128)(2,1)}, bf16[256,256]{1,0:T(8,128)(2,1)S(1)}, u32[]{:S(2)}) copy-start(bf16[256,256]{1,0:T(8,128)(2,1)S(1)} %get-tuple-element.26) | copy-start | bytes 393220
  61.4 4.2 %copy-start.9 = (bf16[256,256]{1,0:T(8,128)(2,1)}, bf16[256,256]{1,0:T(8,128)(2,1)S(1)}, u32[]{:S(2)}) copy-start(bf16[256,256]{1,0:T(8,128)(2,1)S(1)} %get-tuple-element.24) | copy-start | bytes 393220
  62.5 3.2 %copy-start.10 = (bf16[256,256]{1,0:T(8,128)(2,1)}, bf16[256,256]{1,0:T(8,128)(2,1)S(1)}, u32[]{:S(2)}) copy-start(bf16[256,256]{1,0:T(8,128)(2,1)S(1)} %get-tuple-element.22) | copy-start | bytes 393220
  62.5 7.3 %copy-start.7 = (bf16[256,256]{1,0:T(8,128)(2,1)}, bf16[256,256]{1,0:T(8,128)(2,1)S(1)}, u32[]{:S(2)}) copy-start(bf16[256,256]{1,0:T(8,128)(2,1)S(1)} %get-tuple-element.21) | copy-start | bytes 393220
  64.9 7.2 %copy-start.3 = (bf16[64,16,512]{2,1,0:T(8,128)(2,1)}, bf16[64,16,512]{2,1,0:T(8,128)(2,1)S(1)}, u32[]{:S(2)}) copy-start(bf16[64,16,512]{2,1,0:T(8,128)(2,1)S(1)} %all-to-all-done) | copy-start | bytes 3145732
  66.4 11.0 %all-to-all-start.1 = ((f32[4,64,256]{2,1,0:T(8,128)}), f32[4,64,256]{2,1,0:T(8,128)S(1)}, u32[]{:S(2)}, u32[]{:S(2)}) async-start(f32[4,64,256]{2,1,0:T(8,128)} %broadcast_in_dim.20), calls=%async_computation.1 | async-start | bytes 524288 | tf_op jit(solution)/shard_map/all_to_all | solution.py:41
  77.4 0.6 copy-start.13
  77.4 0.6 copy-start.15
  81.0 33.2 %collective-permute-start.7 = (bf16[256,1536]{1,0:T(8,128)(2,1)S(1)}, bf16[256,1536]{1,0:T(8,128)(2,1)S(1)}, u32[]{:S(2)}, u32[]{:S(2)}) collective-permute-start(bf16[256,1536]{1,0:T(8,128)(2,1)S(1)} %pad_maximum_fusion.4), channel_id=1, source_target_pairs={{0,12},{4,0},{8,4},{12,8},{1,13},{5,1},{9,5},{13,9},{2,14},{6,2},{... | collective-permute-start | bytes 2359304 | tf_op jit(solution)/shard_map/ppermute | solution.py:46
  84.1 30.1 %collective-permute-start.6 = (bf16[256,1536]{1,0:T(8,128)(2,1)S(1)}, bf16[256,1536]{1,0:T(8,128)(2,1)S(1)}, u32[]{:S(2)}, u32[]{:S(2)}) collective-permute-start(bf16[256,1536]{1,0:T(8,128)(2,1)S(1)} %pad_maximum_fusion.3), channel_id=1, source_target_pairs={{0,8},{4,12},{8,0},{12,4},{1,9},{5,13},{9,1},{13,5},{2,10},{6,14},... | collective-permute-start | bytes 2359304 | tf_op jit(solution)/shard_map/ppermute | solution.py:46
  87.5 35.7 %collective-permute-start.5 = (bf16[256,1536]{1,0:T(8,128)(2,1)S(1)}, bf16[256,1536]{1,0:T(8,128)(2,1)S(1)}, u32[]{:S(2)}, u32[]{:S(2)}) collective-permute-start(bf16[256,1536]{1,0:T(8,128)(2,1)S(1)} %pad_maximum_fusion.2), channel_id=1, source_target_pairs={{0,4},{4,8},{8,12},{12,0},{1,5},{5,9},{9,13},{13,1},{2,6},{6,10},{... | collective-permute-start | bytes 2359304 | tf_op jit(solution)/shard_map/ppermute | solution.py:46
  89.5 22.7 %collective-permute-start.4 = (bf16[320,512]{1,0:T(8,128)(2,1)S(1)}, bf16[320,512]{1,0:T(8,128)(2,1)S(1)}, u32[]{:S(2)}, u32[]{:S(2)}) collective-permute-start(bf16[320,512]{1,0:T(8,128)(2,1)S(1)} %fusion.27), channel_id=1, source_target_pairs={{0,2},{1,3},{2,0},{3,1},{4,6},{5,7},{6,4},{7,5},{8,10},{9,11},{10,... | collective-permute-start | bytes 983048 | tf_op jit(solution)/shard_map/ppermute | solution.py:46
  112.2 11.1 %copy-start.11 = (bf16[320,512]{1,0:T(8,128)(2,1)}, bf16[320,512]{1,0:T(8,128)(2,1)S(1)}, u32[]{:S(2)}) copy-start(bf16[320,512]{1,0:T(8,128)(2,1)S(1)} %collective-permute-done.4) | copy-start | bytes 983044
  123.6 6.6 %collective-permute-start.8 = (bf16[768,1536]{1,0:T(8,128)(2,1)S(1)}, bf16[768,1536]{1,0:T(8,128)(2,1)}, u32[]{:S(2)}, u32[]{:S(2)}) collective-permute-start(bf16[768,1536]{1,0:T(8,128)(2,1)S(1)} %maximum_select_fusion), channel_id=1, source_target_pairs={{0,16},{16,0},{1,17},{17,1},{2,18},{18,2},{3,19},{19,3},{4,20},{20... | collective-permute-start | bytes 7077896 | tf_op jit(solution)/shard_map/ppermute | solution.py:46
  125.6 7.3 %copy-start.8 = (bf16[256,256]{1,0:T(8,128)(2,1)S(1)}, bf16[256,256]{1,0:T(8,128)(2,1)}, u32[]{:S(2)}) copy-start(bf16[256,256]{1,0:T(8,128)(2,1)} %copy-done.7) | copy-start | bytes 393220
  133.7 3.3 %copy-start.2 = (f32[256,1536]{1,0:T(8,128)}, f32[256,1536]{1,0:T(8,128)S(1)}, u32[]{:S(2)}) copy-start(f32[256,1536]{1,0:T(8,128)S(1)} %convolution_add_fusion) | copy-start | bytes 4718596
  133.7 3.3 %copy-start.14 = (bf16[64,256]{1,0:T(8,128)(2,1)S(1)}, bf16[64,256]{1,0:T(8,128)(2,1)}, u32[]{:S(2)}) copy-start(bf16[64,256]{1,0:T(8,128)(2,1)} %copy-done.13) | copy-start | bytes 98308
  133.7 3.3 %copy-start.16 = (bf16[64,256]{1,0:T(8,128)(2,1)S(1)}, bf16[64,256]{1,0:T(8,128)(2,1)}, u32[]{:S(2)}) copy-start(bf16[64,256]{1,0:T(8,128)(2,1)} %copy-done.15) | copy-start | bytes 98308
  135.6 19.7 %copy-start.4 = (bf16[64,16,512]{2,1,0:T(8,128)(2,1)S(1)}, bf16[64,16,512]{2,1,0:T(8,128)(2,1)}, u32[]{:S(2)}) copy-start(bf16[64,16,512]{2,1,0:T(8,128)(2,1)} %copy-done.3) | copy-start | bytes 3145732
  137.0 18.8 %copy-start.12 = (bf16[320,512]{1,0:T(8,128)(2,1)S(1)}, bf16[320,512]{1,0:T(8,128)(2,1)}, u32[]{:S(2)}) copy-start(bf16[320,512]{1,0:T(8,128)(2,1)} %copy-done.11) | copy-start | bytes 983044
  137.1 44.6 %collective-permute-start.10 = (bf16[320,512]{1,0:T(8,128)(2,1)S(1)}, bf16[320,512]{1,0:T(8,128)(2,1)}, u32[]{:S(2)}, u32[]{:S(2)}) collective-permute-start(bf16[320,512]{1,0:T(8,128)(2,1)S(1)} %get-tuple-element.33), channel_id=1, source_target_pairs={{0,3},{1,0},{2,1},{3,2},{4,7},{5,4},{6,5},{7,6},{8,11},{9,8},{10,9... | collective-permute-start | bytes 983048 | tf_op jit(solution)/shard_map/ppermute | solution.py:46
  153.3 36.5 %collective-permute-start.9 = (bf16[320,512]{1,0:T(8,128)(2,1)S(1)}, bf16[320,512]{1,0:T(8,128)(2,1)}, u32[]{:S(2)}, u32[]{:S(2)}) collective-permute-start(bf16[320,512]{1,0:T(8,128)(2,1)S(1)} %get-tuple-element.32), channel_id=1, source_target_pairs={{0,1},{1,2},{2,3},{3,0},{4,5},{5,6},{6,7},{7,4},{8,9},{9,10},{10,1... | collective-permute-start | bytes 983048 | tf_op jit(solution)/shard_map/ppermute | solution.py:46

commit v7 on v3

--- a/solution.py
+++ b/solution.py
@@ -81,26 +81,26 @@
     lhs_mine = jnp.concatenate([block[:rows, :half] for block in got], axis=1)
     lhs_other = jnp.concatenate([block[:rows, half:] for block in got], axis=1)
     far_mine = jnp.concatenate([block[rows:] for block in got], axis=0)
-    (far,) = product(far_mine, shifted(far_mine, "c", 1), (2,), weight)
-    far = far.astype(bf16)
-    far_sum = shifted(far, "zh", 2)
-
     selector = slot[None, :] == jnp.arange(WORKING_SLOTS, dtype=jnp.int32)[:, None]
     all_ranks = lax.dot_general(down, x_block, (((1,), (1,)), ((), ())), preferred_element_type=f32)
     ranks = jnp.sum(all_ranks.reshape(WORKING_SLOTS, ADAPTER_RANK, rows) * selector.astype(f32)[:, None, :], axis=0)
-    ranks = following(sum_over(ranks, "x"), far_sum)
+    ranks = sum_over(ranks, "x")
     rounded = sum_over(ranks, "zh").astype(bf16)
-    expanded = (rounded[None] * selector.astype(bf16)[:, None, :]).reshape(WORKING_SLOTS * ADAPTER_RANK, rows)
+
+    (far,) = product(far_mine, shifted(far_mine, "c", 1), (2,), weight)
+    far = following(far.astype(bf16), ranks)
+    far_sum = shifted(far, "zh", 2)
 
     near_weight = after(weight, far)
     near = [
         shifted(jnp.concatenate([weight_of(near_weight, by, z_by) for z_by in (1, 3, 0)], axis=1), "x", by)
         for by in range(1, xs)
     ]
-    near_mine = following(after(jnp.concatenate(near, axis=0), far_sum), rounded)
+    near_mine = following(following(jnp.concatenate(near, axis=0), far_sum), rounded)
     up_part, down_part, total = product(near_mine, shifted(near_mine, "c", 1), (1, 3, 0), weight)
     up_sum = shifted(up_part.astype(bf16), "zh", 1)
     down_sum = shifted(down_part.astype(bf16), "zh", 3)
+    expanded = (rounded[None] * selector.astype(bf16)[:, None, :]).reshape(WORKING_SLOTS * ADAPTER_RANK, rows)
     term = lax.dot_general(expanded, up, (((0,), (0,)), ((), ())), preferred_element_type=f32)
     total = total + far_sum.astype(f32) + ADAPTER_SCALE * term
     return (total + up_sum.astype(f32) + down_sum.astype(f32)).astype(bf16)

time: 210 us -> 202 us (0.962)
  the two profiles are of different devices: /device:TPU:3 before, /device:TPU:56 now
where the time goes in v7:
time: 202 us; the launch traced here: 200 us
  starting transfers between devices  77.7 us (38%)
  waiting for transfers between devices  76.5 us (38%)
  matrix products  19.5 us (10%)
  local copies, waits for them, and re-layouts  13.2 us (7%)
  other arithmetic  8.5 us (4%)
  between operations  4.43 us (2%)
    ppermute x11, waiting for transfers between devices, shifted(): lax.ppermute(value, axis, [(i, (i + by) % size) for i in range(size)])  71.6 us
    ppermute x11, starting transfers between devices, shifted(): lax.ppermute(value, axis, [(i, (i + by) % size) for i in range(size)])  44.1 us
    all_to_all x1, starting transfers between devices, body(): lax.all_to_all(outgoing, REPLICA, split_axis=0, concat_axis=0, tiled=True)  17 us
    all_to_all x2, starting transfers between devices, sum_over(): lax.all_to_all(spread, axis, split_axis=0, concat_axis=0, tiled=True)  16.6 us
    dot_general x4, matrix products, product(): own = jnp.dot(x_block, own, preferred_element_type=f32)  9.1 us
    dot_general x2, matrix products, product(): jnp.dot(lhs_other, other, preferred_element_type=f32)  4.98 us
    all_to_all x2, waiting for transfers between devices, sum_over(): lax.all_to_all(spread, axis, split_axis=0, concat_axis=0, tiled=True)  4.93 us
  transfers between devices with their start and end apart: 14, of which 7 were waited for; matrix products, arithmetic and copies ran while one was open for 11% of the time, Pallas kernels for 0%

profile of v7, /device:TPU:56, one launch (start us, length us, event | category | flops | bytes accessed | tf_op | source)
XLA Modules:
  0.0 199.8 jit_solution(2102662793095536160)
XLA Ops:
  0.0 0.8 copy.27
  0.8 0.1 eq.42
  0.9 0.9 select_reduce_fusion
  1.9 0.5 fusion.3
  2.4 1.5 fusion.2
  3.9 1.2 pad_maximum_fusion
  5.1 17.0 %all-to-all-start = ((bf16[64,16,512]{2,1,0:T(8,128)(2,1)}), bf16[64,16,512]{2,1,0:T(8,128)(2,1)S(1)}, u32[]{:S(2)}, u32[]{:S(2)}) async-start(bf16[64,16,512]{2,1,0:T(8,128)(2,1)} %pad_maximum_fusion), calls=%async_computation | async-start | bytes 2097152 | tf_op jit(solution)/shard_map/all_to_all | solution.py:74
  22.1 0.1 maximum_select_fusion.1
  22.2 1.2 fusion.47
  23.4 0.0 copy-start.14
  23.4 1.3 pad_maximum_fusion.7
  24.7 1.9 collective-permute-start
  26.6 2.4 %collective-permute-start.1 = (bf16[512,512]{1,0:T(8,128)(2,1)}, bf16[512,512]{1,0:T(8,128)(2,1)}, u32[]{:S(2)}, u32[]{:S(2)}) collective-permute-start(bf16[512,512]{1,0:T(8,128)(2,1)} %get-tuple-element.28), channel_id=1, source_target_pairs={{0,8},{4,12},{8,0},{12,4},{1,9},{5,13},{9,1},{13,5},{2,10},{6,14},... | collective-permute-start | bytes 1572872 | tf_op jit(solution)/shard_map/ppermute | solution.py:46
  29.0 4.7 %collective-permute-start.2 = (bf16[512,512]{1,0:T(8,128)(2,1)}, bf16[512,512]{1,0:T(8,128)(2,1)}, u32[]{:S(2)}, u32[]{:S(2)}) collective-permute-start(bf16[512,512]{1,0:T(8,128)(2,1)} %get-tuple-element.29), channel_id=1, source_target_pairs={{0,12},{4,0},{8,4},{12,8},{1,13},{5,1},{9,5},{13,9},{2,14},{6,2},{... | collective-permute-start | bytes 1572872 | tf_op jit(solution)/shard_map/ppermute | solution.py:46
  33.8 2.2 %convolution_bitcast_fusion.3 = f32[256,512]{1,0:T(8,128)} fusion(bf16[256,512]{1,0:T(8,128)(2,1)S(1)} %copy-done.1, bf16[512,8192]{1,0:T(8,128)(2,1)} %param.8, s32[]{:T(128)S(6)} %select_n.105), kind=kOutput, calls=%fused_computation.13 | convolution fusion | flops 134217728 | bytes 1310724 | tf_op jit(solution)/shard_map/dot_general | solution.py:68
  35.9 17.3 %collective-permute-done = bf16[512,512]{1,0:T(8,128)(2,1)S(1)} collective-permute-done((bf16[512,512]{1,0:T(8,128)(2,1)}, bf16[512,512]{1,0:T(8,128)(2,1)S(1)}, u32[]{:S(2)}, u32[]{:S(2)}) %collective-permute-start) | collective-permute-done | bytes 524320 | tf_op jit(solution)/shard_map/ppermute | solution.py:46
  53.2 0.8 copy-done.5
  54.0 0.0 collective-permute-done.1
  54.0 1.0 slice.82
  55.0 0.8 collective-permute-done.2
  55.8 1.0 slice.83
  56.8 0.9 pad_maximum_fusion.1
  57.7 1.9 collective-permute-start.3
  59.7 1.0 fusion.49
  60.7 1.7 fusion.50
  62.4 0.0 all-to-all-done
  62.4 0.7 fusion.6
  63.1 0.7 broadcast_in_dim.42
  63.9 3.9 %all-to-all-start.1 = ((f32[4,64,256]{2,1,0:T(8,128)}), f32[4,64,256]{2,1,0:T(8,128)S(1)}, u32[]{:S(2)}, u32[]{:S(2)}) async-start(f32[4,64,256]{2,1,0:T(8,128)} %broadcast_in_dim.42), calls=%async_computation.1 | async-start | bytes 524288 | tf_op jit(solution)/shard_map/all_to_all | solution.py:41
  67.8 0.0 collective-permute-done.3
  67.8 2.4 %fusion.33 = f32[256,512]{1,0:T(8,128)} fusion(bf16[768,512]{1,0:T(8,128)(2,1)} %collective-permute-done.3, bf16[256,256]{1,0:T(8,128)(2,1)} %get-tuple-element.26, bf16[256,256]{1,0:T(8,128)(2,1)S(1)} %get-tuple-element.24, bf16[256,256]{1,0:T(8,128)(2,1)S(1)} %get-tuple-element.22), kind=kOutput, calls=%fused_computation.56 | convolution fusion | flops 202506240 | bytes 1703936 | tf_op jit(solution)/shard_map/dot_general | solution.py:62
  70.2 4.9 %all-to-all-done.1 = f32[4,64,256]{2,1,0:T(8,128)S(1)} async-done(((f32[4,64,256]{2,1,0:T(8,128)}), f32[4,64,256]{2,1,0:T(8,128)S(1)}, u32[]{:S(2)}, u32[]{:S(2)}) %all-to-all-start.1) | async-done | bytes 262176 | tf_op jit(solution)/shard_map/all_to_all | solution.py:41
  75.1 0.5 slice.80
  76.9 0.7 broadcast_in_dim.43
  77.6 12.7 %all-to-all-start.2 = ((f32[4,64,256]{2,1,0:T(8,128)}), f32[4,64,256]{2,1,0:T(8,128)S(1)}, u32[]{:S(2)}, u32[]{:S(2)}) async-start(f32[4,64,256]{2,1,0:T(8,128)} %broadcast_in_dim.43), calls=%async_computation.2 | async-start | bytes 524288 | tf_op jit(solution)/shard_map/all_to_all | solution.py:41
  90.3 1.6 fusion.7
  91.9 1.9 fusion.46
  93.7 1.0 pad_maximum_fusion.3
  94.7 2.5 %collective-permute-start.6 = (bf16[256,1536]{1,0:T(8,128)(2,1)}, bf16[256,1536]{1,0:T(8,128)(2,1)}, u32[]{:S(2)}, u32[]{:S(2)}) collective-permute-start(bf16[256,1536]{1,0:T(8,128)(2,1)} %pad_maximum_fusion.3), channel_id=1, source_target_pairs={{0,8},{4,12},{8,0},{12,4},{1,9},{5,13},{9,1},{13,5},{2,10},{6,14},... | collective-permute-start | bytes 2359304 | tf_op jit(solution)/shard_map/ppermute | solution.py:46
  97.2 0.9 pad_maximum_fusion.4
  98.2 4.5 %collective-permute-start.7 = (bf16[256,1536]{1,0:T(8,128)(2,1)}, bf16[256,1536]{1,0:T(8,128)(2,1)}, u32[]{:S(2)}, u32[]{:S(2)}) collective-permute-start(bf16[256,1536]{1,0:T(8,128)(2,1)} %pad_maximum_fusion.4), channel_id=1, source_target_pairs={{0,12},{4,0},{8,4},{12,8},{1,13},{5,1},{9,5},{13,9},{2,14},{6,2},{... | collective-permute-start | bytes 2359304 | tf_op jit(solution)/shard_map/ppermute | solution.py:46
  102.7 0.1 pad_maximum_fusion.2
  102.8 1.9 collective-permute-start.5
  104.7 12.6 %collective-permute-start.4 = (bf16[256,512]{1,0:T(8,128)(2,1)S(1)}, bf16[256,512]{1,0:T(8,128)(2,1)S(1)}, u32[]{:S(2)}, u32[]{:S(2)}) collective-permute-start(bf16[256,512]{1,0:T(8,128)(2,1)S(1)} %fusion.7), channel_id=1, source_target_pairs={{0,2},{1,3},{2,0},{3,1},{4,6},{5,7},{6,4},{7,5},{8,10},{9,11},{10,... | collective-permute-start | bytes 786440 | tf_op jit(solution)/shard_map/ppermute | solution.py:46
  117.3 20.6 %collective-permute-done.4 = bf16[256,512]{1,0:T(8,128)(2,1)S(1)} collective-permute-done((bf16[256,512]{1,0:T(8,128)(2,1)S(1)}, bf16[256,512]{1,0:T(8,128)(2,1)S(1)}, u32[]{:S(2)}, u32[]{:S(2)}) %collective-permute-start.4) | collective-permute-done | bytes 262176 | tf_op jit(solution)/shard_map/ppermute | solution.py:46
  137.9 0.6 slice.87
  139.7 0.0 all-to-all-done.2
  139.8 0.5 slice.79
  141.6 0.0 collective-permute-done.7
  141.6 0.0 collective-permute-done.5
  141.6 2.2 %fusion = bf16[768,1536]{1,0:T(8,128)(2,1)S(1)} fusion(bf16[256,1536]{1,0:T(8,128)(2,1)} %collective-permute-done.7, bf16[256,1536]{1,0:T(8,128)(2,1)} %collective-permute-done.6, bf16[256,1536]{1,0:T(8,128)(2,1)} %collective-permute-done.5, pred[]{:T(512)} %bitcast.9, pred[]{:T(512)} %bitcast.6), kind=kLoop, calls=%fused_computation.2 | loop fusion | flops 9437184 | bytes 4718594 | tf_op jit(solution)/shard_map/jit(_where)/select_n | solution.py:23
  143.8 1.9 collective-permute-start.8
  145.8 4.6 %collective-permute-done.8 = bf16[768,1536]{1,0:T(8,128)(2,1)} collective-permute-done((bf16[768,1536]{1,0:T(8,128)(2,1)S(1)}, bf16[768,1536]{1,0:T(8,128)(2,1)}, u32[]{:S(2)}, u32[]{:S(2)}) %collective-permute-start.8) | collective-permute-done | bytes 2359328 | tf_op jit(solution)/shard_map/ppermute | solution.py:46
  150.4 2.6 %fusion.32 = f32[256,1536]{1,0:T(8,128)S(1)} fusion(bf16[768,1536]{1,0:T(8,128)(2,1)} %collective-permute-done.8, bf16[256,256]{1,0:T(8,128)(2,1)} %get-tuple-element.26, bf16[256,256]{1,0:T(8,128)(2,1)} %copy-done.9, bf16[256,256]{1,0:T(8,128)(2,1)S(1)} %get-tuple-element.22), kind=kOutput, calls=%fused_computation.55 | convolution fusion | flops 605159424 | bytes 4325376 | tf_op jit(solution)/shard_map/dot_general | solution.py:62
  153.0 0.8 convolution_add_fusion
  153.8 2.5 %fusion.8 = bf16[256,512]{1,0:T(8,128)(2,1)} fusion(f32[256,1536]{1,0:T(8,128)S(1)} %convolution_add_fusion, bf16[256,512]{1,0:T(8,128)(2,1)S(1)} %copy-done.1, bf16[512,8192]{1,0:T(8,128)(2,1)} %param.8, s32[]{:T(128)S(6)} %select_n.121), kind=kOutput, calls=%fused_computation.32 | convolution fusion | flops 134479872 | bytes 1572868 | tf_op jit(solution)/shard_map/dot_general | solution.py:68
  156.4 2.0 %fusion.9 = bf16[256,512]{1,0:T(8,128)(2,1)} fusion(f32[256,1536]{1,0:T(8,128)S(1)} %convolution_add_fusion, bf16[256,512]{1,0:T(8,128)(2,1)S(1)} %copy-done.1, bf16[512,8192]{1,0:T(8,128)(2,1)} %param.8, s32[]{:T(128)S(6)} %select_n.120), kind=kOutput, calls=%fused_computation.34 | convolution fusion | flops 134479872 | bytes 1572868 | tf_op jit(solution)/shard_map/dot_general | solution.py:68
  158.4 1.9 collective-permute-start.9
  160.3 7.8 %collective-permute-start.10 = (bf16[256,512]{1,0:T(8,128)(2,1)}, bf16[256,512]{1,0:T(8,128)(2,1)}, u32[]{:S(2)}, u32[]{:S(2)}) collective-permute-start(bf16[256,512]{1,0:T(8,128)(2,1)} %fusion.8), channel_id=1, source_target_pairs={{0,3},{1,0},{2,1},{3,2},{4,7},{5,4},{6,5},{7,6},{8,11},{9,8},{10,9... | collective-permute-start | bytes 786440 | tf_op jit(solution)/shard_map/ppermute | solution.py:46
  168.2 0.6 copy.39
  168.8 0.3 fusion.4
  169.1 6.0 %collective-permute-done.9 = bf16[256,512]{1,0:T(8,128)(2,1)S(1)} collective-permute-done((bf16[256,512]{1,0:T(8,128)(2,1)}, bf16[256,512]{1,0:T(8,128)(2,1)S(1)}, u32[]{:S(2)}, u32[]{:S(2)}) %collective-permute-start.9) | collective-permute-done | bytes 262176 | tf_op jit(solution)/shard_map/ppermute | solution.py:46
  175.1 22.4 %collective-permute-done.10 = bf16[256,512]{1,0:T(8,128)(2,1)} collective-permute-done((bf16[256,512]{1,0:T(8,128)(2,1)}, bf16[256,512]{1,0:T(8,128)(2,1)}, u32[]{:S(2)}, u32[]{:S(2)}) %collective-permute-start.10) | collective-permute-done | bytes 262176 | tf_op jit(solution)/shard_map/ppermute | solution.py:46
  197.5 2.4 %fusion.15 = bf16[256,512]{1,0:T(8,128)(2,1)} fusion(f32[256,512]{1,0:T(8,128)S(1)} %fusion.4, f32[256,1536]{1,0:T(8,128)} %copy-done.2, bf16[256,512]{1,0:T(8,128)(2,1)} %collective-permute-done.10, bf16[256,512]{1,0:T(8,128)(2,1)S(1)} %collective-permute-done.9, bf16[256,512]{1,0:T(8,128)(2,1)S(1)} %copy-done.11, bf16[256,512]{1,0:T(8,128)(2,1)S(1)} %copy-done.1, ...), kind=kOutput, calls=%fused_computation.41 | convolution fusion | flops 135397376 | bytes 2883588 | tf_op jit(solution)/shard_map/dot_general | solution.py:68
  (35 shorter events, 0.2 us)
Async XLA Ops:
  0.0 1.9 copy-start
  5.1 17.1 %copy-start.1 = (bf16[256,512]{1,0:T(8,128)(2,1)S(1)}, bf16[256,512]{1,0:T(8,128)(2,1)}, u32[]{:S(2)}) copy-start(bf16[256,512]{1,0:T(8,128)(2,1)} %param.7) | copy-start | bytes 786436
  5.1 57.3 %all-to-all-start = ((bf16[64,16,512]{2,1,0:T(8,128)(2,1)}), bf16[64,16,512]{2,1,0:T(8,128)(2,1)S(1)}, u32[]{:S(2)}, u32[]{:S(2)}) async-start(bf16[64,16,512]{2,1,0:T(8,128)(2,1)} %pad_maximum_fusion), calls=%async_computation | async-start | bytes 2097152 | tf_op jit(solution)/shard_map/all_to_all | solution.py:74
  23.4 10.3 %copy-start.14 = (s32[256]{0:T(256)S(1)}, s32[256]{0:T(256)}, u32[]{:S(2)}) copy-start(s32[256]{0:T(256)} %param.13) | copy-start | bytes 3076
  24.7 28.5 %collective-permute-start = (bf16[512,512]{1,0:T(8,128)(2,1)}, bf16[512,512]{1,0:T(8,128)(2,1)S(1)}, u32[]{:S(2)}, u32[]{:S(2)}) collective-permute-start(bf16[512,512]{1,0:T(8,128)(2,1)} %get-tuple-element.27), channel_id=1, source_target_pairs={{0,4},{4,8},{8,12},{12,0},{1,5},{5,9},{9,13},{13,1},{2,6},{6,10},{... | collective-permute-start | bytes 1572872 | tf_op jit(solution)/shard_map/ppermute | solution.py:46
  26.6 27.4 %collective-permute-start.1 = (bf16[512,512]{1,0:T(8,128)(2,1)}, bf16[512,512]{1,0:T(8,128)(2,1)}, u32[]{:S(2)}, u32[]{:S(2)}) collective-permute-start(bf16[512,512]{1,0:T(8,128)(2,1)} %get-tuple-element.28), channel_id=1, source_target_pairs={{0,8},{4,12},{8,0},{12,4},{1,9},{5,13},{9,1},{13,5},{2,10},{6,14},... | collective-permute-start | bytes 1572872 | tf_op jit(solution)/shard_map/ppermute | solution.py:46
  29.0 26.9 %collective-permute-start.2 = (bf16[512,512]{1,0:T(8,128)(2,1)}, bf16[512,512]{1,0:T(8,128)(2,1)}, u32[]{:S(2)}, u32[]{:S(2)}) collective-permute-start(bf16[512,512]{1,0:T(8,128)(2,1)} %get-tuple-element.29), channel_id=1, source_target_pairs={{0,12},{4,0},{8,4},{12,8},{1,13},{5,1},{9,5},{13,9},{2,14},{6,2},{... | collective-permute-start | bytes 1572872 | tf_op jit(solution)/shard_map/ppermute | solution.py:46
  53.2 0.8 copy-start.5
  54.0 5.6 %copy-start.6 = (bf16[512,512]{1,0:T(8,128)(2,1)S(1)}, bf16[512,512]{1,0:T(8,128)(2,1)}, u32[]{:S(2)}) copy-start(bf16[512,512]{1,0:T(8,128)(2,1)} %copy-done.5) | copy-start | bytes 1572868
  57.7 10.0 %collective-permute-start.3 = (bf16[768,512]{1,0:T(8,128)(2,1)}, bf16[768,512]{1,0:T(8,128)(2,1)}, u32[]{:S(2)}, u32[]{:S(2)}) collective-permute-start(bf16[768,512]{1,0:T(8,128)(2,1)} %pad_maximum_fusion.1), channel_id=1, source_target_pairs={{0,16},{16,0},{1,17},{17,1},{2,18},{18,2},{3,19},{19,3},{4,20},{20... | collective-permute-start | bytes 2359304 | tf_op jit(solution)/shard_map/ppermute | solution.py:46
  60.7 9.5 %copy-start.9 = (bf16[256,256]{1,0:T(8,128)(2,1)}, bf16[256,256]{1,0:T(8,128)(2,1)S(1)}, u32[]{:S(2)}) copy-start(bf16[256,256]{1,0:T(8,128)(2,1)S(1)} %get-tuple-element.24) | copy-start | bytes 393220
  62.4 27.9 %copy-start.7 = (bf16[256,256]{1,0:T(8,128)(2,1)}, bf16[256,256]{1,0:T(8,128)(2,1)S(1)}, u32[]{:S(2)}) copy-start(bf16[256,256]{1,0:T(8,128)(2,1)S(1)} %get-tuple-element.25) | copy-start | bytes 393220
  62.4 7.8 %copy-start.3 = (bf16[64,16,512]{2,1,0:T(8,128)(2,1)}, bf16[64,16,512]{2,1,0:T(8,128)(2,1)S(1)}, u32[]{:S(2)}) copy-start(bf16[64,16,512]{2,1,0:T(8,128)(2,1)S(1)} %all-to-all-done) | copy-start | bytes 3145732
  63.9 11.2 %all-to-all-start.1 = ((f32[4,64,256]{2,1,0:T(8,128)}), f32[4,64,256]{2,1,0:T(8,128)S(1)}, u32[]{:S(2)}, u32[]{:S(2)}) async-start(f32[4,64,256]{2,1,0:T(8,128)} %broadcast_in_dim.42), calls=%async_computation.1 | async-start | bytes 524288 | tf_op jit(solution)/shard_map/all_to_all | solution.py:41
  77.6 62.1 %all-to-all-start.2 = ((f32[4,64,256]{2,1,0:T(8,128)}), f32[4,64,256]{2,1,0:T(8,128)S(1)}, u32[]{:S(2)}, u32[]{:S(2)}) async-start(f32[4,64,256]{2,1,0:T(8,128)} %broadcast_in_dim.43), calls=%async_computation.2 | async-start | bytes 524288 | tf_op jit(solution)/shard_map/all_to_all | solution.py:41
  94.7 46.9 %collective-permute-start.6 = (bf16[256,1536]{1,0:T(8,128)(2,1)}, bf16[256,1536]{1,0:T(8,128)(2,1)}, u32[]{:S(2)}, u32[]{:S(2)}) collective-permute-start(bf16[256,1536]{1,0:T(8,128)(2,1)} %pad_maximum_fusion.3), channel_id=1, source_target_pairs={{0,8},{4,12},{8,0},{12,4},{1,9},{5,13},{9,1},{13,5},{2,10},{6,14},... | collective-permute-start | bytes 2359304 | tf_op jit(solution)/shard_map/ppermute | solution.py:46
  98.2 43.5 %collective-permute-start.7 = (bf16[256,1536]{1,0:T(8,128)(2,1)}, bf16[256,1536]{1,0:T(8,128)(2,1)}, u32[]{:S(2)}, u32[]{:S(2)}) collective-permute-start(bf16[256,1536]{1,0:T(8,128)(2,1)} %pad_maximum_fusion.4), channel_id=1, source_target_pairs={{0,12},{4,0},{8,4},{12,8},{1,13},{5,1},{9,5},{13,9},{2,14},{6,2},{... | collective-permute-start | bytes 2359304 | tf_op jit(solution)/shard_map/ppermute | solution.py:46
  102.8 38.9 %collective-permute-start.5 = (bf16[256,1536]{1,0:T(8,128)(2,1)S(1)}, bf16[256,1536]{1,0:T(8,128)(2,1)}, u32[]{:S(2)}, u32[]{:S(2)}) collective-permute-start(bf16[256,1536]{1,0:T(8,128)(2,1)S(1)} %pad_maximum_fusion.2), channel_id=1, source_target_pairs={{0,4},{4,8},{8,12},{12,0},{1,5},{5,9},{9,13},{13,1},{2,6},{6,10},{... | collective-permute-start | bytes 2359304 | tf_op jit(solution)/shard_map/ppermute | solution.py:46
  104.7 33.2 %collective-permute-start.4 = (bf16[256,512]{1,0:T(8,128)(2,1)S(1)}, bf16[256,512]{1,0:T(8,128)(2,1)S(1)}, u32[]{:S(2)}, u32[]{:S(2)}) collective-permute-start(bf16[256,512]{1,0:T(8,128)(2,1)S(1)} %fusion.7), channel_id=1, source_target_pairs={{0,2},{1,3},{2,0},{3,1},{4,6},{5,7},{6,4},{7,5},{8,10},{9,11},{10,... | collective-permute-start | bytes 786440 | tf_op jit(solution)/shard_map/ppermute | solution.py:46
  137.9 3.7 %copy-start.10 = (bf16[256,512]{1,0:T(8,128)(2,1)}, bf16[256,512]{1,0:T(8,128)(2,1)S(1)}, u32[]{:S(2)}) copy-start(bf16[256,512]{1,0:T(8,128)(2,1)S(1)} %collective-permute-done.4) | copy-start | bytes 786436
  139.8 1.9 copy-start.12
  143.8 6.6 %collective-permute-start.8 = (bf16[768,1536]{1,0:T(8,128)(2,1)S(1)}, bf16[768,1536]{1,0:T(8,128)(2,1)}, u32[]{:S(2)}, u32[]{:S(2)}) collective-permute-start(bf16[768,1536]{1,0:T(8,128)(2,1)S(1)} %fusion), channel_id=1, source_target_pairs={{0,16},{16,0},{1,17},{17,1},{2,18},{18,2},{3,19},{19,3},{4,20},{20... | collective-permute-start | bytes 7077896 | tf_op jit(solution)/shard_map/ppermute | solution.py:46
  145.8 7.2 %copy-start.8 = (bf16[256,256]{1,0:T(8,128)(2,1)S(1)}, bf16[256,256]{1,0:T(8,128)(2,1)}, u32[]{:S(2)}) copy-start(bf16[256,256]{1,0:T(8,128)(2,1)} %copy-done.7) | copy-start | bytes 393220
  153.8 4.6 %copy-start.2 = (f32[256,1536]{1,0:T(8,128)}, f32[256,1536]{1,0:T(8,128)S(1)}, u32[]{:S(2)}) copy-start(f32[256,1536]{1,0:T(8,128)S(1)} %convolution_add_fusion) | copy-start | bytes 4718596
  153.8 14.4 %copy-start.4 = (bf16[64,16,512]{2,1,0:T(8,128)(2,1)S(1)}, bf16[64,16,512]{2,1,0:T(8,128)(2,1)}, u32[]{:S(2)}) copy-start(bf16[64,16,512]{2,1,0:T(8,128)(2,1)} %copy-done.3) | copy-start | bytes 3145732
  156.4 12.4 %copy-start.13 = (bf16[64,256]{1,0:T(8,128)(2,1)S(1)}, bf16[64,256]{1,0:T(8,128)(2,1)}, u32[]{:S(2)}) copy-start(bf16[64,256]{1,0:T(8,128)(2,1)} %copy-done.12) | copy-start | bytes 98308
  158.4 16.7 %collective-permute-start.9 = (bf16[256,512]{1,0:T(8,128)(2,1)}, bf16[256,512]{1,0:T(8,128)(2,1)S(1)}, u32[]{:S(2)}, u32[]{:S(2)}) collective-permute-start(bf16[256,512]{1,0:T(8,128)(2,1)} %fusion.9), channel_id=1, source_target_pairs={{0,1},{1,2},{2,3},{3,0},{4,5},{5,6},{6,7},{7,4},{8,9},{9,10},{10,1... | collective-permute-start | bytes 786440 | tf_op jit(solution)/shard_map/ppermute | solution.py:46
  160.3 37.2 %collective-permute-start.10 = (bf16[256,512]{1,0:T(8,128)(2,1)}, bf16[256,512]{1,0:T(8,128)(2,1)}, u32[]{:S(2)}, u32[]{:S(2)}) collective-permute-start(bf16[256,512]{1,0:T(8,128)(2,1)} %fusion.8), channel_id=1, source_target_pairs={{0,3},{1,0},{2,1},{3,2},{4,7},{5,4},{6,5},{7,6},{8,11},{9,8},{10,9... | collective-permute-start | bytes 786440 | tf_op jit(solution)/shard_map/ppermute | solution.py:46
  168.2 29.3 %copy-start.11 = (bf16[256,512]{1,0:T(8,128)(2,1)S(1)}, bf16[256,512]{1,0:T(8,128)(2,1)}, u32[]{:S(2)}) copy-start(bf16[256,512]{1,0:T(8,128)(2,1)} %copy-done.10) | copy-start | bytes 786436

commit v8 on v1

--- a/solution.py
+++ b/solution.py
@@ -34,14 +34,10 @@
     return down, up
 
 
-def sum_over_tensor(part):
-    shape = part.shape
-    pieces = part.reshape(16, -1, 128)
-    pieces = lax.all_to_all(pieces, TENSOR, split_axis=0, concat_axis=0, tiled=True)
-    own = jnp.sum(pieces, axis=0).astype(bf16)
-    spread = jnp.broadcast_to(own[None], (16,) + own.shape)
-    spread = lax.all_to_all(spread, TENSOR, split_axis=0, concat_axis=0, tiled=True)
-    return spread.reshape(shape)
+def sum_over(part, axis):
+    size = lax.axis_size(axis)
+    spread = jnp.broadcast_to(part[None], (size,) + part.shape)
+    return jnp.sum(lax.all_to_all(spread, axis, split_axis=0, concat_axis=0, tiled=True), axis=0)
 
 
 def shifted(value, axis, by):
@@ -62,13 +58,12 @@
     lhs_other = jnp.concatenate([block[:, half:] for block in blocks], axis=1)
 
     down, up = fetch_adapters(down_store, up_store, working_adapters, store_row)
-    selector = slot[:, None] == jnp.arange(WORKING_SLOTS, dtype=jnp.int32)[None, :]
-    all_ranks = lax.dot_general(x_block, down, (((1,), (1,)), ((), ())), preferred_element_type=f32)
-    rank_local = jnp.sum(
-        all_ranks.reshape(rows, WORKING_SLOTS, ADAPTER_RANK) * selector.astype(f32)[:, :, None], axis=1
-    )
-    rounded = sum_over_tensor(rank_local)
-    expanded = (rounded[:, None, :] * selector.astype(bf16)[:, :, None]).reshape(rows, WORKING_SLOTS * ADAPTER_RANK)
+    selector = slot[None, :] == jnp.arange(WORKING_SLOTS, dtype=jnp.int32)[:, None]
+    all_ranks = lax.dot_general(down, x_block, (((1,), (1,)), ((), ())), preferred_element_type=f32)
+    ranks = jnp.sum(all_ranks.reshape(WORKING_SLOTS, ADAPTER_RANK, rows) * selector.astype(f32)[:, None, :], axis=0)
+    ranks = sum_over(ranks, "x")
+    high = lax.reduce_precision(ranks, 8, 7)
+    both = jnp.concatenate([high, ranks - high], axis=1).astype(bf16)
 
     def columns(x_by, z_by):
         return (lax.rem(x_at + x_by, xs) * zs + lax.rem(z_at + z_by, zs)) * features
@@ -89,9 +84,13 @@
             own = lax.dynamic_slice(weight, (0, columns(0, z_by)), (features, features))
             part = partial[:, k * features:(k + 1) * features] + jnp.dot(x_block, own, preferred_element_type=f32)
             if z_by:
-                part = shifted(part.astype(bf16), "zh", z_by).astype(f32)
+                block = shifted(jnp.concatenate([part.astype(bf16), both], axis=0), "zh", z_by).astype(f32)
+                part = block[:rows]
+                ranks = ranks + (block[rows:, :rows] + block[rows:, rows:])
             total = part if total is None else total + part
-    term = jnp.dot(expanded, up, preferred_element_type=f32)
+    rounded = ranks.astype(bf16)
+    expanded = (rounded[None] * selector.astype(bf16)[:, None, :]).reshape(WORKING_SLOTS * ADAPTER_RANK, rows)
+    term = lax.dot_general(expanded, up, (((0,), (0,)), ((), ())), preferred_element_type=f32)
     return (total + ADAPTER_SCALE * term).astype(bf16)
 
 

time: 192 us -> 188 us (0.979)
  starting transfers between devices: 130 us -> 97.5 us
  waiting for transfers between devices: 25 us -> 53 us
  local copies, waits for them, and re-layouts: 14.5 us -> 12 us
  other arithmetic: 4.81 us -> 7.17 us
    ppermute x18, waiting for transfers between devices: 5.92 us -> 48.3 us  [shifted(): lax.ppermute(value, axis, [(i, (i + by) % size) for i in range(size)])]
    all_to_all x2 -> x1, starting transfers between devices: 33.8 us -> 4.96 us  [sum_over(): lax.all_to_all(spread, axis, split_axis=0, concat_axis=0, tiled=True)]
    all_to_all x2 -> x1, waiting for transfers between devices: 19.1 us -> 4.74 us  [sum_over(): lax.all_to_all(spread, axis, split_axis=0, concat_axis=0, tiled=True)]
    ppermute x18, starting transfers between devices: 82.7 us -> 77.9 us  [shifted(): lax.ppermute(value, axis, [(i, (i + by) % size) for i in range(size)])]
    unnamed x41 -> x43, local copies, waits for them, and re-layouts: 7.6 us -> 6.65 us
  transfers between devices with their start and end apart: 21 -> 20, of which waited for: 4 -> 6; matrix products, arithmetic and copies ran while one was open for 15% -> 16% of each run, Pallas kernels for 0% -> 0%
where the time goes in v8:
time: 188 us; the launch traced here: 185 us
  starting transfers between devices  97.5 us (52%)
  waiting for transfers between devices  53 us (28%)
  matrix products  15.1 us (8%)
  local copies, waits for them, and re-layouts  12 us (6%)
  other arithmetic  7.17 us (4%)
    ppermute x18, starting transfers between devices, shifted(): lax.ppermute(value, axis, [(i, (i + by) % size) for i in range(size)])  77.9 us
    ppermute x18, waiting for transfers between devices, shifted(): lax.ppermute(value, axis, [(i, (i + by) % size) for i in range(size)])  48.3 us
    all_to_all x1, starting transfers between devices, fetch_adapters(): lax.all_to_all(outgoing, REPLICA, split_axis=0, concat_axis=0, tiled=True)  14.6 us
    dot_general x4, matrix products, body(): jnp.dot(x_block, own, preferred_element_type=f32)  6.75 us
    unnamed x43, local copies, waits for them, and re-layouts  6.65 us
    all_to_all x1, starting transfers between devices, sum_over(): lax.all_to_all(spread, axis, split_axis=0, concat_axis=0, tiled=True)  4.96 us
    all_to_all x1, waiting for transfers between devices, sum_over(): lax.all_to_all(spread, axis, split_axis=0, concat_axis=0, tiled=True)  4.74 us
  transfers between devices with their start and end apart: 20, of which 6 were waited for; matrix products, arithmetic and copies ran while one was open for 16% of the time, Pallas kernels for 0%

profile of v8, /device:TPU:56, one launch (start us, length us, event | category | flops | bytes accessed | tf_op | source)
XLA Modules:
  0.0 185.4 jit_solution(14639489013294582600)
XLA Ops:
  0.0 3.1 %fusion.50 = (bf16[256,512]{1,0:T(8,128)(2,1)}, bf16[256,512]{1,0:T(8,128)(2,1)}, bf16[256,512]{1,0:T(8,128)(2,1)}, bf16[256,512]{1,0:T(8,128)(2,1)S(1)}, bf16[2...) fusion(bf16[512,8192]{1,0:T(8,128)(2,1)} %param.8, ...), kind=kLoop, calls=%fused_computation.84 | loop fusion | bytes 6291508 | tf_op jit(solution)/shard_map/dynamic_slice | solution.py:73
  3.1 0.9 pad_maximum_fusion.1
  4.0 3.5 %collective-permute-start.8 = (bf16[256,1024]{1,0:T(8,128)(2,1)}, bf16[256,1024]{1,0:T(8,128)(2,1)}, u32[]{:S(2)}, u32[]{:S(2)}) collective-permute-start(bf16[256,1024]{1,0:T(8,128)(2,1)} %pad_maximum_fusion.1), channel_id=1, source_target_pairs={{0,4},{4,8},{8,12},{12,0},{1,5},{5,9},{9,13},{13,1},{2,6},{6,10},{... | collective-permute-start | bytes 1572872 | tf_op jit(solution)/shard_map/ppermute | solution.py:45
  7.5 0.8 pad_maximum_fusion.2
  8.3 4.6 %collective-permute-start.9 = (bf16[256,1024]{1,0:T(8,128)(2,1)}, bf16[256,1024]{1,0:T(8,128)(2,1)}, u32[]{:S(2)}, u32[]{:S(2)}) collective-permute-start(bf16[256,1024]{1,0:T(8,128)(2,1)} %pad_maximum_fusion.2), channel_id=1, source_target_pairs={{0,8},{4,12},{8,0},{12,4},{1,9},{5,13},{9,1},{13,5},{2,10},{6,14},... | collective-permute-start | bytes 1572872 | tf_op jit(solution)/shard_map/ppermute | solution.py:45
  13.0 1.9 %collective-permute-start.3 = (bf16[256,512]{1,0:T(8,128)(2,1)}, bf16[256,512]{1,0:T(8,128)(2,1)}, u32[]{:S(2)}, u32[]{:S(2)}) collective-permute-start(bf16[256,512]{1,0:T(8,128)(2,1)} %get-tuple-element.15), channel_id=1, source_target_pairs={{0,4},{4,8},{8,12},{12,0},{1,5},{5,9},{9,13},{13,1},{2,6},{6,10},{... | collective-permute-start | bytes 786440 | tf_op jit(solution)/shard_map/ppermute | solution.py:45
  14.9 4.8 %collective-permute-start.4 = (bf16[256,512]{1,0:T(8,128)(2,1)}, bf16[256,512]{1,0:T(8,128)(2,1)}, u32[]{:S(2)}, u32[]{:S(2)}) collective-permute-start(bf16[256,512]{1,0:T(8,128)(2,1)} %get-tuple-element.14), channel_id=1, source_target_pairs={{0,8},{4,12},{8,0},{12,4},{1,9},{5,13},{9,1},{13,5},{2,10},{6,14},... | collective-permute-start | bytes 786440 | tf_op jit(solution)/shard_map/ppermute | solution.py:45
  19.7 0.1 copy.18
  19.8 0.1 eq.42
  19.9 0.2 select_reduce_fusion
  20.2 0.5 fusion.2
  20.7 0.5 fusion.3
  21.2 1.1 pad_maximum_fusion
  22.3 14.6 %all-to-all-start = ((bf16[64,16,512]{2,1,0:T(8,128)(2,1)}), bf16[64,16,512]{2,1,0:T(8,128)(2,1)S(1)}, u32[]{:S(2)}, u32[]{:S(2)}) async-start(bf16[64,16,512]{2,1,0:T(8,128)(2,1)} %pad_maximum_fusion), calls=%async_computation | async-start | bytes 2097152 | tf_op jit(solution)/shard_map/all_to_all | solution.py:30
  36.9 1.9 %collective-permute-start.14 = (bf16[256,512]{1,0:T(8,128)(2,1)}, bf16[256,512]{1,0:T(8,128)(2,1)}, u32[]{:S(2)}, u32[]{:S(2)}) collective-permute-start(bf16[256,512]{1,0:T(8,128)(2,1)} %get-tuple-element.7), channel_id=1, source_target_pairs={{0,4},{4,8},{8,12},{12,0},{1,5},{5,9},{9,13},{13,1},{2,6},{6,10},{... | collective-permute-start | bytes 786440 | tf_op jit(solution)/shard_map/ppermute | solution.py:45
  38.9 0.0 copy-start.16
  38.9 0.8 maximum_select_fusion
  39.7 1.3 convolution_bitcast_fusion.3
  41.0 1.3 convolution_bitcast_fusion
  42.4 0.9 pad_maximum_fusion.3
  43.2 5.1 %collective-permute-start.10 = (bf16[256,1024]{1,0:T(8,128)(2,1)}, bf16[256,1024]{1,0:T(8,128)(2,1)S(1)}, u32[]{:S(2)}, u32[]{:S(2)}) collective-permute-start(bf16[256,1024]{1,0:T(8,128)(2,1)} %pad_maximum_fusion.3), channel_id=1, source_target_pairs={{0,12},{4,0},{8,4},{12,8},{1,13},{5,1},{9,5},{13,9},{2,14},{6,2},{... | collective-permute-start | bytes 1572872 | tf_op jit(solution)/shard_map/ppermute | solution.py:45
  48.4 1.0 constant_dynamic-update-slice_fusion.2
  49.4 0.9 collective-permute-done.14
  50.3 1.9 %collective-permute-start = (bf16[256,512]{1,0:T(8,128)(2,1)}, bf16[256,512]{1,0:T(8,128)(2,1)S(1)}, u32[]{:S(2)}, u32[]{:S(2)}) collective-permute-start(bf16[256,512]{1,0:T(8,128)(2,1)} %maximum_select_fusion), channel_id=1, source_target_pairs={{0,4},{4,8},{8,12},{12,0},{1,5},{5,9},{9,13},{13,1},{2,6},{6,10},{... | collective-permute-start | bytes 786440 | tf_op jit(solution)/shard_map/ppermute | solution.py:45
  52.2 1.7 constant_dynamic-update-slice_fusion.8
  53.9 3.9 %collective-permute-start.1 = (bf16[256,512]{1,0:T(8,128)(2,1)}, bf16[256,512]{1,0:T(8,128)(2,1)S(1)}, u32[]{:S(2)}, u32[]{:S(2)}) collective-permute-start(bf16[256,512]{1,0:T(8,128)(2,1)} %maximum_select_fusion), channel_id=1, source_target_pairs={{0,8},{4,12},{8,0},{12,4},{1,9},{5,13},{9,1},{13,5},{2,10},{6,14},... | collective-permute-start | bytes 786440 | tf_op jit(solution)/shard_map/ppermute | solution.py:45
  57.8 1.0 constant_dynamic-update-slice_fusion.1
  58.8 3.5 %collective-permute-start.5 = (bf16[256,512]{1,0:T(8,128)(2,1)}, bf16[256,512]{1,0:T(8,128)(2,1)S(1)}, u32[]{:S(2)}, u32[]{:S(2)}) collective-permute-start(bf16[256,512]{1,0:T(8,128)(2,1)} %get-tuple-element.5), channel_id=1, source_target_pairs={{0,12},{4,0},{8,4},{12,8},{1,13},{5,1},{9,5},{13,9},{2,14},{6,2},{... | collective-permute-start | bytes 786440 | tf_op jit(solution)/shard_map/ppermute | solution.py:45
  62.3 1.1 constant_dynamic-update-slice_fusion.5
  63.4 4.6 %collective-permute-start.15 = (bf16[256,512]{1,0:T(8,128)(2,1)}, bf16[256,512]{1,0:T(8,128)(2,1)S(1)}, u32[]{:S(2)}, u32[]{:S(2)}) collective-permute-start(bf16[256,512]{1,0:T(8,128)(2,1)} %get-tuple-element.6), channel_id=1, source_target_pairs={{0,8},{4,12},{8,0},{12,4},{1,9},{5,13},{9,1},{13,5},{2,10},{6,14},... | collective-permute-start | bytes 786440 | tf_op jit(solution)/shard_map/ppermute | solution.py:45
  68.0 1.1 constant_dynamic-update-slice_fusion.4
  69.1 2.5 %collective-permute-start.16 = (bf16[256,512]{1,0:T(8,128)(2,1)S(1)}, bf16[256,512]{1,0:T(8,128)(2,1)S(1)}, u32[]{:S(2)}, u32[]{:S(2)}) collective-permute-start(bf16[256,512]{1,0:T(8,128)(2,1)S(1)} %copy-done.13), channel_id=1, source_target_pairs={{0,12},{4,0},{8,4},{12,8},{1,13},{5,1},{9,5},{13,9},{2,14},{6,2},{... | collective-permute-start | bytes 786440 | tf_op jit(solution)/shard_map/ppermute | solution.py:45
  71.7 4.3 %collective-permute-done.5 = bf16[256,512]{1,0:T(8,128)(2,1)S(1)} collective-permute-done((bf16[256,512]{1,0:T(8,128)(2,1)}, bf16[256,512]{1,0:T(8,128)(2,1)S(1)}, u32[]{:S(2)}, u32[]{:S(2)}) %collective-permute-start.5) | collective-permute-done | bytes 262176 | tf_op jit(solution)/shard_map/ppermute | solution.py:45
  76.0 1.9 %collective-permute-start.11 = (bf16[768,1024]{1,0:T(8,128)(2,1)S(1)}, bf16[768,1024]{1,0:T(8,128)(2,1)S(1)}, u32[]{:S(2)}, u32[]{:S(2)}) collective-permute-start(bf16[768,1024]{1,0:T(8,128)(2,1)S(1)} %constant_dynamic-update-slice_fusion.3), channel_id=1, source_target_pairs={{0,16},{16,0},{1,17},{17,1},{2,18},{18,2},{3,19},{19,3},{4,20},{20... | collective-permute-start | bytes 4718600 | tf_op jit(solution)/shard_map/ppermute | solution.py:45
  78.0 6.0 %collective-permute-start.2 = (bf16[256,512]{1,0:T(8,128)(2,1)S(1)}, bf16[256,512]{1,0:T(8,128)(2,1)S(1)}, u32[]{:S(2)}, u32[]{:S(2)}) collective-permute-start(bf16[256,512]{1,0:T(8,128)(2,1)S(1)} %copy-done.12), channel_id=1, source_target_pairs={{0,12},{4,0},{8,4},{12,8},{1,13},{5,1},{9,5},{13,9},{2,14},{6,2},{... | collective-permute-start | bytes 786440 | tf_op jit(solution)/shard_map/ppermute | solution.py:45
  84.0 0.7 constant_dynamic-update-slice_fusion.7
  84.7 2.1 %collective-permute-start.6 = (bf16[768,512]{1,0:T(8,128)(2,1)S(1)}, bf16[768,512]{1,0:T(8,128)(2,1)S(1)}, u32[]{:S(2)}, u32[]{:S(2)}) collective-permute-start(bf16[768,512]{1,0:T(8,128)(2,1)S(1)} %constant_dynamic-update-slice_fusion), channel_id=1, source_target_pairs={{0,16},{16,0},{1,17},{17,1},{2,18},{18,2},{3,19},{19,3},{4,20},{20... | collective-permute-start | bytes 2359304 | tf_op jit(solution)/shard_map/ppermute | solution.py:45
  86.8 0.7 constant_dynamic-update-slice_fusion.6
  87.6 2.2 %collective-permute-start.17 = (bf16[768,512]{1,0:T(8,128)(2,1)}, bf16[768,512]{1,0:T(8,128)(2,1)}, u32[]{:S(2)}, u32[]{:S(2)}) collective-permute-start(bf16[768,512]{1,0:T(8,128)(2,1)} %constant_dynamic-update-slice_fusion.6), channel_id=1, source_target_pairs={{0,16},{16,0},{1,17},{17,1},{2,18},{18,2},{3,19},{19,3},{4,20},{20... | collective-permute-start | bytes 2359304 | tf_op jit(solution)/shard_map/ppermute | solution.py:45
  89.8 0.3 collective-permute-done.2
  90.2 0.4 fusion.49
  90.6 1.1 fusion.5
  91.7 0.6 fusion.48
  92.3 0.6 convolution_add_fusion
  92.9 2.0 %fusion.11 = bf16[256,512]{1,0:T(8,128)(2,1)} fusion(f32[256,1024]{1,0:T(8,128)S(1)} %convolution_add_fusion, bf16[256,512]{1,0:T(8,128)(2,1)S(1)} %copy-done.1, bf16[512,8192]{1,0:T(8,128)(2,1)} %param.8, s32[]{:T(128)S(6)} %select_n.89), kind=kOutput, calls=%fused_computation.29 | convolution fusion | flops 134479872 | bytes 1572868 | tf_op jit(solution)/shard_map/dot_general | solution.py:85
  94.9 0.7 fusion.6
  95.6 0.7 broadcast_in_dim.16
  96.4 5.0 %all-to-all-start.1 = ((f32[4,64,256]{2,1,0:T(8,128)}), f32[4,64,256]{2,1,0:T(8,128)}, u32[]{:S(2)}, u32[]{:S(2)}) async-start(f32[4,64,256]{2,1,0:T(8,128)} %broadcast_in_dim.16), calls=%async_computation.1 | async-start | bytes 524288 | tf_op jit(solution)/shard_map/all_to_all | solution.py:40
  101.3 2.0 %fusion.12 = bf16[256,512]{1,0:T(8,128)(2,1)} fusion(f32[256,1024]{1,0:T(8,128)S(1)} %convolution_add_fusion, bf16[256,512]{1,0:T(8,128)(2,1)S(1)} %copy-done.1, bf16[512,8192]{1,0:T(8,128)(2,1)} %param.8, s32[]{:T(128)S(6)} %select_n.88), kind=kOutput, calls=%fused_computation.32 | convolution fusion | flops 134479872 | bytes 1572868 | tf_op jit(solution)/shard_map/dot_general | solution.py:85
  103.4 4.7 %all-to-all-done.1 = f32[4,64,256]{2,1,0:T(8,128)} async-done(((f32[4,64,256]{2,1,0:T(8,128)}), f32[4,64,256]{2,1,0:T(8,128)}, u32[]{:S(2)}, u32[]{:S(2)}) %all-to-all-start.1) | async-done | bytes 262176 | tf_op jit(solution)/shard_map/all_to_all | solution.py:40
  108.1 1.0 reduce_sum.29
  109.1 1.2 fusion.27
  110.4 17.6 %collective-permute-start.7 = (bf16[320,512]{1,0:T(8,128)(2,1)S(1)}, bf16[320,512]{1,0:T(8,128)(2,1)S(1)}, u32[]{:S(2)}, u32[]{:S(2)}) collective-permute-start(bf16[320,512]{1,0:T(8,128)(2,1)S(1)} %get-tuple-element.25), channel_id=1, source_target_pairs={{0,2},{1,3},{2,0},{3,1},{4,6},{5,7},{6,4},{7,5},{8,10},{9,11},{10,... | collective-permute-start | bytes 983048 | tf_op jit(solution)/shard_map/ppermute | solution.py:45
  128.0 6.1 %collective-permute-start.12 = (bf16[320,512]{1,0:T(8,128)(2,1)S(1)}, bf16[320,512]{1,0:T(8,128)(2,1)S(1)}, u32[]{:S(2)}, u32[]{:S(2)}) collective-permute-start(bf16[320,512]{1,0:T(8,128)(2,1)S(1)} %get-tuple-element.26), channel_id=1, source_target_pairs={{0,1},{1,2},{2,3},{3,0},{4,5},{5,6},{6,7},{7,4},{8,9},{9,10},{10,1... | collective-permute-start | bytes 983048 | tf_op jit(solution)/shard_map/ppermute | solution.py:45
  134.1 3.6 %collective-permute-start.13 = (bf16[320,512]{1,0:T(8,128)(2,1)S(1)}, bf16[320,512]{1,0:T(8,128)(2,1)S(1)}, u32[]{:S(2)}, u32[]{:S(2)}) collective-permute-start(bf16[320,512]{1,0:T(8,128)(2,1)S(1)} %get-tuple-element.27), channel_id=1, source_target_pairs={{0,3},{1,0},{2,1},{3,2},{4,7},{5,4},{6,5},{7,6},{8,11},{9,8},{10,9... | collective-permute-start | bytes 983048 | tf_op jit(solution)/shard_map/ppermute | solution.py:45
  137.8 1.5 fusion.47
  139.4 1.5 fusion.1
  140.9 0.6 copy.24
  141.5 0.1 convert_element_type.50
  141.5 6.8 %collective-permute-done.12 = bf16[320,512]{1,0:T(8,128)(2,1)S(1)} collective-permute-done((bf16[320,512]{1,0:T(8,128)(2,1)S(1)}, bf16[320,512]{1,0:T(8,128)(2,1)S(1)}, u32[]{:S(2)}, u32[]{:S(2)}) %collective-permute-start.12) | collective-permute-done | bytes 327712 | tf_op jit(solution)/shard_map/ppermute | solution.py:45
  148.4 0.1 convert_element_type.52
  148.5 35.8 %collective-permute-done.13 = bf16[320,512]{1,0:T(8,128)(2,1)S(1)} collective-permute-done((bf16[320,512]{1,0:T(8,128)(2,1)S(1)}, bf16[320,512]{1,0:T(8,128)(2,1)S(1)}, u32[]{:S(2)}, u32[]{:S(2)}) %collective-permute-start.13) | collective-permute-done | bytes 327712 | tf_op jit(solution)/shard_map/ppermute | solution.py:45
  184.3 0.1 convert_element_type.54
  184.4 1.0 fusion.10
  (58 shorter events, 0.3 us)
Async XLA Ops:
  0.0 20.2 %copy-start = (bf16[512,1,512]{2,0,1:T(8,128)(2,1)S(1)}, bf16[512,1,512]{2,0,1:T(8,128)(2,1)}, u32[]{:S(2)}) copy-start(bf16[512,1,512]{2,0,1:T(8,128)(2,1)} %param.9) | copy-start | bytes 1572868
  3.1 16.6 %copy-start.14 = (s32[64,8]{0,1:T(8,128)S(1)}, s32[64,8]{0,1:T(8,128)}, u32[]{:S(2)}) copy-start(s32[64,8]{0,1:T(8,128)} %param.11) | copy-start | bytes 6148
  3.1 16.8 %copy-start.15 = (s32[512]{0:T(512)S(1)}, s32[512]{0:T(512)}, u32[]{:S(2)}) copy-start(s32[512]{0:T(512)} %param.12) | copy-start | bytes 6148
  4.0 16.7 %copy-start.17 = (bf16[512,1,512]{2,0,1:T(8,128)(2,1)S(1)}, bf16[512,1,512]{2,0,1:T(8,128)(2,1)}, u32[]{:S(2)}) copy-start(bf16[512,1,512]{2,0,1:T(8,128)(2,1)} %param.10) | copy-start | bytes 1572868
  4.0 54.8 %collective-permute-start.8 = (bf16[256,1024]{1,0:T(8,128)(2,1)}, bf16[256,1024]{1,0:T(8,128)(2,1)}, u32[]{:S(2)}, u32[]{:S(2)}) collective-permute-start(bf16[256,1024]{1,0:T(8,128)(2,1)} %pad_maximum_fusion.1), channel_id=1, source_target_pairs={{0,4},{4,8},{8,12},{12,0},{1,5},{5,9},{9,13},{13,1},{2,6},{6,10},{... | collective-permute-start | bytes 1572872 | tf_op jit(solution)/shard_map/ppermute | solution.py:45
  8.3 55.1 %collective-permute-start.9 = (bf16[256,1024]{1,0:T(8,128)(2,1)}, bf16[256,1024]{1,0:T(8,128)(2,1)}, u32[]{:S(2)}, u32[]{:S(2)}) collective-permute-start(bf16[256,1024]{1,0:T(8,128)(2,1)} %pad_maximum_fusion.2), channel_id=1, source_target_pairs={{0,8},{4,12},{8,0},{12,4},{1,9},{5,13},{9,1},{13,5},{2,10},{6,14},... | collective-permute-start | bytes 1572872 | tf_op jit(solution)/shard_map/ppermute | solution.py:45
  13.0 30.3 %collective-permute-start.3 = (bf16[256,512]{1,0:T(8,128)(2,1)}, bf16[256,512]{1,0:T(8,128)(2,1)}, u32[]{:S(2)}, u32[]{:S(2)}) collective-permute-start(bf16[256,512]{1,0:T(8,128)(2,1)} %get-tuple-element.15), channel_id=1, source_target_pairs={{0,4},{4,8},{8,12},{12,0},{1,5},{5,9},{9,13},{13,1},{2,6},{6,10},{... | collective-permute-start | bytes 786440 | tf_op jit(solution)/shard_map/ppermute | solution.py:45
  14.9 39.0 %collective-permute-start.4 = (bf16[256,512]{1,0:T(8,128)(2,1)}, bf16[256,512]{1,0:T(8,128)(2,1)}, u32[]{:S(2)}, u32[]{:S(2)}) collective-permute-start(bf16[256,512]{1,0:T(8,128)(2,1)} %get-tuple-element.14), channel_id=1, source_target_pairs={{0,8},{4,12},{8,0},{12,4},{1,9},{5,13},{9,1},{13,5},{2,10},{6,14},... | collective-permute-start | bytes 786440 | tf_op jit(solution)/shard_map/ppermute | solution.py:45
  22.3 16.5 %copy-start.1 = (bf16[256,512]{1,0:T(8,128)(2,1)S(1)}, bf16[256,512]{1,0:T(8,128)(2,1)}, u32[]{:S(2)}) copy-start(bf16[256,512]{1,0:T(8,128)(2,1)} %param.7) | copy-start | bytes 786436
  22.3 72.6 %all-to-all-start = ((bf16[64,16,512]{2,1,0:T(8,128)(2,1)}), bf16[64,16,512]{2,1,0:T(8,128)(2,1)S(1)}, u32[]{:S(2)}, u32[]{:S(2)}) async-start(bf16[64,16,512]{2,1,0:T(8,128)(2,1)} %pad_maximum_fusion), calls=%async_computation | async-start | bytes 2097152 | tf_op jit(solution)/shard_map/all_to_all | solution.py:30
  36.9 13.4 %collective-permute-start.14 = (bf16[256,512]{1,0:T(8,128)(2,1)}, bf16[256,512]{1,0:T(8,128)(2,1)}, u32[]{:S(2)}, u32[]{:S(2)}) collective-permute-start(bf16[256,512]{1,0:T(8,128)(2,1)} %get-tuple-element.7), channel_id=1, source_target_pairs={{0,4},{4,8},{8,12},{12,0},{1,5},{5,9},{9,13},{13,1},{2,6},{6,10},{... | collective-permute-start | bytes 786440 | tf_op jit(solution)/shard_map/ppermute | solution.py:45
  38.9 3.5 %copy-start.16 = (s32[256]{0:T(256)S(1)}, s32[256]{0:T(256)}, u32[]{:S(2)}) copy-start(s32[256]{0:T(256)} %param.13) | copy-start | bytes 3076
  43.2 25.8 %collective-permute-start.10 = (bf16[256,1024]{1,0:T(8,128)(2,1)}, bf16[256,1024]{1,0:T(8,128)(2,1)S(1)}, u32[]{:S(2)}, u32[]{:S(2)}) collective-permute-start(bf16[256,1024]{1,0:T(8,128)(2,1)} %pad_maximum_fusion.3), channel_id=1, source_target_pairs={{0,12},{4,0},{8,4},{12,8},{1,13},{5,1},{9,5},{13,9},{2,14},{6,2},{... | collective-permute-start | bytes 1572872 | tf_op jit(solution)/shard_map/ppermute | solution.py:45
  49.3 19.7 %copy-start.13 = (bf16[256,512]{1,0:T(8,128)(2,1)S(1)}, bf16[256,512]{1,0:T(8,128)(2,1)}, u32[]{:S(2)}) copy-start(bf16[256,512]{1,0:T(8,128)(2,1)} %get-tuple-element.16) | copy-start | bytes 786436
  50.3 37.3 %collective-permute-start = (bf16[256,512]{1,0:T(8,128)(2,1)}, bf16[256,512]{1,0:T(8,128)(2,1)S(1)}, u32[]{:S(2)}, u32[]{:S(2)}) collective-permute-start(bf16[256,512]{1,0:T(8,128)(2,1)} %maximum_select_fusion), channel_id=1, source_target_pairs={{0,4},{4,8},{8,12},{12,0},{1,5},{5,9},{9,13},{13,1},{2,6},{6,10},{... | collective-permute-start | bytes 786440 | tf_op jit(solution)/shard_map/ppermute | solution.py:45
  53.9 35.9 %collective-permute-start.1 = (bf16[256,512]{1,0:T(8,128)(2,1)}, bf16[256,512]{1,0:T(8,128)(2,1)S(1)}, u32[]{:S(2)}, u32[]{:S(2)}) collective-permute-start(bf16[256,512]{1,0:T(8,128)(2,1)} %maximum_select_fusion), channel_id=1, source_target_pairs={{0,8},{4,12},{8,0},{12,4},{1,9},{5,13},{9,1},{13,5},{2,10},{6,14},... | collective-permute-start | bytes 786440 | tf_op jit(solution)/shard_map/ppermute | solution.py:45
  58.8 17.2 %collective-permute-start.5 = (bf16[256,512]{1,0:T(8,128)(2,1)}, bf16[256,512]{1,0:T(8,128)(2,1)S(1)}, u32[]{:S(2)}, u32[]{:S(2)}) collective-permute-start(bf16[256,512]{1,0:T(8,128)(2,1)} %get-tuple-element.5), channel_id=1, source_target_pairs={{0,12},{4,0},{8,4},{12,8},{1,13},{5,1},{9,5},{13,9},{2,14},{6,2},{... | collective-permute-start | bytes 786440 | tf_op jit(solution)/shard_map/ppermute | solution.py:45
  63.4 14.5 %copy-start.12 = (bf16[256,512]{1,0:T(8,128)(2,1)S(1)}, bf16[256,512]{1,0:T(8,128)(2,1)}, u32[]{:S(2)}) copy-start(bf16[256,512]{1,0:T(8,128)(2,1)} %maximum_select_fusion) | copy-start | bytes 786436
  63.4 14.5 %collective-permute-start.15 = (bf16[256,512]{1,0:T(8,128)(2,1)}, bf16[256,512]{1,0:T(8,128)(2,1)S(1)}, u32[]{:S(2)}, u32[]{:S(2)}) collective-permute-start(bf16[256,512]{1,0:T(8,128)(2,1)} %get-tuple-element.6), channel_id=1, source_target_pairs={{0,8},{4,12},{8,0},{12,4},{1,9},{5,13},{9,1},{13,5},{2,10},{6,14},... | collective-permute-start | bytes 786440 | tf_op jit(solution)/shard_map/ppermute | solution.py:45
  69.1 15.6 %collective-permute-start.16 = (bf16[256,512]{1,0:T(8,128)(2,1)S(1)}, bf16[256,512]{1,0:T(8,128)(2,1)S(1)}, u32[]{:S(2)}, u32[]{:S(2)}) collective-permute-start(bf16[256,512]{1,0:T(8,128)(2,1)S(1)} %copy-done.13), channel_id=1, source_target_pairs={{0,12},{4,0},{8,4},{12,8},{1,13},{5,1},{9,5},{13,9},{2,14},{6,2},{... | collective-permute-start | bytes 786440 | tf_op jit(solution)/shard_map/ppermute | solution.py:45
  76.0 15.7 %collective-permute-start.11 = (bf16[768,1024]{1,0:T(8,128)(2,1)S(1)}, bf16[768,1024]{1,0:T(8,128)(2,1)S(1)}, u32[]{:S(2)}, u32[]{:S(2)}) collective-permute-start(bf16[768,1024]{1,0:T(8,128)(2,1)S(1)} %constant_dynamic-update-slice_fusion.3), channel_id=1, source_target_pairs={{0,16},{16,0},{1,17},{17,1},{2,18},{18,2},{3,19},{19,3},{4,20},{20... | collective-permute-start | bytes 4718600 | tf_op jit(solution)/shard_map/ppermute | solution.py:45
  78.0 12.2 %collective-permute-start.2 = (bf16[256,512]{1,0:T(8,128)(2,1)S(1)}, bf16[256,512]{1,0:T(8,128)(2,1)S(1)}, u32[]{:S(2)}, u32[]{:S(2)}) collective-permute-start(bf16[256,512]{1,0:T(8,128)(2,1)S(1)} %copy-done.12), channel_id=1, source_target_pairs={{0,12},{4,0},{8,4},{12,8},{1,13},{5,1},{9,5},{13,9},{2,14},{6,2},{... | collective-permute-start | bytes 786440 | tf_op jit(solution)/shard_map/ppermute | solution.py:45
  84.7 5.5 %collective-permute-start.6 = (bf16[768,512]{1,0:T(8,128)(2,1)S(1)}, bf16[768,512]{1,0:T(8,128)(2,1)S(1)}, u32[]{:S(2)}, u32[]{:S(2)}) collective-permute-start(bf16[768,512]{1,0:T(8,128)(2,1)S(1)} %constant_dynamic-update-slice_fusion), channel_id=1, source_target_pairs={{0,16},{16,0},{1,17},{17,1},{2,18},{18,2},{3,19},{19,3},{4,20},{20... | collective-permute-start | bytes 2359304 | tf_op jit(solution)/shard_map/ppermute | solution.py:45
  87.6 50.2 %collective-permute-start.17 = (bf16[768,512]{1,0:T(8,128)(2,1)}, bf16[768,512]{1,0:T(8,128)(2,1)}, u32[]{:S(2)}, u32[]{:S(2)}) collective-permute-start(bf16[768,512]{1,0:T(8,128)(2,1)} %constant_dynamic-update-slice_fusion.6), channel_id=1, source_target_pairs={{0,16},{16,0},{1,17},{17,1},{2,18},{18,2},{3,19},{19,3},{4,20},{20... | collective-permute-start | bytes 2359304 | tf_op jit(solution)/shard_map/ppermute | solution.py:45
  89.8 1.9 %copy-start.6 = (bf16[256,256]{1,0:T(8,128)(2,1)}, bf16[256,256]{1,0:T(8,128)(2,1)S(1)}, u32[]{:S(2)}) copy-start(bf16[256,256]{1,0:T(8,128)(2,1)S(1)} %get-tuple-element.18) | copy-start | bytes 393220
  89.8 1.8 copy-start.8
  89.8 2.4 %copy-start.2 = (bf16[256,256]{1,0:T(8,128)(2,1)}, bf16[256,256]{1,0:T(8,128)(2,1)S(1)}, u32[]{:S(2)}) copy-start(bf16[256,256]{1,0:T(8,128)(2,1)S(1)} %get-tuple-element.19) | copy-start | bytes 393220
  90.2 1.5 copy-start.10
  90.2 2.1 %copy-start.4 = (bf16[256,256]{1,0:T(8,128)(2,1)}, bf16[256,256]{1,0:T(8,128)(2,1)S(1)}, u32[]{:S(2)}) copy-start(bf16[256,256]{1,0:T(8,128)(2,1)S(1)} %get-tuple-element.21) | copy-start | bytes 393220
  96.4 11.7 %all-to-all-start.1 = ((f32[4,64,256]{2,1,0:T(8,128)}), f32[4,64,256]{2,1,0:T(8,128)}, u32[]{:S(2)}, u32[]{:S(2)}) async-start(f32[4,64,256]{2,1,0:T(8,128)} %broadcast_in_dim.16), calls=%async_computation.1 | async-start | bytes 524288 | tf_op jit(solution)/shard_map/all_to_all | solution.py:40
  103.4 34.4 %copy-start.7 = (bf16[256,256]{1,0:T(8,128)(2,1)S(1)}, bf16[256,256]{1,0:T(8,128)(2,1)}, u32[]{:S(2)}) copy-start(bf16[256,256]{1,0:T(8,128)(2,1)} %copy-done.6) | copy-start | bytes 393220
  103.4 34.4 %copy-start.9 = (bf16[256,256]{1,0:T(8,128)(2,1)S(1)}, bf16[256,256]{1,0:T(8,128)(2,1)}, u32[]{:S(2)}) copy-start(bf16[256,256]{1,0:T(8,128)(2,1)} %copy-done.8) | copy-start | bytes 393220
  103.4 34.4 %copy-start.11 = (bf16[256,256]{1,0:T(8,128)(2,1)S(1)}, bf16[256,256]{1,0:T(8,128)(2,1)}, u32[]{:S(2)}) copy-start(bf16[256,256]{1,0:T(8,128)(2,1)} %copy-done.10) | copy-start | bytes 393220
  109.1 30.2 %copy-start.3 = (bf16[256,256]{1,0:T(8,128)(2,1)S(1)}, bf16[256,256]{1,0:T(8,128)(2,1)}, u32[]{:S(2)}) copy-start(bf16[256,256]{1,0:T(8,128)(2,1)} %copy-done.2) | copy-start | bytes 393220
  109.1 30.2 %copy-start.5 = (bf16[256,256]{1,0:T(8,128)(2,1)S(1)}, bf16[256,256]{1,0:T(8,128)(2,1)}, u32[]{:S(2)}) copy-start(bf16[256,256]{1,0:T(8,128)(2,1)} %copy-done.4) | copy-start | bytes 393220
  110.4 31.1 %collective-permute-start.7 = (bf16[320,512]{1,0:T(8,128)(2,1)S(1)}, bf16[320,512]{1,0:T(8,128)(2,1)S(1)}, u32[]{:S(2)}, u32[]{:S(2)}) collective-permute-start(bf16[320,512]{1,0:T(8,128)(2,1)S(1)} %get-tuple-element.25), channel_id=1, source_target_pairs={{0,2},{1,3},{2,0},{3,1},{4,6},{5,7},{6,4},{7,5},{8,10},{9,11},{10,... | collective-permute-start | bytes 983048 | tf_op jit(solution)/shard_map/ppermute | solution.py:45
  128.0 20.4 %collective-permute-start.12 = (bf16[320,512]{1,0:T(8,128)(2,1)S(1)}, bf16[320,512]{1,0:T(8,128)(2,1)S(1)}, u32[]{:S(2)}, u32[]{:S(2)}) collective-permute-start(bf16[320,512]{1,0:T(8,128)(2,1)S(1)} %get-tuple-element.26), channel_id=1, source_target_pairs={{0,1},{1,2},{2,3},{3,0},{4,5},{5,6},{6,7},{7,4},{8,9},{9,10},{10,1... | collective-permute-start | bytes 983048 | tf_op jit(solution)/shard_map/ppermute | solution.py:45
  134.1 50.1 %collective-permute-start.13 = (bf16[320,512]{1,0:T(8,128)(2,1)S(1)}, bf16[320,512]{1,0:T(8,128)(2,1)S(1)}, u32[]{:S(2)}, u32[]{:S(2)}) collective-permute-start(bf16[320,512]{1,0:T(8,128)(2,1)S(1)} %get-tuple-element.27), channel_id=1, source_target_pairs={{0,3},{1,0},{2,1},{3,2},{4,7},{5,4},{6,5},{7,6},{8,11},{9,8},{10,9... | collective-permute-start | bytes 983048 | tf_op jit(solution)/shard_map/ppermute | solution.py:45
